TPU v7x, 1024 devices: a whole 4x8x16 slice. The times are simulated.
1024 devices in a mesh: grp: 16 (over y, z_hi), ep: 64 (over x, z_lo, core).
Axes of the slice: x: 4, y: 8, z: 16 (z_hi: 2, z_lo: 8; z = z_hi * 8 + z_lo), core: 2. Of those that a mesh axis runs over, the one named last changes fastest.
Arguments:
- tokens: bfloat16 [4096, 7168], P('ep', 'grp'), may hold values from -6 to 6
- expert_ids: int32 [4096, 2], P('ep'), may hold values from 0 to 15, all different within a row; in each aligned block of 64 rows (0 to 63, 64 to 127, ...) at most 16 rows name the same one
- route_weight: float32 [4096, 2], P('ep'), may hold values from 0.1 to 1
- out_grad: bfloat16 [4096, 7168], P('ep', 'grp'), may hold values from -6 to 6
- w_gate: bfloat16 [64, 7168, 256], P('ep', 'grp'), may hold values from -0.0625 to 0.0625
- w_up: bfloat16 [64, 7168, 256], P('ep', 'grp'), may hold values from -0.0625 to 0.0625
- w_down: bfloat16 [64, 256, 7168], P('ep', None, 'grp'), may hold values from -0.1875 to 0.1875
Outputs:
- mixed: float32 [4096, 7168], P('ep', 'grp')
- tokens_grad: float32 [4096, 7168], P('ep', 'grp')
- gate_grad: float32 [64, 7168, 256], P('ep', 'grp')
- up_grad: float32 [64, 7168, 256], P('ep', 'grp')
- down_grad: float32 [64, 256, 7168], P('ep', None, 'grp')
Inputs may be any that keep to these rules, and one draw needn't show every extreme that they name: `expert_ids`: each token names 2 different experts. Among the 64 tokens of one index of ep no expert is named by more than 16 tokens, a bound that some block reaches.
All inputs are finite; a program needn't handle non-finite values.
Results may differ from a plain program's by a relative error of at most 0.007.
Values may be sent and summed in bfloat16 or wider, within the bound.
No kernel may reach another device: no remote copies, remote signals or barrier semaphores. Data moves between devices by JAX's collectives and lax.ppermute only.
A program may use at most 32 MiB of HBM per device.

v0:
```python
import math

import jax
import jax.numpy as jnp
from jax import lax
from jax.sharding import PartitionSpec as P

SLICES = 4
TOP = 2


def activate(gate_pre, up_pre, act_grad):
    gate_sigmoid = jax.nn.sigmoid(gate_pre)
    hidden = (gate_pre * gate_sigmoid * up_pre).astype(jnp.bfloat16)
    gate_delta = (
        act_grad * up_pre * gate_sigmoid * (1.0 + gate_pre * (1.0 - gate_sigmoid))
    ).astype(jnp.bfloat16)
    up_delta = (act_grad * gate_pre * gate_sigmoid).astype(jnp.bfloat16)
    return (hidden, gate_delta, up_delta)


def body(tokens, expert_ids, route_weight, out_grad, w_gate, w_up, w_down):
    tok_rows, part_width = tokens.shape
    peer_count = lax.axis_size("ep")
    expert_count = peer_count // SLICES
    capacity = min(tok_rows, 4 * SLICES * tok_rows // peer_count)
    assign_count = TOP * tok_rows
    flat_ids = expert_ids.reshape(assign_count)
    flat_weight = route_weight.reshape(assign_count)
    owner_mask = flat_ids[:, None] == jnp.arange(expert_count, dtype=jnp.int32)[None, :]
    running = jnp.cumsum(owner_mask.astype(jnp.int32), axis=0)
    slot_index = jnp.sum(jnp.where(owner_mask, running - 1, 0), axis=1)
    target = flat_ids * capacity + slot_index
    select_rows = (
        jnp.arange(expert_count * capacity, dtype=jnp.int32)[:, None] == target[None, :]
    ).astype(jnp.bfloat16)
    token_rows = jnp.repeat(tokens, TOP, axis=0)
    grad_rows = (
        flat_weight[:, None] * jnp.repeat(out_grad, TOP, axis=0).astype(jnp.float32)
    ).astype(jnp.bfloat16)
    send_tokens = jnp.dot(select_rows, token_rows, preferred_element_type=jnp.float32).astype(
        jnp.bfloat16
    )
    send_grads = jnp.dot(select_rows, grad_rows, preferred_element_type=jnp.float32).astype(
        jnp.bfloat16
    )
    fan_shape = (expert_count, SLICES, capacity, part_width)
    fan_tokens = jnp.broadcast_to(
        send_tokens.reshape(expert_count, 1, capacity, part_width), fan_shape
    ).reshape(-1, part_width)
    fan_grads = jnp.broadcast_to(
        send_grads.reshape(expert_count, 1, capacity, part_width), fan_shape
    ).reshape(-1, part_width)
    recv_tokens, recv_grads = (
        lax.all_to_all(fan_tokens, "ep", split_axis=0, concat_axis=0, tiled=True),
        lax.all_to_all(fan_grads, "ep", split_axis=0, concat_axis=0, tiled=True),
    )
    gate_local = w_gate[0]
    up_local = w_up[0]
    down_local = w_down[0]
    contract_last = (((1,), (1,)), ((), ()))
    contract_first = (((0,), (0,)), ((), ()))
    gate_part = jnp.dot(recv_tokens, gate_local, preferred_element_type=jnp.float32)
    up_part = jnp.dot(recv_tokens, up_local, preferred_element_type=jnp.float32)
    grad_part = lax.dot_general(
        recv_grads, down_local, contract_last, preferred_element_type=jnp.float32
    )
    gate_pre, up_pre, act_grad = lax.psum((gate_part, up_part, grad_part), "grp")
    hidden, gate_delta, up_delta = activate(gate_pre, up_pre, act_grad)
    out_rows = jnp.dot(hidden, down_local, preferred_element_type=jnp.float32).astype(jnp.bfloat16)
    in_rows = (
        lax.dot_general(gate_delta, gate_local, contract_last, preferred_element_type=jnp.float32)
        + lax.dot_general(up_delta, up_local, contract_last, preferred_element_type=jnp.float32)
    ).astype(jnp.bfloat16)
    factor = 1.0 / math.sqrt(8 * tok_rows)
    gate_grad = (
        lax.dot_general(recv_tokens, gate_delta, contract_first, preferred_element_type=jnp.float32)
        * factor
    )[None]
    up_grad = (
        lax.dot_general(recv_tokens, up_delta, contract_first, preferred_element_type=jnp.float32)
        * factor
    )[None]
    down_grad = (
        lax.dot_general(hidden, recv_grads, contract_first, preferred_element_type=jnp.float32)
        * factor
    )[None]
    back_out, back_in = (
        lax.all_to_all(out_rows, "ep", split_axis=0, concat_axis=0, tiled=True),
        lax.all_to_all(in_rows, "ep", split_axis=0, concat_axis=0, tiled=True),
    )
    summed_out = jnp.sum(back_out.reshape(fan_shape).astype(jnp.float32), axis=1).reshape(
        -1, part_width
    )
    summed_in = jnp.sum(back_in.reshape(fan_shape).astype(jnp.float32), axis=1).reshape(
        -1, part_width
    )
    per_out = summed_out[target]
    per_in = summed_in[target]
    mixed = jnp.sum((flat_weight[:, None] * per_out).reshape(tok_rows, TOP, part_width), axis=1)
    tokens_grad = jnp.sum(per_in.reshape(tok_rows, TOP, part_width), axis=1)
    return (mixed, tokens_grad, gate_grad, up_grad, down_grad)


def solution(mesh):
    return jax.shard_map(
        body,
        mesh=mesh,
        in_specs=(
            P("ep", "grp"),
            P("ep", None),
            P("ep", None),
            P("ep", "grp"),
            P("ep", "grp", None),
            P("ep", "grp", None),
            P("ep", None, "grp"),
        ),
        out_specs=(
            P("ep", "grp"),
            P("ep", "grp"),
            P("ep", "grp", None),
            P("ep", "grp", None),
            P("ep", None, "grp"),
        ),
        check_vma=False,
    )
```

profile of v0, /device:TPU:1, one launch (start us, length us, event | category | flops | bytes accessed | tf_op | source)
XLA Modules:
  0.0 905.3 jit_solution(1941059123689411640)
XLA Ops:
  7.2 0.0 copy-start
  7.2 0.8 copy.19
  8.0 0.1 reshape.96
  8.1 0.1 fusion.16
  8.2 0.2 reduce_window_sum.11
  8.4 0.2 select_reduce_fusion
  8.6 0.9 broadcast_in_dim.39
  9.5 0.1 reshape.97
  9.6 0.3 convolution_convert_fusion.2
  9.9 0.0 copy-start.8
  9.9 0.1 copy.20
  10.1 0.0 copy-start.6
  10.1 1.1 broadcast_in_dim.41
  11.2 20.2 %all-to-all-start = ((bf16[64,16,448]{2,1,0:T(8,128)(2,1)}), bf16[64,16,448]{2,1,0:T(8,128)(2,1)S(1)}, u32[]{:S(2)}, u32[]{:S(2)}) async-start(bf16[64,16,448]{2,1,0:T(8,128)(2,1)} %bitcast.1), calls=%async_computation | async-start | bytes 2097152 | tf_op jit(solution)/shard_map/all_to_all | solution.py:55
  31.4 0.0 copy-done.8
  31.4 0.1 copy.18
  31.5 0.1 mul.88
  31.6 0.0 copy-done.6
  31.7 0.1 broadcast_in_dim.42
  31.7 0.2 convert_element_type.54
  31.9 0.3 convolution_convert_fusion.1
  32.3 0.1 copy.24
  32.4 50.3 %all-to-all-done = bf16[64,16,448]{2,1,0:T(8,128)(2,1)S(1)} async-done(((bf16[64,16,448]{2,1,0:T(8,128)(2,1)}), bf16[64,16,448]{2,1,0:T(8,128)(2,1)S(1)}, u32[]{:S(2)}, u32[]{:S(2)}) %all-to-all-start) | async-done | bytes 917536 | tf_op jit(solution)/shard_map/all_to_all | solution.py:55
  82.7 1.1 broadcast_in_dim.44
  83.9 8.3 all-to-all-start.2
  92.1 0.0 all-reduce.3.cloned.1.call-start
  92.2 0.0 copy-done
  92.2 0.0 copy-start.3
  92.2 1.5 fusion.11
  93.7 0.0 copy-done.4
  93.7 1.4 fusion.7
  95.1 48.4 %all-to-all-done.2 = bf16[64,16,448]{2,1,0:T(8,128)(2,1)S(1)} async-done(((bf16[64,16,448]{2,1,0:T(8,128)(2,1)}), bf16[64,16,448]{2,1,0:T(8,128)(2,1)S(1)}, u32[]{:S(2)}, u32[]{:S(2)}) %all-to-all-start.2) | async-done | bytes 917536 | tf_op jit(solution)/shard_map/all_to_all | solution.py:56
  143.4 0.0 copy-done.3
  143.5 1.4 fusion.3
  144.9 0.0 all-reduce.3.cloned.1.call-update
  144.9 618.8 %all-reduce.3.cloned.1.call-done = (f32[1024,256]{1,0:T(8,128)}, f32[1024,256]{1,0:T(8,128)}, f32[1024,256]{1,0:T(8,128)}) async-done(((f32[1024,256]{1,0:T(8,128)}, f32[1024,256]{1,0:T(8,128)}, f32[1024,256]{1,0:T(8,128)}), (f32[1024,256]{1,0:T(8,128)}, f32[1024,256]{1,0:T(8,128)}, f32[1024,256]{1,0:T(8,128)})) %all-reduce.3.cloned.1.call-update) | async-done | bytes 3145744 | tf_op jit(solution)/shard_map/psum | solution.py:68
  763.7 2.4 multiply_convert_fusion
  766.1 0.0 copy-start.1
  766.2 0.0 copy-start.5
  766.2 0.4 fusion.9
  766.6 0.3 copy-done.1
  766.9 0.4 copy-done.5
  767.3 1.4 add_convert_fusion
  768.6 2.2 copy.25
  770.9 12.4 %all-to-all-start.3 = ((bf16[64,16,448]{2,1,0:T(8,128)(2,1)}), bf16[64,16,448]{2,1,0:T(8,128)(2,1)}, u32[]{:S(2)}, u32[]{:S(2)}) async-start(bf16[64,16,448]{2,1,0:T(8,128)(2,1)} %bitcast.65), calls=%async_computation.3 | async-start | bytes 2097152 | tf_op jit(solution)/shard_map/all_to_all | solution.py:90
  783.3 2.3 convolution_convert_fusion
  785.6 2.3 copy.21
  787.8 46.7 %all-to-all-done.3 = bf16[64,16,448]{2,1,0:T(8,128)(2,1)} async-done(((bf16[64,16,448]{2,1,0:T(8,128)(2,1)}), bf16[64,16,448]{2,1,0:T(8,128)(2,1)}, u32[]{:S(2)}, u32[]{:S(2)}) %all-to-all-start.3) | async-done | bytes 917536 | tf_op jit(solution)/shard_map/all_to_all | solution.py:90
  834.5 8.3 all-to-all-start.1
  842.9 0.1 copy.22
  842.9 0.1 mul.86
  843.1 1.3 fusion
  844.4 0.0 copy-done.2
  844.4 1.2 fusion.1
  845.7 1.2 fusion.2
  846.9 1.5 convert_reduce_fusion
  848.4 0.8 gather_fusion.1
  849.1 0.2 reshape.100
  849.3 44.8 %all-to-all-done.1 = bf16[64,16,448]{2,1,0:T(8,128)(2,1)} async-done(((bf16[64,16,448]{2,1,0:T(8,128)(2,1)}), bf16[64,16,448]{2,1,0:T(8,128)(2,1)}, u32[]{:S(2)}, u32[]{:S(2)}) %all-to-all-start.1) | async-done | bytes 917536 | tf_op jit(solution)/shard_map/all_to_all | solution.py:89
  894.1 1.5 convert_reduce_fusion.1
  895.5 0.8 gather_fusion
  896.3 0.2 gather.9
  896.5 1.0 multiply_reduce_fusion
  897.5 1.0 reduce_sum.52
  (8 shorter events, 0.0 us)
Async XLA Ops:
  7.2 85.0 %copy-start = (bf16[1,448,256]{2,1,0:T(8,128)(2,1)S(1)}, bf16[1,448,256]{2,1,0:T(8,128)(2,1)}, u32[]{:S(2)}) copy-start(bf16[1,448,256]{2,1,0:T(8,128)(2,1)} %param.11) | copy-start | bytes 688132
  9.9 21.5 %copy-start.8 = (f32[64,2]{0,1:T(2,128)S(1)}, f32[64,2]{0,1:T(2,128)}, u32[]{:S(2)}) copy-start(f32[64,2]{0,1:T(2,128)} %param.9) | copy-start | bytes 1540
  10.1 21.6 %copy-start.6 = (bf16[64,448]{1,0:T(8,128)(2,1)S(1)}, bf16[64,448]{1,0:T(8,128)(2,1)}, u32[]{:S(2)}) copy-start(bf16[64,448]{1,0:T(8,128)(2,1)} %param.10) | copy-start | bytes 172036
  11.2 71.6 %all-to-all-start = ((bf16[64,16,448]{2,1,0:T(8,128)(2,1)}), bf16[64,16,448]{2,1,0:T(8,128)(2,1)S(1)}, u32[]{:S(2)}, u32[]{:S(2)}) async-start(bf16[64,16,448]{2,1,0:T(8,128)(2,1)} %bitcast.1), calls=%async_computation | async-start | bytes 2097152 | tf_op jit(solution)/shard_map/all_to_all | solution.py:55
  83.9 9.8 %copy-start.4 = (bf16[1,448,256]{2,1,0:T(8,128)(2,1)S(1)}, bf16[1,448,256]{2,1,0:T(8,128)(2,1)}, u32[]{:S(2)}) copy-start(bf16[1,448,256]{2,1,0:T(8,128)(2,1)} %param.12) | copy-start | bytes 688132
  83.9 59.6 %all-to-all-start.2 = ((bf16[64,16,448]{2,1,0:T(8,128)(2,1)}), bf16[64,16,448]{2,1,0:T(8,128)(2,1)S(1)}, u32[]{:S(2)}, u32[]{:S(2)}) async-start(bf16[64,16,448]{2,1,0:T(8,128)(2,1)} %bitcast.12), calls=%async_computation.2 | async-start | bytes 2097152 | tf_op jit(solution)/shard_map/all_to_all | solution.py:56
  92.1 671.6 %all-reduce.3.cloned.1.call-start = ((), (), s32[]{:S(2)}) async-start(), calls=%async_computation.4 | async-start | bytes 6291456 | tf_op jit(solution)/shard_map/psum | solution.py:68
  92.2 51.3 %copy-start.3 = (bf16[1,256,448]{1,2,0:T(8,128)(2,1)S(1)}, bf16[1,256,448]{1,2,0:T(8,128)(2,1)}, u32[]{:S(2)}) copy-start(bf16[1,256,448]{1,2,0:T(8,128)(2,1)} %param.13) | copy-start | bytes 688132
  766.1 0.8 copy-start.1
  766.2 1.1 copy-start.5
  770.9 63.6 %all-to-all-start.3 = ((bf16[64,16,448]{2,1,0:T(8,128)(2,1)}), bf16[64,16,448]{2,1,0:T(8,128)(2,1)}, u32[]{:S(2)}, u32[]{:S(2)}) async-start(bf16[64,16,448]{2,1,0:T(8,128)(2,1)} %bitcast.65), calls=%async_computation.3 | async-start | bytes 2097152 | tf_op jit(solution)/shard_map/all_to_all | solution.py:90
  785.6 57.3 %copy-start.7 = (s32[64,2]{0,1:T(2,128)S(1)}, s32[64,2]{0,1:T(2,128)}, u32[]{:S(2)}) copy-start(s32[64,2]{0,1:T(2,128)} %param.8) | copy-start | bytes 1540
  834.5 59.6 %all-to-all-start.1 = ((bf16[64,16,448]{2,1,0:T(8,128)(2,1)}), bf16[64,16,448]{2,1,0:T(8,128)(2,1)}, u32[]{:S(2)}, u32[]{:S(2)}) async-start(bf16[64,16,448]{2,1,0:T(8,128)(2,1)} %bitcast.64), calls=%async_computation.1 | async-start | bytes 2097152 | tf_op jit(solution)/shard_map/all_to_all | solution.py:89
  843.1 1.3 copy-start.2
Sparse Core Ops, SparseCore 0:
  145.0 618.6 all-reduce.2
where the time goes:
time: 906 us; the launch traced here: 905 us
  waiting for transfers between devices  809 us (89%)
  starting transfers between devices  49.2 us (5%)
  between operations  14.3 us (2%)
  matrix products  12.8 us (1%)
  local copies, waits for them, and re-layouts  12.3 us (1%)
    psum x1, waiting for transfers between devices, body(): lax.psum((gate_part, up_part, grad_part), 'grp')  619 us
    all_to_all x1, waiting for transfers between devices, body(): lax.all_to_all(fan_tokens, 'ep', split_axis=0, concat_axis=0, tiled=True)  50.3 us
    all_to_all x1, waiting for transfers between devices, body(): lax.all_to_all(fan_grads, 'ep', split_axis=0, concat_axis=0, tiled=True)  48.4 us
    all_to_all x1, waiting for transfers between devices, body(): lax.all_to_all(in_rows, 'ep', split_axis=0, concat_axis=0, tiled=True)  46.7 us
    all_to_all x1, waiting for transfers between devices, body(): lax.all_to_all(out_rows, 'ep', split_axis=0, concat_axis=0, tiled=True)  44.8 us
    all_to_all x1, starting transfers between devices, body(): lax.all_to_all(fan_tokens, 'ep', split_axis=0, concat_axis=0, tiled=True)  20.2 us
  transfers between devices with their start and end apart: 5, of which 5 were waited for; matrix products, arithmetic and copies ran while one was open for 2% of the time, Pallas kernels for 0%

commit v1 on v0

v1 whole, which is shorter than its diff:
```python
import math

import jax
import jax.numpy as jnp
from jax import lax
from jax.sharding import Mesh, PartitionSpec as P

TOP = 2
CAP = 16
EXPERTS = 16
OWN = ("x", "zp")
SLICE = ("zb", "c")
EP = OWN + SLICE
GRP = ("y", "zh")

LAST = (((1,), (1,)), ((), ()))
FIRST = (((0,), (0,)), ((), ()))
F32 = jnp.float32
BF = jnp.bfloat16


def dot(a, b, dims=(((1,), (0,)), ((), ()))):
    return lax.dot_general(a, b, dims, preferred_element_type=F32)


def swap(value, axis):
    return lax.all_to_all(value, axis, split_axis=0, concat_axis=0, tiled=True)


def sum_y(part):
    rows, cols = part.shape
    got = swap(part.astype(BF).reshape(8, rows // 8, cols), "y")
    return jnp.sum(got.astype(F32), axis=0)


def sum_zh(part):
    other = lax.ppermute(part.astype(BF), "zh", [(0, 1), (1, 0)])
    return part + other.astype(F32)


def body(tokens, expert_ids, route_weight, out_grad, w_gate, w_up, w_down):
    tok_rows, width = tokens.shape
    slots = EXPERTS * CAP
    ids = expert_ids.reshape(-1)
    weight = route_weight.reshape(-1)
    owner_mask = ids[:, None] == jnp.arange(EXPERTS, dtype=jnp.int32)[None, :]
    running = jnp.cumsum(owner_mask.astype(jnp.int32), axis=0)
    target = ids * CAP + jnp.sum(jnp.where(owner_mask, running - 1, 0), axis=1)
    hit = jnp.arange(slots, dtype=jnp.int32)[:, None] == target[None, :]
    slot_weight = jnp.sum(jnp.where(hit, weight[None, :], 0.0), axis=1)
    pick = jnp.sum(hit.reshape(slots, tok_rows, TOP).astype(F32), axis=2).astype(BF)
    place = hit.astype(BF)

    send_tokens = dot(pick, tokens).astype(BF)
    send_grads = (slot_weight[:, None] * dot(pick, out_grad)).astype(BF)

    def dispatch(value):
        got = swap(value.reshape(EXPERTS, CAP, width), OWN)
        return lax.all_gather(got.reshape(slots, width), SLICE, axis=0, tiled=True)

    rows = dispatch(send_tokens)
    grad_rows = dispatch(send_grads)
    w_gate, w_up, w_down = w_gate[0], w_up[0], w_down[0]
    w_in = jnp.concatenate([w_gate, w_up], axis=1)
    hs = w_gate.shape[1]

    pre = sum_zh(sum_y(dot(rows, w_in)))
    act_grad = sum_zh(sum_y(dot(grad_rows, w_down, LAST)))
    gate_pre, up_pre = pre[:, :hs], pre[:, hs:]
    sig = jax.nn.sigmoid(gate_pre)
    hidden = (gate_pre * sig * up_pre).astype(BF)
    gate_delta = (act_grad * up_pre * sig * (1.0 + gate_pre * (1.0 - sig))).astype(BF)
    up_delta = (act_grad * gate_pre * sig).astype(BF)
    deltas = jnp.concatenate([gate_delta, up_delta], axis=1)

    hidden = swap(jnp.broadcast_to(hidden[None], (8,) + hidden.shape), "y").reshape(-1, hs)
    deltas = lax.all_gather(deltas, "y", axis=0, tiled=True)

    def collect(value):
        got = swap(value.astype(BF).reshape(4, slots, width), SLICE)
        summed = jnp.sum(got.astype(F32), axis=0).astype(BF)
        return swap(summed.reshape(EXPERTS, CAP, width), OWN).reshape(slots, width)

    back_out = collect(dot(hidden, w_down))
    back_in = collect(dot(deltas, w_in, LAST))

    factor = 1.0 / math.sqrt(8 * tok_rows)
    gate_grad = (dot(rows, deltas[:, :hs], FIRST) * factor)[None]
    up_grad = (dot(rows, deltas[:, hs:], FIRST) * factor)[None]
    down_grad = (dot(hidden, grad_rows, FIRST) * factor)[None]

    per_out = dot(place, back_out, FIRST) * weight[:, None]
    mixed = jnp.sum(per_out.reshape(tok_rows, TOP, width), axis=1)
    tokens_grad = dot(pick, back_in, FIRST)
    return (mixed, tokens_grad, gate_grad, up_grad, down_grad)


def solution(mesh):
    fine = Mesh(mesh.devices.reshape(8, 2, 4, 4, 2, 2), GRP + EP)
    return jax.shard_map(
        body,
        mesh=fine,
        in_specs=(
            P(EP, GRP),
            P(EP, None),
            P(EP, None),
            P(EP, GRP),
            P(EP, GRP, None),
            P(EP, GRP, None),
            P(EP, None, GRP),
        ),
        out_specs=(
            P(EP, GRP),
            P(EP, GRP),
            P(EP, GRP, None),
            P(EP, GRP, None),
            P(EP, None, GRP),
        ),
        check_vma=False,
    )
```

time: 906 us -> 302 us (0.33)
  waiting for transfers between devices: 809 us -> 132 us
  blocking collectives: 0 us -> 47.4 us
  starting transfers between devices: 49.2 us -> 82.2 us
    psum x1 -> x0, waiting for transfers between devices: 619 us -> none  [body(): lax.psum((gate_part, up_part, grad_part), 'grp')]
    all_to_all x4 -> x8, waiting for transfers between devices: 190 us -> 79.7 us  [swap(): return lax.all_to_all(value, axis, split_axis=0, concat_axis=0, tiled=True)]
    all_gather x0 -> x1, waiting for transfers between devices: none -> 41 us  [body(): deltas = lax.all_gather(deltas, 'y', axis=0, tiled=True)]
    all_gather x0 -> x2, blocking collectives: none -> 27.5 us  [dispatch(): return lax.all_gather(got.reshape(slots, width), SLICE, axis=0, tiled=True)]
    all_to_all x0 -> x1, blocking collectives: none -> 19.9 us  [swap(): return lax.all_to_all(value, axis, split_axis=0, concat_axis=0, tiled=True)]
    all_to_all x4 -> x8, starting transfers between devices: 49.2 us -> 66 us  [swap(): return lax.all_to_all(value, axis, split_axis=0, concat_axis=0, tiled=True)]
    ppermute x0 -> x2, starting transfers between devices: none -> 16.2 us  [sum_zh(): other = lax.ppermute(part.astype(BF), 'zh', [(0, 1), (1, 0)])]
    ppermute x0 -> x2, waiting for transfers between devices: none -> 11.7 us  [sum_zh(): other = lax.ppermute(part.astype(BF), 'zh', [(0, 1), (1, 0)])]
  transfers between devices with their start and end apart: 5 -> 11, of which waited for: 5 -> 8; matrix products, arithmetic and copies ran while one was open for 2% -> 6% of each run, Pallas kernels for 0% -> 0%
where the time goes in v1:
time: 302 us; the launch traced here: 301 us
  waiting for transfers between devices  132 us (44%)
  starting transfers between devices  82.2 us (27%)
  blocking collectives  47.4 us (16%)
  between operations  14.3 us (5%)
  matrix products  11.5 us (4%)
  local copies, waits for them, and re-layouts  8.1 us (3%)
  other arithmetic  4.93 us (2%)
    all_to_all x8, waiting for transfers between devices, swap(): return lax.all_to_all(value, axis, split_axis=0, concat_axis=0, tiled=True)  79.7 us
    all_to_all x8, starting transfers between devices, swap(): return lax.all_to_all(value, axis, split_axis=0, concat_axis=0, tiled=True)  66 us
    all_gather x1, waiting for transfers between devices, body(): deltas = lax.all_gather(deltas, 'y', axis=0, tiled=True)  41 us
    all_gather x2, blocking collectives, dispatch(): return lax.all_gather(got.reshape(slots, width), SLICE, axis=0, tiled=True)  27.5 us
    all_to_all x1, blocking collectives, swap(): return lax.all_to_all(value, axis, split_axis=0, concat_axis=0, tiled=True)  19.9 us
    ppermute x2, starting transfers between devices, sum_zh(): other = lax.ppermute(part.astype(BF), 'zh', [(0, 1), (1, 0)])  16.2 us
    ppermute x2, waiting for transfers between devices, sum_zh(): other = lax.ppermute(part.astype(BF), 'zh', [(0, 1), (1, 0)])  11.7 us
    dot_general x11, matrix products, dot(): return lax.dot_general(a, b, dims, preferred_element_type=F32)  11.5 us
  transfers between devices with their start and end apart: 11, of which 8 were waited for; matrix products, arithmetic and copies ran while one was open for 6% of the time, Pallas kernels for 0%

profile of v1, /device:TPU:1, one launch (start us, length us, event | category | flops | bytes accessed | tf_op | source)
XLA Modules:
  0.0 300.8 jit_solution(5823759791001876933)
XLA Ops:
  7.2 0.0 copy-start
  7.2 0.8 copy.61
  8.0 0.1 reshape.78
  8.2 0.1 fusion.9
  8.3 0.2 reduce_window_sum.11
  8.4 0.2 select_reduce_fusion.1
  8.6 0.1 reduce_sum.81
  8.7 0.1 copy.62
  8.8 0.7 multiply_add_fusion
  9.5 0.1 convert_reduce_fusion.2
  9.6 1.1 convolution_convert_fusion.4
  10.7 0.8 copy.63
  11.6 17.0 %all-to-all-start = ((bf16[16,16,448]{2,1,0:T(8,128)(2,1)}), bf16[16,16,448]{2,1,0:T(8,128)(2,1)S(1)}, u32[]{:S(2)}, u32[]{:S(2)}) async-start(bf16[16,16,448]{2,1,0:T(8,128)(2,1)} %bitcast), calls=%async_computation | async-start | bytes 524288 | tf_op jit(solution)/shard_map/all_to_all | solution.py:27
  28.6 0.1 copy.67
  28.7 0.1 mul.75
  28.9 0.1 select_reduce_fusion
  29.0 0.3 fusion.3
  29.3 0.0 copy-start.6
  29.3 0.0 copy-start.7
  29.3 0.8 copy.69
  30.1 13.0 %all-to-all-done = bf16[16,16,448]{2,1,0:T(8,128)(2,1)S(1)} async-done(((bf16[16,16,448]{2,1,0:T(8,128)(2,1)}), bf16[16,16,448]{2,1,0:T(8,128)(2,1)S(1)}, u32[]{:S(2)}, u32[]{:S(2)}) %all-to-all-start) | async-done | bytes 229408 | tf_op jit(solution)/shard_map/all_to_all | solution.py:27
  43.1 7.3 %all-to-all-start.5 = ((bf16[16,16,448]{2,1,0:T(8,128)(2,1)}), bf16[16,16,448]{2,1,0:T(8,128)(2,1)S(1)}, u32[]{:S(2)}, u32[]{:S(2)}) async-start(bf16[16,16,448]{2,1,0:T(8,128)(2,1)} %bitcast.9), calls=%async_computation.5 | async-start | bytes 524288 | tf_op jit(solution)/shard_map/all_to_all | solution.py:27
  50.5 15.0 %all_gather.9 = bf16[1024,448]{1,0:T(8,128)(2,1)S(1)} all-gather(bf16[256,448]{1,0:T(8,128)(2,1)S(1)} %bitcast.50), channel_id=1, replica_groups=mesh['y'=8,'zh'=2,'x'=4,'zp'=4,'zb'=2,'c'=2] {'zb','c'}, dimensions={0}, use_global_device_ids=true | all-gather | bytes 1146880 | tf_op jit(solution)/shard_map/all_gather | solution.py:59
  65.5 1.0 copy-done.1
  66.5 1.7 convolution_convert_fusion
  68.2 6.8 %all-to-all-start.1 = ((bf16[8,128,512]{2,1,0:T(8,128)(2,1)}), bf16[8,128,512]{2,1,0:T(8,128)(2,1)S(1)}, u32[]{:S(2)}, u32[]{:S(2)}) async-start(bf16[8,128,512]{2,1,0:T(8,128)(2,1)} %bitcast.4), calls=%async_computation.1 | async-start | bytes 2097152 | tf_op jit(solution)/shard_map/all_to_all | solution.py:27
  75.0 12.4 %all_gather.10 = bf16[1024,448]{1,0:T(8,128)(2,1)S(1)} all-gather(bf16[256,448]{1,0:T(8,128)(2,1)S(1)} %bitcast.51), channel_id=1, replica_groups=mesh['y'=8,'zh'=2,'x'=4,'zp'=4,'zb'=2,'c'=2] {'zb','c'}, dimensions={0}, use_global_device_ids=true | all-gather | bytes 1146880 | tf_op jit(solution)/shard_map/all_gather | solution.py:59
  87.5 1.2 convolution_convert_fusion.3
  88.7 15.5 %all-to-all-done.1 = bf16[8,128,512]{2,1,0:T(8,128)(2,1)S(1)} async-done(((bf16[8,128,512]{2,1,0:T(8,128)(2,1)}), bf16[8,128,512]{2,1,0:T(8,128)(2,1)S(1)}, u32[]{:S(2)}, u32[]{:S(2)}) %all-to-all-start.1) | async-done | bytes 1048608 | tf_op jit(solution)/shard_map/all_to_all | solution.py:27
  104.2 3.5 %all-to-all-start.6 = ((bf16[8,128,256]{2,1,0:T(8,128)(2,1)}), bf16[8,128,256]{2,1,0:T(8,128)(2,1)S(1)}, u32[]{:S(2)}, u32[]{:S(2)}) async-start(bf16[8,128,256]{2,1,0:T(8,128)(2,1)} %bitcast.11), calls=%async_computation.6 | async-start | bytes 1048576 | tf_op jit(solution)/shard_map/all_to_all | solution.py:27
  107.7 0.1 convert_reduce_fusion
  107.9 10.0 %collective-permute-start = (bf16[128,512]{1,0:T(8,128)(2,1)S(1)}, bf16[128,512]{1,0:T(8,128)(2,1)S(1)}, u32[]{:S(2)}, u32[]{:S(2)}) collective-permute-start(bf16[128,512]{1,0:T(8,128)(2,1)S(1)} %convert_element_type.65), channel_id=1, source_target_pairs={{0,64},{64,0},{1,65},{65,1},{2,66},{66,2},{3,67},{67,3},{4,68},{68... | collective-permute-start | bytes 393224 | tf_op jit(solution)/shard_map/ppermute | solution.py:37
  117.8 7.7 %all-to-all-done.6 = bf16[8,128,256]{2,1,0:T(8,128)(2,1)S(1)} async-done(((bf16[8,128,256]{2,1,0:T(8,128)(2,1)}), bf16[8,128,256]{2,1,0:T(8,128)(2,1)S(1)}, u32[]{:S(2)}, u32[]{:S(2)}) %all-to-all-start.6) | async-done | bytes 524320 | tf_op jit(solution)/shard_map/all_to_all | solution.py:27
  125.6 0.1 convert_reduce_fusion.1
  125.7 6.3 %collective-permute-start.1 = (bf16[128,256]{1,0:T(8,128)(2,1)S(1)}, bf16[128,256]{1,0:T(8,128)(2,1)S(1)}, u32[]{:S(2)}, u32[]{:S(2)}) collective-permute-start(bf16[128,256]{1,0:T(8,128)(2,1)S(1)} %convert_element_type.72), channel_id=1, source_target_pairs={{0,64},{64,0},{1,65},{65,1},{2,66},{66,2},{3,67},{67,3},{4,68},{68... | collective-permute-start | bytes 196616 | tf_op jit(solution)/shard_map/ppermute | solution.py:37
  132.0 11.7 %collective-permute-done.1 = bf16[128,256]{1,0:T(8,128)(2,1)S(1)} collective-permute-done((bf16[128,256]{1,0:T(8,128)(2,1)S(1)}, bf16[128,256]{1,0:T(8,128)(2,1)S(1)}, u32[]{:S(2)}, u32[]{:S(2)}) %collective-permute-start.1) | collective-permute-done | bytes 65568 | tf_op jit(solution)/shard_map/ppermute | solution.py:37
  143.7 0.1 multiply_convert_fusion.1
  143.8 19.9 %all_to_all.45 = bf16[8,128,256]{2,1,0:T(8,128)(2,1)S(1)} all-to-all(bf16[8,128,256]{2,1,0:T(8,128)(2,1)S(1)} %broadcast_in_dim.36), channel_id=1, replica_groups=mesh['y'=8,'zh'=2,'x'=4,'zp'=4,'zb'=2,'c'=2] {'y'}, dimensions={0} | all-to-all | bytes 1048576 | tf_op jit(solution)/shard_map/all_to_all | solution.py:27
  163.7 0.4 convolution_convert_fusion.1
  164.2 1.0 copy.80
  165.1 6.3 %all-to-all-start.3 = ((bf16[4,256,448]{1,2,0:T(8,128)(2,1)}), bf16[4,256,448]{1,2,0:T(8,128)(2,1)S(1)}, u32[]{:S(2)}, u32[]{:S(2)}) async-start(bf16[4,256,448]{1,2,0:T(8,128)(2,1)} %bitcast.46), calls=%async_computation.3 | async-start | bytes 1835008 | tf_op jit(solution)/shard_map/all_to_all | solution.py:27
  171.4 0.7 pad_maximum_fusion.3
  172.1 0.0 all-gather.2.cloned.1.call-update
  172.1 41.0 %all-gather.2.cloned.1.call-done = bf16[1024,512]{1,0:T(8,128)(2,1)} async-done(((bf16[128,512]{1,0:T(8,128)(2,1)}), bf16[1024,512]{1,0:T(8,128)(2,1)}) %all-gather.2.cloned.1.call-update) | async-done | bytes 1048592 | tf_op jit(solution)/shard_map/all_gather | solution.py:77
  213.1 1.9 convolution_convert_fusion.2
  215.0 1.0 copy.79
  216.0 9.5 %all-to-all-start.7 = ((bf16[4,256,448]{1,2,0:T(8,128)(2,1)}), bf16[4,256,448]{1,2,0:T(8,128)(2,1)}, u32[]{:S(2)}, u32[]{:S(2)}) async-start(bf16[4,256,448]{1,2,0:T(8,128)(2,1)} %bitcast.45), calls=%async_computation.7 | async-start | bytes 1835008 | tf_op jit(solution)/shard_map/all_to_all | solution.py:27
  225.5 0.2 reduce_sum.84
  225.8 0.8 copy.66
  226.6 11.2 %all-to-all-done.7 = bf16[4,256,448]{1,2,0:T(8,128)(2,1)} async-done(((bf16[4,256,448]{1,2,0:T(8,128)(2,1)}), bf16[4,256,448]{1,2,0:T(8,128)(2,1)}, u32[]{:S(2)}, u32[]{:S(2)}) %all-to-all-start.7) | async-done | bytes 917536 | tf_op jit(solution)/shard_map/all_to_all | solution.py:27
  237.8 11.8 %all-to-all-start.4 = ((bf16[16,16,448]{2,1,0:T(8,128)(2,1)}), bf16[16,16,448]{2,1,0:T(8,128)(2,1)S(1)}, u32[]{:S(2)}, u32[]{:S(2)}) async-start(bf16[16,16,448]{2,1,0:T(8,128)(2,1)} %bitcast.7), calls=%async_computation.4 | async-start | bytes 524288 | tf_op jit(solution)/shard_map/all_to_all | solution.py:27
  249.7 1.4 reduce_sum.88
  251.1 0.8 copy.72
  251.9 17.7 %all-to-all-done.4 = bf16[16,16,448]{2,1,0:T(8,128)(2,1)S(1)} async-done(((bf16[16,16,448]{2,1,0:T(8,128)(2,1)}), bf16[16,16,448]{2,1,0:T(8,128)(2,1)S(1)}, u32[]{:S(2)}, u32[]{:S(2)}) %all-to-all-start.4) | async-done | bytes 229408 | tf_op jit(solution)/shard_map/all_to_all | solution.py:27
  269.6 3.7 %all-to-all-start.8 = ((bf16[16,16,448]{2,1,0:T(8,128)(2,1)}), bf16[16,16,448]{2,1,0:T(8,128)(2,1)S(1)}, u32[]{:S(2)}, u32[]{:S(2)}) async-start(bf16[16,16,448]{2,1,0:T(8,128)(2,1)} %bitcast.12), calls=%async_computation.8 | async-start | bytes 524288 | tf_op jit(solution)/shard_map/all_to_all | solution.py:27
  273.3 1.3 fusion
  274.6 1.2 fusion.1
  275.8 1.2 fusion.2
  277.0 0.3 convolution_multiply_fusion.4
  277.3 0.1 copy.68
  277.5 0.2 reshape.86
  277.6 1.0 reduce_sum.85
  278.6 14.5 %all-to-all-done.8 = bf16[16,16,448]{2,1,0:T(8,128)(2,1)S(1)} async-done(((bf16[16,16,448]{2,1,0:T(8,128)(2,1)}), bf16[16,16,448]{2,1,0:T(8,128)(2,1)S(1)}, u32[]{:S(2)}, u32[]{:S(2)}) %all-to-all-start.8) | async-done | bytes 229408 | tf_op jit(solution)/shard_map/all_to_all | solution.py:27
  293.1 0.8 fusion.16
  (23 shorter events, 0.1 us)
Async XLA Ops:
  7.2 80.3 %copy-start = (bf16[1,256,448]{1,2,0:T(8,128)(2,1)S(1)}, bf16[1,256,448]{1,2,0:T(8,128)(2,1)}, u32[]{:S(2)}) copy-start(bf16[1,256,448]{1,2,0:T(8,128)(2,1)} %param.13) | copy-start | bytes 688132
  7.2 21.4 %copy-start.4 = (f32[64,2]{0,1:T(2,128)S(1)}, f32[64,2]{0,1:T(2,128)}, u32[]{:S(2)}) copy-start(f32[64,2]{0,1:T(2,128)} %param.9) | copy-start | bytes 1540
  7.2 21.8 %copy-start.3 = (bf16[64,448]{1,0:T(8,128)(2,1)S(1)}, bf16[64,448]{1,0:T(8,128)(2,1)}, u32[]{:S(2)}) copy-start(bf16[64,448]{1,0:T(8,128)(2,1)} %param.10) | copy-start | bytes 172036
  11.6 31.6 %all-to-all-start = ((bf16[16,16,448]{2,1,0:T(8,128)(2,1)}), bf16[16,16,448]{2,1,0:T(8,128)(2,1)S(1)}, u32[]{:S(2)}, u32[]{:S(2)}) async-start(bf16[16,16,448]{2,1,0:T(8,128)(2,1)} %bitcast), calls=%async_computation | async-start | bytes 524288 | tf_op jit(solution)/shard_map/all_to_all | solution.py:27
  29.3 37.2 %copy-start.6 = (bf16[1,448,256]{2,1,0:T(8,128)(2,1)S(1)}, bf16[1,448,256]{2,1,0:T(8,128)(2,1)}, u32[]{:S(2)}) copy-start(bf16[1,448,256]{2,1,0:T(8,128)(2,1)} %param.12) | copy-start | bytes 688132
  29.3 37.2 %copy-start.7 = (bf16[1,448,256]{2,1,0:T(8,128)(2,1)S(1)}, bf16[1,448,256]{2,1,0:T(8,128)(2,1)}, u32[]{:S(2)}) copy-start(bf16[1,448,256]{2,1,0:T(8,128)(2,1)} %param.11) | copy-start | bytes 688132
  43.1 25.1 %all-to-all-start.5 = ((bf16[16,16,448]{2,1,0:T(8,128)(2,1)}), bf16[16,16,448]{2,1,0:T(8,128)(2,1)S(1)}, u32[]{:S(2)}, u32[]{:S(2)}) async-start(bf16[16,16,448]{2,1,0:T(8,128)(2,1)} %bitcast.9), calls=%async_computation.5 | async-start | bytes 524288 | tf_op jit(solution)/shard_map/all_to_all | solution.py:27
  65.5 1.0 copy-start.1
  68.2 36.0 %all-to-all-start.1 = ((bf16[8,128,512]{2,1,0:T(8,128)(2,1)}), bf16[8,128,512]{2,1,0:T(8,128)(2,1)S(1)}, u32[]{:S(2)}, u32[]{:S(2)}) async-start(bf16[8,128,512]{2,1,0:T(8,128)(2,1)} %bitcast.4), calls=%async_computation.1 | async-start | bytes 2097152 | tf_op jit(solution)/shard_map/all_to_all | solution.py:27
  104.2 21.4 %all-to-all-start.6 = ((bf16[8,128,256]{2,1,0:T(8,128)(2,1)}), bf16[8,128,256]{2,1,0:T(8,128)(2,1)S(1)}, u32[]{:S(2)}, u32[]{:S(2)}) async-start(bf16[8,128,256]{2,1,0:T(8,128)(2,1)} %bitcast.11), calls=%async_computation.6 | async-start | bytes 1048576 | tf_op jit(solution)/shard_map/all_to_all | solution.py:27
  107.9 24.1 %collective-permute-start = (bf16[128,512]{1,0:T(8,128)(2,1)S(1)}, bf16[128,512]{1,0:T(8,128)(2,1)S(1)}, u32[]{:S(2)}, u32[]{:S(2)}) collective-permute-start(bf16[128,512]{1,0:T(8,128)(2,1)S(1)} %convert_element_type.65), channel_id=1, source_target_pairs={{0,64},{64,0},{1,65},{65,1},{2,66},{66,2},{3,67},{67,3},{4,68},{68... | collective-permute-start | bytes 393224 | tf_op jit(solution)/shard_map/ppermute | solution.py:37
  125.7 18.0 %collective-permute-start.1 = (bf16[128,256]{1,0:T(8,128)(2,1)S(1)}, bf16[128,256]{1,0:T(8,128)(2,1)S(1)}, u32[]{:S(2)}, u32[]{:S(2)}) collective-permute-start(bf16[128,256]{1,0:T(8,128)(2,1)S(1)} %convert_element_type.72), channel_id=1, source_target_pairs={{0,64},{64,0},{1,65},{65,1},{2,66},{66,2},{3,67},{67,3},{4,68},{68... | collective-permute-start | bytes 196616 | tf_op jit(solution)/shard_map/ppermute | solution.py:37
  165.1 48.0 %copy-start.8 = (bf16[1,448,256]{2,1,0:T(8,128)(2,1)S(1)}, bf16[1,448,256]{2,1,0:T(8,128)(2,1)}, u32[]{:S(2)}) copy-start(bf16[1,448,256]{2,1,0:T(8,128)(2,1)} %param.11) | copy-start | bytes 688132
  165.1 50.9 %all-to-all-start.3 = ((bf16[4,256,448]{1,2,0:T(8,128)(2,1)}), bf16[4,256,448]{1,2,0:T(8,128)(2,1)S(1)}, u32[]{:S(2)}, u32[]{:S(2)}) async-start(bf16[4,256,448]{1,2,0:T(8,128)(2,1)} %bitcast.46), calls=%async_computation.3 | async-start | bytes 1835008 | tf_op jit(solution)/shard_map/all_to_all | solution.py:27
  171.4 41.7 %all-gather.2.cloned.1.call-start = ((), (), s32[]{:S(2)}) async-start(), calls=%async_computation.9 | async-start | bytes 1179648 | tf_op jit(solution)/shard_map/all_gather | solution.py:77
  216.0 21.8 %all-to-all-start.7 = ((bf16[4,256,448]{1,2,0:T(8,128)(2,1)}), bf16[4,256,448]{1,2,0:T(8,128)(2,1)}, u32[]{:S(2)}, u32[]{:S(2)}) async-start(bf16[4,256,448]{1,2,0:T(8,128)(2,1)} %bitcast.45), calls=%async_computation.7 | async-start | bytes 1835008 | tf_op jit(solution)/shard_map/all_to_all | solution.py:27
  237.8 31.8 %all-to-all-start.4 = ((bf16[16,16,448]{2,1,0:T(8,128)(2,1)}), bf16[16,16,448]{2,1,0:T(8,128)(2,1)S(1)}, u32[]{:S(2)}, u32[]{:S(2)}) async-start(bf16[16,16,448]{2,1,0:T(8,128)(2,1)} %bitcast.7), calls=%async_computation.4 | async-start | bytes 524288 | tf_op jit(solution)/shard_map/all_to_all | solution.py:27
  269.6 5.0 %copy-start.5 = (bf16[1024,512]{1,0:T(8,128)(2,1)S(1)}, bf16[1024,512]{1,0:T(8,128)(2,1)}, u32[]{:S(2)}) copy-start(bf16[1024,512]{1,0:T(8,128)(2,1)} %all-gather.2.cloned.1.call-done) | copy-start | bytes 3145732
  269.6 23.5 %all-to-all-start.8 = ((bf16[16,16,448]{2,1,0:T(8,128)(2,1)}), bf16[16,16,448]{2,1,0:T(8,128)(2,1)S(1)}, u32[]{:S(2)}, u32[]{:S(2)}) async-start(bf16[16,16,448]{2,1,0:T(8,128)(2,1)} %bitcast.12), calls=%async_computation.8 | async-start | bytes 524288 | tf_op jit(solution)/shard_map/all_to_all | solution.py:27
  273.3 1.3 copy-start.2
Sparse Core Ops, SparseCore 0:
  175.5 37.5 all-gather.1

commit v2 on v1

--- a/solution.py
+++ b/solution.py
@@ -38,6 +38,11 @@
     return part + other.astype(F32)
 
 
+def gather_y(part):
+    rows, cols = part.shape
+    return swap(jnp.broadcast_to(part[None], (8, rows, cols)), "y").reshape(8 * rows, cols)
+
+
 def body(tokens, expert_ids, route_weight, out_grad, w_gate, w_up, w_down):
     tok_rows, width = tokens.shape
     slots = EXPERTS * CAP
@@ -64,25 +69,39 @@
     w_in = jnp.concatenate([w_gate, w_up], axis=1)
     hs = w_gate.shape[1]
 
-    pre = sum_zh(sum_y(dot(rows, w_in)))
-    act_grad = sum_zh(sum_y(dot(grad_rows, w_down, LAST)))
+    pre_part = sum_y(dot(rows, w_in))
+    act_part = sum_y(dot(grad_rows, w_down, LAST))
+    pre = sum_zh(pre_part)
     gate_pre, up_pre = pre[:, :hs], pre[:, hs:]
     sig = jax.nn.sigmoid(gate_pre)
     hidden = (gate_pre * sig * up_pre).astype(BF)
+    hidden, act_part = lax.optimization_barrier((hidden, act_part))
+    hidden = gather_y(hidden)
+    act_grad = sum_zh(act_part)
     gate_delta = (act_grad * up_pre * sig * (1.0 + gate_pre * (1.0 - sig))).astype(BF)
     up_delta = (act_grad * gate_pre * sig).astype(BF)
-    deltas = jnp.concatenate([gate_delta, up_delta], axis=1)
+    deltas = gather_y(jnp.concatenate([gate_delta, up_delta], axis=1))
 
-    hidden = swap(jnp.broadcast_to(hidden[None], (8,) + hidden.shape), "y").reshape(-1, hs)
-    deltas = lax.all_gather(deltas, "y", axis=0, tiled=True)
+    core = lax.axis_index("c")
+    half = lax.axis_index("zb")
 
-    def collect(value):
-        got = swap(value.astype(BF).reshape(4, slots, width), SLICE)
-        summed = jnp.sum(got.astype(F32), axis=0).astype(BF)
+    def collect(value, matrix, dims):
+        parts = value.reshape(2, 2, slots, value.shape[1])
+
+        def term(index):
+            part = lax.dynamic_index_in_dim(parts, index, 1, keepdims=False)
+            return dot(part.reshape(2 * slots, -1), matrix, dims)
+
+        got = lax.ppermute(term(1 - core).astype(BF), "c", [(0, 1), (1, 0)])
+        both = (term(core) + got.astype(F32)).reshape(2, slots, width)
+        away = lax.dynamic_index_in_dim(both, 1 - half, 0, keepdims=False).astype(BF)
+        keep = lax.dynamic_index_in_dim(both, half, 0, keepdims=False)
+        got = lax.ppermute(away, "zb", [(0, 1), (1, 0)])
+        summed = (keep + got.astype(F32)).astype(BF)
         return swap(summed.reshape(EXPERTS, CAP, width), OWN).reshape(slots, width)
 
-    back_out = collect(dot(hidden, w_down))
-    back_in = collect(dot(deltas, w_in, LAST))
+    back_out = collect(hidden, w_down, (((1,), (0,)), ((), ())))
+    back_in = collect(deltas, w_in, LAST)
 
     factor = 1.0 / math.sqrt(8 * tok_rows)
     gate_grad = (dot(rows, deltas[:, :hs], FIRST) * factor)[None]

time: 302 us -> 256 us (0.85)
  waiting for transfers between devices: 132 us -> 64 us
  starting transfers between devices: 82.2 us -> 119 us
  blocking collectives: 47.4 us -> 27.5 us
  local copies, waits for them, and re-layouts: 8.1 us -> 21.4 us
  between operations: 14.3 us -> 1.04 us
  matrix products: 11.5 us -> 17.3 us
    all_gather x1 -> x0, waiting for transfers between devices: 41 us -> none  [body(): deltas = lax.all_gather(deltas, 'y', axis=0, tiled=True)]
    all_to_all x8, waiting for transfers between devices: 79.7 us -> 49.5 us  [swap(): return lax.all_to_all(value, axis, split_axis=0, concat_axis=0, tiled=True)]
    ppermute x0 -> x4, starting transfers between devices: none -> 25.7 us  [the longest x2 21.4 us: collect(): got = lax.ppermute(term(1 - core).astype(BF), 'c', [(0, 1), (1, 0)])]
    all_to_all x1 -> x0, blocking collectives: 19.9 us -> none  [swap(): return lax.all_to_all(value, axis, split_axis=0, concat_axis=0, tiled=True)]
    ppermute x0 -> x4, waiting for transfers between devices: none -> 10.4 us  [the longest x2 8.67 us: collect(): got = lax.ppermute(away, 'zb', [(0, 1), (1, 0)])]
    ppermute x2, waiting for transfers between devices: 11.7 us -> 4.06 us  [sum_zh(): other = lax.ppermute(part.astype(BF), 'zh', [(0, 1), (1, 0)])]
    all_to_all x8, starting transfers between devices: 66 us -> 73.4 us  [swap(): return lax.all_to_all(value, axis, split_axis=0, concat_axis=0, tiled=True)]
    dot_general x11 -> x13, matrix products: 11.5 us -> 17.3 us  [dot(): return lax.dot_general(a, b, dims, preferred_element_type=F32)]
  transfers between devices with their start and end apart: 11 -> 14, of which waited for: 8 -> 8; matrix products, arithmetic and copies ran while one was open for 6% -> 13% of each run, Pallas kernels for 0% -> 0%
where the time goes in v2:
time: 256 us; the launch traced here: 254 us
  starting transfers between devices  119 us (46%)
  waiting for transfers between devices  64 us (25%)
  blocking collectives  27.5 us (11%)
  local copies, waits for them, and re-layouts  21.4 us (8%)
  matrix products  17.3 us (7%)
  other arithmetic  4.47 us (2%)
    all_to_all x8, starting transfers between devices, swap(): return lax.all_to_all(value, axis, split_axis=0, concat_axis=0, tiled=True)  73.4 us
    all_to_all x8, waiting for transfers between devices, swap(): return lax.all_to_all(value, axis, split_axis=0, concat_axis=0, tiled=True)  49.5 us
    all_gather x2, blocking collectives, dispatch(): return lax.all_gather(got.reshape(slots, width), SLICE, axis=0, tiled=True)  27.5 us
    ppermute x2, starting transfers between devices, collect(): got = lax.ppermute(term(1 - core).astype(BF), 'c', [(0, 1), (1, 0)])  21.4 us
    ppermute x2, starting transfers between devices, sum_zh(): other = lax.ppermute(part.astype(BF), 'zh', [(0, 1), (1, 0)])  19.6 us
    dot_general x13, matrix products, dot(): return lax.dot_general(a, b, dims, preferred_element_type=F32)  17.3 us
    ppermute x2, waiting for transfers between devices, collect(): got = lax.ppermute(away, 'zb', [(0, 1), (1, 0)])  8.67 us
    reshape x2, local copies, waits for them, and re-layouts, collect(): both = (term(core) + got.astype(F32)).reshape(2, slots, width)  5.39 us
  transfers between devices with their start and end apart: 14, of which 8 were waited for; matrix products, arithmetic and copies ran while one was open for 13% of the time, Pallas kernels for 0%

profile of v2, /device:TPU:1, one launch (start us, length us, event | category | flops | bytes accessed | tf_op | source)
XLA Modules:
  0.0 254.4 jit_solution(146812033388020035)
XLA Ops:
  0.7 0.8 copy.39
  1.5 0.1 reshape.100
  1.7 0.2 reduce_window_sum.11
  1.9 0.2 select_reduce_fusion.1
  2.1 0.1 reduce_sum.57
  2.3 0.7 multiply_add_fusion
  3.1 1.1 convolution_convert_fusion.4
  4.2 0.8 copy.41
  5.0 17.0 %all-to-all-start = ((bf16[16,16,448]{2,1,0:T(8,128)(2,1)}), bf16[16,16,448]{2,1,0:T(8,128)(2,1)S(1)}, u32[]{:S(2)}, u32[]{:S(2)}) async-start(bf16[16,16,448]{2,1,0:T(8,128)(2,1)} %bitcast), calls=%async_computation | async-start | bytes 524288 | tf_op jit(solution)/shard_map/all_to_all | solution.py:27
  22.2 0.1 broadcast_in_dim.44
  22.4 0.3 fusion.3
  22.7 0.8 copy.43
  23.6 13.0 %all-to-all-done = bf16[16,16,448]{2,1,0:T(8,128)(2,1)S(1)} async-done(((bf16[16,16,448]{2,1,0:T(8,128)(2,1)}), bf16[16,16,448]{2,1,0:T(8,128)(2,1)S(1)}, u32[]{:S(2)}, u32[]{:S(2)}) %all-to-all-start) | async-done | bytes 229408 | tf_op jit(solution)/shard_map/all_to_all | solution.py:27
  36.6 7.3 %all-to-all-start.2 = ((bf16[16,16,448]{2,1,0:T(8,128)(2,1)}), bf16[16,16,448]{2,1,0:T(8,128)(2,1)S(1)}, u32[]{:S(2)}, u32[]{:S(2)}) async-start(bf16[16,16,448]{2,1,0:T(8,128)(2,1)} %bitcast.5), calls=%async_computation.2 | async-start | bytes 524288 | tf_op jit(solution)/shard_map/all_to_all | solution.py:27
  43.9 15.0 %all_gather.6 = bf16[1024,448]{1,0:T(8,128)(2,1)S(1)} all-gather(bf16[256,448]{1,0:T(8,128)(2,1)S(1)} %bitcast.77), channel_id=1, replica_groups=mesh['y'=8,'zh'=2,'x'=4,'zp'=4,'zb'=2,'c'=2] {'zb','c'}, dimensions={0}, use_global_device_ids=true | all-gather | bytes 1146880 | tf_op jit(solution)/shard_map/all_gather | solution.py:64
  58.9 1.0 copy-done.2
  59.9 1.7 convolution_convert_fusion
  61.6 6.8 %all-to-all-start.1 = ((bf16[8,128,512]{2,1,0:T(8,128)(2,1)}), bf16[8,128,512]{2,1,0:T(8,128)(2,1)S(1)}, u32[]{:S(2)}, u32[]{:S(2)}) async-start(bf16[8,128,512]{2,1,0:T(8,128)(2,1)} %bitcast.4), calls=%async_computation.1 | async-start | bytes 2097152 | tf_op jit(solution)/shard_map/all_to_all | solution.py:27
  68.5 12.4 %all_gather.7 = bf16[1024,448]{1,0:T(8,128)(2,1)S(1)} all-gather(bf16[256,448]{1,0:T(8,128)(2,1)S(1)} %bitcast.78), channel_id=1, replica_groups=mesh['y'=8,'zh'=2,'x'=4,'zp'=4,'zb'=2,'c'=2] {'zb','c'}, dimensions={0}, use_global_device_ids=true | all-gather | bytes 1146880 | tf_op jit(solution)/shard_map/all_gather | solution.py:64
  80.9 1.2 convolution_convert_fusion.1
  82.2 15.5 %all-to-all-done.1 = bf16[8,128,512]{2,1,0:T(8,128)(2,1)S(1)} async-done(((bf16[8,128,512]{2,1,0:T(8,128)(2,1)}), bf16[8,128,512]{2,1,0:T(8,128)(2,1)S(1)}, u32[]{:S(2)}, u32[]{:S(2)}) %all-to-all-start.1) | async-done | bytes 1048608 | tf_op jit(solution)/shard_map/all_to_all | solution.py:27
  97.7 3.5 %all-to-all-start.3 = ((bf16[8,128,256]{2,1,0:T(8,128)(2,1)}), bf16[8,128,256]{2,1,0:T(8,128)(2,1)S(1)}, u32[]{:S(2)}, u32[]{:S(2)}) async-start(bf16[8,128,256]{2,1,0:T(8,128)(2,1)} %bitcast.8), calls=%async_computation.3 | async-start | bytes 1048576 | tf_op jit(solution)/shard_map/all_to_all | solution.py:27
  101.2 0.1 convert_reduce_fusion
  101.3 10.0 %collective-permute-start = (bf16[128,512]{1,0:T(8,128)(2,1)S(1)}, bf16[128,512]{1,0:T(8,128)(2,1)S(1)}, u32[]{:S(2)}, u32[]{:S(2)}) collective-permute-start(bf16[128,512]{1,0:T(8,128)(2,1)S(1)} %convert_element_type.91), channel_id=1, source_target_pairs={{0,64},{64,0},{1,65},{65,1},{2,66},{66,2},{3,67},{67,3},{4,68},{68... | collective-permute-start | bytes 393224 | tf_op jit(solution)/shard_map/ppermute | solution.py:37
  111.3 7.7 %all-to-all-done.3 = bf16[8,128,256]{2,1,0:T(8,128)(2,1)S(1)} async-done(((bf16[8,128,256]{2,1,0:T(8,128)(2,1)}), bf16[8,128,256]{2,1,0:T(8,128)(2,1)S(1)}, u32[]{:S(2)}, u32[]{:S(2)}) %all-to-all-start.3) | async-done | bytes 524320 | tf_op jit(solution)/shard_map/all_to_all | solution.py:27
  119.2 0.9 broadcast_in_dim.47
  120.1 3.5 %all-to-all-start.4 = ((bf16[8,128,256]{2,1,0:T(8,128)(2,1)}), bf16[8,128,256]{2,1,0:T(8,128)(2,1)S(1)}, u32[]{:S(2)}, u32[]{:S(2)}) async-start(bf16[8,128,256]{2,1,0:T(8,128)(2,1)} %broadcast_in_dim.47), calls=%async_computation.4 | async-start | bytes 1048576 | tf_op jit(solution)/shard_map/all_to_all | solution.py:27
  123.6 9.7 %collective-permute-start.3 = (bf16[128,256]{1,0:T(8,128)(2,1)S(1)}, bf16[128,256]{1,0:T(8,128)(2,1)S(1)}, u32[]{:S(2)}, u32[]{:S(2)}) collective-permute-start(bf16[128,256]{1,0:T(8,128)(2,1)S(1)} %convert_element_type.103), channel_id=1, source_target_pairs={{0,64},{64,0},{1,65},{65,1},{2,66},{66,2},{3,67},{67,3},{4,68},{68... | collective-permute-start | bytes 196616 | tf_op jit(solution)/shard_map/ppermute | solution.py:37
  133.3 4.1 %collective-permute-done.3 = bf16[128,256]{1,0:T(8,128)(2,1)S(1)} collective-permute-done((bf16[128,256]{1,0:T(8,128)(2,1)S(1)}, bf16[128,256]{1,0:T(8,128)(2,1)S(1)}, u32[]{:S(2)}, u32[]{:S(2)}) %collective-permute-start.3) | collective-permute-done | bytes 65568 | tf_op jit(solution)/shard_map/ppermute | solution.py:37
  137.4 1.1 broadcast_in_dim.48
  138.5 6.6 %all-to-all-start.6 = ((bf16[8,128,512]{2,1,0:T(8,128)(2,1)}), bf16[8,128,512]{2,1,0:T(8,128)(2,1)S(1)}, u32[]{:S(2)}, u32[]{:S(2)}) async-start(bf16[8,128,512]{2,1,0:T(8,128)(2,1)} %broadcast_in_dim.48), calls=%async_computation.6 | async-start | bytes 2097152 | tf_op jit(solution)/shard_map/all_to_all | solution.py:27
  145.1 1.1 convolution_convert_fusion.3
  146.2 14.5 %collective-permute-start.1 = (bf16[512,448]{0,1:T(8,128)(2,1)}, bf16[512,448]{0,1:T(8,128)(2,1)}, u32[]{:S(2)}, u32[]{:S(2)}) collective-permute-start(bf16[512,448]{0,1:T(8,128)(2,1)} %convolution_convert_fusion.3), channel_id=1, source_target_pairs={{0,1},{1,0},{2,3},{3,2},{4,5},{5,4},{6,7},{7,6},{8,9},{9,8},{10,11... | collective-permute-start | bytes 1376264 | tf_op jit(solution)/shard_map/ppermute | solution.py:95
  160.8 1.8 collective-permute-done.1
  162.5 2.3 convert_add_fusion.1
  164.8 2.7 %reshape.109 = f32[2,256,448]{1,0,2:T(2,128)} reshape(f32[512,448]{0,1:T(8,128)} %convert_add_fusion.1) | data formatting | bytes 1835008 | tf_op jit(solution)/shard_map/reshape | solution.py:96
  167.5 1.6 constant_dynamic-slice_fusion.3
  169.1 0.7 copy.61
  169.8 1.9 collective-permute-start.2
  171.8 0.8 copy-done.5
  172.8 1.2 convolution_convert_fusion.2
  174.0 6.8 %collective-permute-start.4 = (bf16[512,448]{0,1:T(8,128)(2,1)}, bf16[512,448]{0,1:T(8,128)(2,1)}, u32[]{:S(2)}, u32[]{:S(2)}) collective-permute-start(bf16[512,448]{0,1:T(8,128)(2,1)} %convolution_convert_fusion.2), channel_id=1, source_target_pairs={{0,1},{1,0},{2,3},{3,2},{4,5},{5,4},{6,7},{7,6},{8,9},{9,8},{10,11... | collective-permute-start | bytes 1376264 | tf_op jit(solution)/shard_map/ppermute | solution.py:95
  180.8 1.6 constant_dynamic-slice_fusion.4
  182.4 1.7 fusion.7
  184.1 1.8 copy.45
  185.9 20.6 %all-to-all-start.5 = ((bf16[16,16,448]{2,1,0:T(8,128)(2,1)}), bf16[16,16,448]{2,1,0:T(8,128)(2,1)}, u32[]{:S(2)}, u32[]{:S(2)}) async-start(bf16[16,16,448]{2,1,0:T(8,128)(2,1)} %bitcast.80), calls=%async_computation.5 | async-start | bytes 524288 | tf_op jit(solution)/shard_map/all_to_all | solution.py:27
  206.5 2.7 %convert_add_fusion = f32[512,448]{0,1:T(8,128)} fusion(bf16[512,448]{0,1:T(8,128)(2,1)} %collective-permute-done.4, bf16[512,512]{1,0:T(8,128)(2,1)S(1)} %bitcast.75, bf16[448,256]{1,0:T(8,128)(2,1)} %bitcast.83, bf16[448,256]{1,0:T(8,128)(2,1)} %bitcast.86), kind=kOutput, calls=%fused_computation.16 | convolution fusion | flops 236257280 | bytes 2359296 | tf_op jit(solution)/shard_map/dot_general | solution.py:23
  209.2 2.7 %reshape.115 = f32[2,256,448]{1,0,2:T(2,128)} reshape(f32[512,448]{0,1:T(8,128)} %convert_add_fusion) | data formatting | bytes 1835008 | tf_op jit(solution)/shard_map/reshape | solution.py:96
  211.9 1.7 constant_dynamic-slice_fusion.7
  213.6 2.4 collective-permute-start.5
  216.0 0.4 constant_dynamic-slice_fusion
  216.4 8.7 %collective-permute-done.5 = bf16[256,448]{0,1:T(8,128)(2,1)S(1)} collective-permute-done((bf16[256,448]{0,1:T(8,128)(2,1)S(1)}, bf16[256,448]{0,1:T(8,128)(2,1)S(1)}, u32[]{:S(2)}, u32[]{:S(2)}) %collective-permute-start.5) | collective-permute-done | bytes 229408 | tf_op jit(solution)/shard_map/ppermute | solution.py:99
  225.1 0.9 copy.48
  226.0 0.2 all-to-all-done.5
  226.2 8.1 %all-to-all-start.7 = ((bf16[16,16,448]{2,1,0:T(8,128)(2,1)}), bf16[16,16,448]{2,1,0:T(8,128)(2,1)S(1)}, u32[]{:S(2)}, u32[]{:S(2)}) async-start(bf16[16,16,448]{2,1,0:T(8,128)(2,1)} %bitcast.19), calls=%async_computation.7 | async-start | bytes 524288 | tf_op jit(solution)/shard_map/all_to_all | solution.py:27
  234.2 1.3 fusion
  235.5 1.2 fusion.1
  236.8 1.2 fusion.2
  238.0 1.2 convolution_multiply_fusion.4
  239.2 0.1 copy.46
  239.4 0.2 reshape.112
  239.5 1.0 reduce_sum.62
  240.5 13.1 %all-to-all-done.7 = bf16[16,16,448]{2,1,0:T(8,128)(2,1)S(1)} async-done(((bf16[16,16,448]{2,1,0:T(8,128)(2,1)}), bf16[16,16,448]{2,1,0:T(8,128)(2,1)S(1)}, u32[]{:S(2)}, u32[]{:S(2)}) %all-to-all-start.7) | async-done | bytes 229408 | tf_op jit(solution)/shard_map/all_to_all | solution.py:27
  253.6 0.8 fusion.26
  (41 shorter events, 1.1 us)
Async XLA Ops:
  0.6 80.3 %copy-start = (bf16[1,256,448]{1,2,0:T(8,128)(2,1)S(1)}, bf16[1,256,448]{1,2,0:T(8,128)(2,1)}, u32[]{:S(2)}) copy-start(bf16[1,256,448]{1,2,0:T(8,128)(2,1)} %param.13) | copy-start | bytes 688132
  0.6 21.4 %copy-start.9 = (f32[64,2]{0,1:T(2,128)S(1)}, f32[64,2]{0,1:T(2,128)}, u32[]{:S(2)}) copy-start(f32[64,2]{0,1:T(2,128)} %param.9) | copy-start | bytes 1540
  0.7 21.8 %copy-start.8 = (bf16[64,448]{1,0:T(8,128)(2,1)S(1)}, bf16[64,448]{1,0:T(8,128)(2,1)}, u32[]{:S(2)}) copy-start(bf16[64,448]{1,0:T(8,128)(2,1)} %param.10) | copy-start | bytes 172036
  5.0 31.5 %all-to-all-start = ((bf16[16,16,448]{2,1,0:T(8,128)(2,1)}), bf16[16,16,448]{2,1,0:T(8,128)(2,1)S(1)}, u32[]{:S(2)}, u32[]{:S(2)}) async-start(bf16[16,16,448]{2,1,0:T(8,128)(2,1)} %bitcast), calls=%async_computation | async-start | bytes 524288 | tf_op jit(solution)/shard_map/all_to_all | solution.py:27
  22.7 37.2 %copy-start.4 = (bf16[1,448,256]{2,1,0:T(8,128)(2,1)S(1)}, bf16[1,448,256]{2,1,0:T(8,128)(2,1)}, u32[]{:S(2)}) copy-start(bf16[1,448,256]{2,1,0:T(8,128)(2,1)} %param.12) | copy-start | bytes 688132
  22.7 37.2 %copy-start.6 = (bf16[1,448,256]{2,1,0:T(8,128)(2,1)S(1)}, bf16[1,448,256]{2,1,0:T(8,128)(2,1)}, u32[]{:S(2)}) copy-start(bf16[1,448,256]{2,1,0:T(8,128)(2,1)} %param.11) | copy-start | bytes 688132
  36.6 25.1 %all-to-all-start.2 = ((bf16[16,16,448]{2,1,0:T(8,128)(2,1)}), bf16[16,16,448]{2,1,0:T(8,128)(2,1)S(1)}, u32[]{:S(2)}, u32[]{:S(2)}) async-start(bf16[16,16,448]{2,1,0:T(8,128)(2,1)} %bitcast.5), calls=%async_computation.2 | async-start | bytes 524288 | tf_op jit(solution)/shard_map/all_to_all | solution.py:27
  58.9 1.0 copy-start.2
  61.6 36.0 %all-to-all-start.1 = ((bf16[8,128,512]{2,1,0:T(8,128)(2,1)}), bf16[8,128,512]{2,1,0:T(8,128)(2,1)S(1)}, u32[]{:S(2)}, u32[]{:S(2)}) async-start(bf16[8,128,512]{2,1,0:T(8,128)(2,1)} %bitcast.4), calls=%async_computation.1 | async-start | bytes 2097152 | tf_op jit(solution)/shard_map/all_to_all | solution.py:27
  97.7 21.4 %all-to-all-start.3 = ((bf16[8,128,256]{2,1,0:T(8,128)(2,1)}), bf16[8,128,256]{2,1,0:T(8,128)(2,1)S(1)}, u32[]{:S(2)}, u32[]{:S(2)}) async-start(bf16[8,128,256]{2,1,0:T(8,128)(2,1)} %bitcast.8), calls=%async_computation.3 | async-start | bytes 1048576 | tf_op jit(solution)/shard_map/all_to_all | solution.py:27
  101.3 17.8 %collective-permute-start = (bf16[128,512]{1,0:T(8,128)(2,1)S(1)}, bf16[128,512]{1,0:T(8,128)(2,1)S(1)}, u32[]{:S(2)}, u32[]{:S(2)}) collective-permute-start(bf16[128,512]{1,0:T(8,128)(2,1)S(1)} %convert_element_type.91), channel_id=1, source_target_pairs={{0,64},{64,0},{1,65},{65,1},{2,66},{66,2},{3,67},{67,3},{4,68},{68... | collective-permute-start | bytes 393224 | tf_op jit(solution)/shard_map/ppermute | solution.py:37
  120.1 17.3 %all-to-all-start.4 = ((bf16[8,128,256]{2,1,0:T(8,128)(2,1)}), bf16[8,128,256]{2,1,0:T(8,128)(2,1)S(1)}, u32[]{:S(2)}, u32[]{:S(2)}) async-start(bf16[8,128,256]{2,1,0:T(8,128)(2,1)} %broadcast_in_dim.47), calls=%async_computation.4 | async-start | bytes 1048576 | tf_op jit(solution)/shard_map/all_to_all | solution.py:27
  123.6 13.7 %collective-permute-start.3 = (bf16[128,256]{1,0:T(8,128)(2,1)S(1)}, bf16[128,256]{1,0:T(8,128)(2,1)S(1)}, u32[]{:S(2)}, u32[]{:S(2)}) collective-permute-start(bf16[128,256]{1,0:T(8,128)(2,1)S(1)} %convert_element_type.103), channel_id=1, source_target_pairs={{0,64},{64,0},{1,65},{65,1},{2,66},{66,2},{3,67},{67,3},{4,68},{68... | collective-permute-start | bytes 196616 | tf_op jit(solution)/shard_map/ppermute | solution.py:37
  138.5 33.2 %all-to-all-start.6 = ((bf16[8,128,512]{2,1,0:T(8,128)(2,1)}), bf16[8,128,512]{2,1,0:T(8,128)(2,1)S(1)}, u32[]{:S(2)}, u32[]{:S(2)}) async-start(bf16[8,128,512]{2,1,0:T(8,128)(2,1)} %broadcast_in_dim.48), calls=%async_computation.6 | async-start | bytes 2097152 | tf_op jit(solution)/shard_map/all_to_all | solution.py:27
  146.2 16.3 %collective-permute-start.1 = (bf16[512,448]{0,1:T(8,128)(2,1)}, bf16[512,448]{0,1:T(8,128)(2,1)}, u32[]{:S(2)}, u32[]{:S(2)}) collective-permute-start(bf16[512,448]{0,1:T(8,128)(2,1)} %convolution_convert_fusion.3), channel_id=1, source_target_pairs={{0,1},{1,0},{2,3},{3,2},{4,5},{5,4},{6,7},{7,6},{8,9},{9,8},{10,11... | collective-permute-start | bytes 1376264 | tf_op jit(solution)/shard_map/ppermute | solution.py:95
  169.8 12.6 %collective-permute-start.2 = (bf16[256,448]{0,1:T(8,128)(2,1)}, bf16[256,448]{0,1:T(8,128)(2,1)}, u32[]{:S(2)}, u32[]{:S(2)}) collective-permute-start(bf16[256,448]{0,1:T(8,128)(2,1)} %bitcast.68), channel_id=1, source_target_pairs={{0,2},{2,0},{1,3},{3,1},{4,6},{6,4},{5,7},{7,5},{8,10},{10,8},{9,1... | collective-permute-start | bytes 688136 | tf_op jit(solution)/shard_map/ppermute | solution.py:99
  171.7 0.9 copy-start.5
  171.7 1.0 copy-start.7
  174.0 32.5 %collective-permute-start.4 = (bf16[512,448]{0,1:T(8,128)(2,1)}, bf16[512,448]{0,1:T(8,128)(2,1)}, u32[]{:S(2)}, u32[]{:S(2)}) collective-permute-start(bf16[512,448]{0,1:T(8,128)(2,1)} %convolution_convert_fusion.2), channel_id=1, source_target_pairs={{0,1},{1,0},{2,3},{3,2},{4,5},{5,4},{6,7},{7,6},{8,9},{9,8},{10,11... | collective-permute-start | bytes 1376264 | tf_op jit(solution)/shard_map/ppermute | solution.py:95
  185.9 40.3 %all-to-all-start.5 = ((bf16[16,16,448]{2,1,0:T(8,128)(2,1)}), bf16[16,16,448]{2,1,0:T(8,128)(2,1)}, u32[]{:S(2)}, u32[]{:S(2)}) async-start(bf16[16,16,448]{2,1,0:T(8,128)(2,1)} %bitcast.80), calls=%async_computation.5 | async-start | bytes 524288 | tf_op jit(solution)/shard_map/all_to_all | solution.py:27
  211.9 4.1 %copy-start.1 = (f32[2,256,448]{1,0,2:T(2,128)S(1)}, f32[2,256,448]{1,0,2:T(2,128)}, u32[]{:S(2)}) copy-start(f32[2,256,448]{1,0,2:T(2,128)} %reshape.115) | copy-start | bytes 2752516
  213.6 11.4 %collective-permute-start.5 = (bf16[256,448]{0,1:T(8,128)(2,1)S(1)}, bf16[256,448]{0,1:T(8,128)(2,1)S(1)}, u32[]{:S(2)}, u32[]{:S(2)}) collective-permute-start(bf16[256,448]{0,1:T(8,128)(2,1)S(1)} %bitcast.89), channel_id=1, source_target_pairs={{0,2},{2,0},{1,3},{3,1},{4,6},{6,4},{5,7},{7,5},{8,10},{10,8},{9,1... | collective-permute-start | bytes 688136 | tf_op jit(solution)/shard_map/ppermute | solution.py:99
  226.2 27.4 %all-to-all-start.7 = ((bf16[16,16,448]{2,1,0:T(8,128)(2,1)}), bf16[16,16,448]{2,1,0:T(8,128)(2,1)S(1)}, u32[]{:S(2)}, u32[]{:S(2)}) async-start(bf16[16,16,448]{2,1,0:T(8,128)(2,1)} %bitcast.19), calls=%async_computation.7 | async-start | bytes 524288 | tf_op jit(solution)/shard_map/all_to_all | solution.py:27
  234.2 1.3 copy-start.3

commit v3 on v1

v3 whole, which is shorter than its diff:
```python
import math

import jax
import jax.numpy as jnp
from jax import lax
from jax.experimental import pallas as pl
from jax.experimental.pallas import tpu as pltpu
from jax.sharding import Mesh, PartitionSpec as P

TOP = 2
CAP = 16
EXPERTS = 16
SLICES = 4
OWN = ("x", "zp")
SLICE = ("zb", "c")
EP = OWN + SLICE
GRP = ("y", "zh")

PLAIN = (((1,), (0,)), ((), ()))
LAST = (((1,), (1,)), ((), ()))
FIRST = (((0,), (0,)), ((), ()))
F32 = jnp.float32
BF = jnp.bfloat16


def dot(a, b, dims=PLAIN):
    return lax.dot_general(a, b, dims, preferred_element_type=F32)


def local(kernel, outs, *args):
    size = sum(a.size * a.dtype.itemsize for a in args)
    size += sum(math.prod(shape) * jnp.dtype(kind).itemsize for shape, kind in outs)
    return pl.pallas_call(
        kernel,
        out_shape=[jax.ShapeDtypeStruct(shape, kind) for shape, kind in outs],
        in_specs=[pl.BlockSpec(memory_space=pltpu.VMEM)] * len(args),
        out_specs=[pl.BlockSpec(memory_space=pltpu.VMEM)] * len(outs),
        compiler_params=pltpu.CompilerParams(vmem_limit_bytes=16 * 2**20),
        cost_estimate=pl.CostEstimate(
            flops=2 * 10**9, bytes_accessed=2 * size, transcendentals=0
        ),
    )(*args)


def pack_kernel(ids_ref, weight_ref, tokens_ref, grad_ref, send_ref, place_ref):
    count = ids_ref.shape[1]
    slots = place_ref.shape[0]
    across = jnp.broadcast_to(ids_ref[...], (count, count))
    first = lax.broadcasted_iota(jnp.int32, (count, count), 0)
    second = lax.broadcasted_iota(jnp.int32, (count, count), 1)
    earlier = (across.T == across) & (first < second)
    rank = jnp.sum(jnp.where(earlier, 1.0, 0.0), axis=0, keepdims=True)
    target = ids_ref[...] * CAP + rank.astype(jnp.int32)
    hit = lax.broadcasted_iota(jnp.int32, (slots, count), 0) == target
    slot_weight = jnp.sum(jnp.where(hit, weight_ref[...], 0.0), axis=1, keepdims=True)
    place = jnp.where(hit, 1.0, 0.0).astype(BF)
    place_ref[...] = place
    tokens = tokens_ref[...]
    grads = grad_ref[...]
    rows = dot(place, jnp.concatenate([tokens, tokens], axis=0))
    grad_rows = slot_weight * dot(place, jnp.concatenate([grads, grads], axis=0))
    send_ref[...] = jnp.concatenate([rows, grad_rows], axis=1).astype(BF)


def pre_kernel(rows_ref, gate_ref, up_ref, out_ref):
    slices, width, hs = gate_ref.shape
    rows = rows_ref[:, :width]
    for s in range(slices):
        out_ref[:, s * hs : (s + 1) * hs] = dot(rows, gate_ref[s]).astype(BF)
        t = slices + s
        out_ref[:, t * hs : (t + 1) * hs] = dot(rows, up_ref[s]).astype(BF)


def act_kernel(rows_ref, down_ref, out_ref):
    slices, width, hs = down_ref.shape
    rows = rows_ref[:, width:]
    for s in range(slices):
        out_ref[:, s * hs : (s + 1) * hs] = dot(rows, down_ref[s]).astype(BF)


def back_kernel(hidden_ref, deltas_ref, gate_ref, up_ref, down_ref, out_ref):
    slices, width, hs = gate_ref.shape
    out_rows = in_rows = 0.0
    for s in range(slices):
        here = slice(s * hs, (s + 1) * hs)
        there = slice((slices + s) * hs, (slices + s + 1) * hs)
        out_rows += dot(hidden_ref[:, here], down_ref[s], LAST)
        in_rows += dot(deltas_ref[:, here], gate_ref[s], LAST)
        in_rows += dot(deltas_ref[:, there], up_ref[s], LAST)
    out_ref[...] = jnp.concatenate([out_rows, in_rows], axis=1).astype(BF)


def down_kernel(factor, *refs):
    rows_refs, unit_refs, grad_ref = refs[:SLICES], refs[SLICES:-1], refs[-1]
    width = grad_ref.shape[0]
    total = 0.0
    for rows_ref, unit_ref in zip(rows_refs, unit_refs):
        total += dot(rows_ref[:, width:], unit_ref[...], FIRST)
    grad_ref[...] = total * factor


def in_kernel(factor, *refs):
    rows_refs, unit_refs, grad_refs = refs[:SLICES], refs[SLICES:-2], refs[-2:]
    width, hs = grad_refs[0].shape
    total = 0.0
    for rows_ref, unit_ref in zip(rows_refs, unit_refs):
        total += dot(rows_ref[:, :width], unit_ref[...], FIRST)
    grad_refs[0][...] = total[:, :hs] * factor
    grad_refs[1][...] = total[:, hs:] * factor


def home_kernel(place_ref, weight_ref, back_ref, mixed_ref, grad_ref):
    tok_rows, width = mixed_ref.shape
    count = weight_ref.shape[1]
    weight = jnp.broadcast_to(weight_ref[...], (count, count)).T[:, :1]
    per = dot(place_ref[...], back_ref[...], FIRST)
    per_out = per[:, :width] * weight
    per_in = per[:, width:]
    mixed_ref[...] = per_out[:tok_rows] + per_out[tok_rows:]
    grad_ref[...] = per_in[:tok_rows] + per_in[tok_rows:]


def swap(value, axis):
    return lax.all_to_all(value, axis, split_axis=0, concat_axis=0, tiled=True)


def sum_y(part):
    rows, cols = part.shape
    got = swap(part.reshape(8, rows // 8, cols), "y")
    return jnp.sum(got.astype(F32), axis=0)


def sum_zh(part):
    other = lax.ppermute(part.astype(BF), "zh", [(0, 1), (1, 0)])
    return part + other.astype(F32)


def gather_y(part):
    rows, cols = part.shape
    return swap(jnp.broadcast_to(part[None], (8, rows, cols)), "y").reshape(8 * rows, cols)


def to_slice(value, step):
    return lax.ppermute(value, SLICE, [(i, i ^ step) for i in range(SLICES)])


def body(tokens, expert_ids, route_weight, out_grad, w_gate, w_up, w_down):
    tok_rows, width = tokens.shape
    hs = w_gate.shape[2]
    units = SLICES * hs
    slots = EXPERTS * CAP
    ids = expert_ids.T.reshape(1, -1)
    weight = route_weight.T.reshape(1, -1)
    send, place = local(
        pack_kernel,
        [((slots, 2 * width), BF), ((slots, TOP * tok_rows), BF)],
        ids, weight, tokens, out_grad,
    )
    w_gate, w_up, w_down = w_gate[0], w_up[0], w_down[0].T
    send, w_gate, w_up = lax.optimization_barrier((send, w_gate, w_up))
    rows = swap(send.reshape(EXPERTS, CAP, 2 * width), OWN).reshape(slots, 2 * width)
    all_gate = lax.all_gather(w_gate, SLICE, axis=0)
    all_up = lax.all_gather(w_up, SLICE, axis=0)
    rows, all_gate, all_up, w_down = lax.optimization_barrier((rows, all_gate, all_up, w_down))
    all_down = lax.all_gather(w_down, SLICE, axis=0)

    (pre_local,) = local(pre_kernel, [((slots, 2 * units), BF)], rows, all_gate, all_up)
    pre_part = sum_y(pre_local)
    (act_local,) = local(act_kernel, [((slots, units), BF)], rows, all_down)
    act_local, rows = lax.optimization_barrier((act_local, rows))
    every = [rows] + [to_slice(rows, step) for step in (1, 2, 3)]
    act_part = sum_y(act_local)
    pre = sum_zh(pre_part)
    gate_pre, up_pre = pre[:, :units], pre[:, units:]
    sig = jax.nn.sigmoid(gate_pre)
    hidden = (gate_pre * sig * up_pre).astype(BF)
    hidden, act_part, every = lax.optimization_barrier((hidden, act_part, every))
    hidden = gather_y(hidden)
    act_grad = sum_zh(act_part)
    gate_delta = (act_grad * up_pre * sig * (1.0 + gate_pre * (1.0 - sig))).astype(BF)
    up_delta = (act_grad * gate_pre * sig).astype(BF)
    deltas = gather_y(jnp.concatenate([gate_delta, up_delta], axis=1))

    own = lax.axis_index(SLICE)

    def part(value, step, blocks):
        cut = [
            lax.dynamic_slice_in_dim(value, b * units + (own ^ step) * hs, hs, 1)
            for b in range(blocks)
        ]
        return jnp.concatenate(cut, axis=1)

    def of_slice(value, blocks):
        return [part(value, 0, blocks)] + [
            to_slice(part(value, step, blocks), step) for step in (1, 2, 3)
        ]

    hidden_own = of_slice(hidden, 1)
    deltas, hidden, hidden_own = lax.optimization_barrier((deltas, hidden, hidden_own))
    (back,) = local(
        back_kernel, [((slots, 2 * width), BF)], hidden, deltas, all_gate, all_up, all_down
    )
    back = swap(back.reshape(EXPERTS, CAP, 2 * width), OWN).reshape(slots, 2 * width)

    factor = 1.0 / math.sqrt(8 * tok_rows)

    def down(*refs):
        down_kernel(factor, *refs)

    def into(*refs):
        in_kernel(factor, *refs)

    one = ((width, hs), F32)
    (down_grad,) = local(down, [one], *every, *hidden_own)
    gate_grad, up_grad = local(into, [one, one], *every, *of_slice(deltas, 2))
    mixed, tokens_grad = local(home_kernel, [((tok_rows, width), F32)] * 2, place, weight, back)
    return (mixed, tokens_grad, gate_grad[None], up_grad[None], down_grad.T[None])


def solution(mesh):
    fine = Mesh(mesh.devices.reshape(8, 2, 4, 4, 2, 2), GRP + EP)
    return jax.shard_map(
        body,
        mesh=fine,
        in_specs=(
            P(EP, GRP),
            P(EP, None),
            P(EP, None),
            P(EP, GRP),
            P(EP, GRP, None),
            P(EP, GRP, None),
            P(EP, None, GRP),
        ),
        out_specs=(
            P(EP, GRP),
            P(EP, GRP),
            P(EP, GRP, None),
            P(EP, GRP, None),
            P(EP, None, GRP),
        ),
        check_vma=False,
    )
```

time: 302 us -> 255 us (0.84)
  the two profiles are of different devices: /device:TPU:1 before, /device:TPU:129 now
where the time goes in v3:
time: 255 us; the launch traced here: 254 us
  starting transfers between devices  91 us (36%)
  waiting for transfers between devices  85.9 us (34%)
  blocking collectives  45.9 us (18%)
  local copies, waits for them, and re-layouts  13.3 us (5%)
  Pallas kernels  11.7 us (5%)
  other arithmetic  5.01 us (2%)
    all_to_all x6, starting transfers between devices, swap(): return lax.all_to_all(value, axis, split_axis=0, concat_axis=0, tiled=True)  50.6 us
    ppermute x2, waiting for transfers between devices, sum_zh(): other = lax.ppermute(part.astype(BF), 'zh', [(0, 1), (1, 0)])  31.6 us
    all_to_all x6, waiting for transfers between devices, swap(): return lax.all_to_all(value, axis, split_axis=0, concat_axis=0, tiled=True)  31.5 us
    all_gather x1, blocking collectives, body(): all_gate = lax.all_gather(w_gate, SLICE, axis=0)  26.8 us
    ppermute x9, starting transfers between devices, to_slice(): return lax.ppermute(value, SLICE, [(i, i ^ step) for i in range(SLICES)])  26.6 us
    ppermute x9, waiting for transfers between devices, to_slice(): return lax.ppermute(value, SLICE, [(i, i ^ step) for i in range(SLICES)])  22.8 us
    ppermute x2, starting transfers between devices, sum_zh(): other = lax.ppermute(part.astype(BF), 'zh', [(0, 1), (1, 0)])  13.8 us
    pallas_call x7, Pallas kernels, local(): pl.pallas_call(kernel, out_shape=[jax.ShapeDtypeStruct(shape, kind) for s...  11.7 us
  transfers between devices with their start and end apart: 17, of which 9 were waited for; matrix products, arithmetic and copies ran while one was open for 2% of the time, Pallas kernels for 3%

profile of v3, /device:TPU:129, one launch (start us, length us, event | category | flops | bytes accessed | tf_op | source)
XLA Modules:
  0.0 253.8 jit_solution(14161636329012537700)
XLA Ops:
  0.6 0.8 reshape.42.ids_ref
  1.4 0.8 reshape.43.weight_ref
  2.2 0.8 copy-done.15
  3.0 0.8 copy-done.16
  3.8 1.2 shard_map.110
  5.1 0.6 copy-done.17
  5.7 14.6 %all-to-all-start = ((bf16[16,16,896]{2,1,0:T(8,128)(2,1)}), bf16[16,16,896]{2,1,0:T(8,128)(2,1)S(1)}, u32[]{:S(2)}, u32[]{:S(2)}) async-start(bf16[16,16,896]{2,1,0:T(8,128)(2,1)} %bitcast.4), calls=%async_computation | async-start | bytes 917504 | tf_op jit(solution)/shard_map/all_to_all | solution.py:124
  20.2 26.8 %all-gather = bf16[1792,256]{1,0:T(8,128)(2,1)S(1)} all-gather(bf16[448,256]{1,0:T(8,128)(2,1)S(1)} %bitcast.42), channel_id=2, replica_groups=mesh['y'=8,'zh'=2,'x'=4,'zp'=4,'zb'=2,'c'=2] {'zb','c'}, dimensions={0}, use_global_device_ids=true | all-gather | bytes 1146880 | tf_op jit(solution)/shard_map/all_gather | solution.py:162
  47.1 9.4 %all-gather.1 = bf16[1792,256]{1,0:T(8,128)(2,1)S(1)} all-gather(bf16[448,256]{1,0:T(8,128)(2,1)S(1)} %bitcast.43), channel_id=3, replica_groups=mesh['y'=8,'zh'=2,'x'=4,'zp'=4,'zb'=2,'c'=2] {'zb','c'}, dimensions={0}, use_global_device_ids=true | all-gather | bytes 1146880 | tf_op jit(solution)/shard_map/all_gather | solution.py:163
  56.5 1.7 shard_map.111
  58.2 6.8 %all-to-all-start.1 = ((bf16[8,32,2048]{2,1,0:T(8,128)(2,1)}), bf16[8,32,2048]{2,1,0:T(8,128)(2,1)S(1)}, u32[]{:S(2)}, u32[]{:S(2)}) async-start(bf16[8,32,2048]{2,1,0:T(8,128)(2,1)} %bitcast.10), calls=%async_computation.1 | async-start | bytes 2097152 | tf_op jit(solution)/shard_map/all_to_all | solution.py:124
  65.0 9.6 %all-gather.2 = bf16[1792,256]{1,0:T(8,128)(2,1)S(1)} all-gather(bf16[448,256]{1,0:T(8,128)(2,1)} %bitcast.44), channel_id=4, replica_groups=mesh['y'=8,'zh'=2,'x'=4,'zp'=4,'zb'=2,'c'=2] {'zb','c'}, dimensions={0}, use_global_device_ids=true | all-gather | bytes 1146880 | tf_op jit(solution)/shard_map/all_gather | solution.py:165
  74.7 1.3 shard_map.112
  75.9 0.9 copy-done
  76.9 17.4 %all-to-all-done.1 = bf16[8,32,2048]{2,1,0:T(8,128)(2,1)S(1)} async-done(((bf16[8,32,2048]{2,1,0:T(8,128)(2,1)}), bf16[8,32,2048]{2,1,0:T(8,128)(2,1)S(1)}, u32[]{:S(2)}, u32[]{:S(2)}) %all-to-all-start.1) | async-done | bytes 1048608 | tf_op jit(solution)/shard_map/all_to_all | solution.py:124
  94.3 1.0 copy-done.19
  95.3 4.2 %all-to-all-start.2 = ((bf16[8,32,1024]{2,1,0:T(8,128)(2,1)}), bf16[8,32,1024]{2,1,0:T(8,128)(2,1)}, u32[]{:S(2)}, u32[]{:S(2)}) async-start(bf16[8,32,1024]{2,1,0:T(8,128)(2,1)} %bitcast.12), calls=%async_computation.2 | async-start | bytes 1048576 | tf_op jit(solution)/shard_map/all_to_all | solution.py:124
  99.4 2.4 collective-permute-start.1
  101.8 2.0 collective-permute-start.2
  103.9 3.4 %collective-permute-start.3 = (bf16[256,896]{1,0:T(8,128)(2,1)S(1)}, bf16[256,896]{1,0:T(8,128)(2,1)}, u32[]{:S(2)}, u32[]{:S(2)}) collective-permute-start(bf16[256,896]{1,0:T(8,128)(2,1)S(1)} %bitcast.37), channel_id=1, source_target_pairs={{0,3},{1,2},{2,1},{3,0},{4,7},{5,6},{6,5},{7,4},{8,11},{9,10},{10,... | collective-permute-start | bytes 1376264 | tf_op jit(solution)/shard_map/ppermute | solution.py:144
  107.3 1.4 convert_reduce_fusion
  108.7 0.7 convert_element_type.28
  109.4 11.7 %collective-permute-start = (bf16[32,2048]{1,0:T(8,128)(2,1)}, bf16[32,2048]{1,0:T(8,128)(2,1)}, u32[]{:S(2)}, u32[]{:S(2)}) collective-permute-start(bf16[32,2048]{1,0:T(8,128)(2,1)} %convert_element_type.28), channel_id=1, source_target_pairs={{0,64},{64,0},{1,65},{65,1},{2,66},{66,2},{3,67},{67,3},{4,68},{68... | collective-permute-start | bytes 393224 | tf_op jit(solution)/shard_map/ppermute | solution.py:134
  121.1 1.8 convert_reduce_fusion.1
  122.9 20.0 %collective-permute-done = bf16[32,2048]{1,0:T(8,128)(2,1)} collective-permute-done((bf16[32,2048]{1,0:T(8,128)(2,1)}, bf16[32,2048]{1,0:T(8,128)(2,1)}, u32[]{:S(2)}, u32[]{:S(2)}) %collective-permute-start) | collective-permute-done | bytes 131104 | tf_op jit(solution)/shard_map/ppermute | solution.py:134
  142.9 0.9 convert_add_fusion
  143.9 0.0 copy-start.22
  143.9 0.0 copy-start.5
  144.0 0.6 copy-done.20
  144.6 0.8 copy-done.7
  145.3 0.9 broadcast_in_dim.22
  146.2 6.8 %all-to-all-start.4 = ((bf16[8,32,1024]{2,1,0:T(8,128)(2,1)}), bf16[8,32,1024]{2,1,0:T(8,128)(2,1)S(1)}, u32[]{:S(2)}, u32[]{:S(2)}) async-start(bf16[8,32,1024]{2,1,0:T(8,128)(2,1)} %broadcast_in_dim.22), calls=%async_computation.4 | async-start | bytes 1048576 | tf_op jit(solution)/shard_map/all_to_all | solution.py:124
  153.0 2.1 collective-permute-start.4
  155.1 11.6 %collective-permute-done.4 = bf16[32,1024]{1,0:T(8,128)(2,1)S(1)} collective-permute-done((bf16[32,1024]{1,0:T(8,128)(2,1)S(1)}, bf16[32,1024]{1,0:T(8,128)(2,1)S(1)}, u32[]{:S(2)}, u32[]{:S(2)}) %collective-permute-start.4) | collective-permute-done | bytes 65568 | tf_op jit(solution)/shard_map/ppermute | solution.py:134
  166.8 0.1 multiply_convert_fusion.1
  166.9 3.2 %all-to-all-done.4 = bf16[8,32,1024]{2,1,0:T(8,128)(2,1)S(1)} async-done(((bf16[8,32,1024]{2,1,0:T(8,128)(2,1)}), bf16[8,32,1024]{2,1,0:T(8,128)(2,1)S(1)}, u32[]{:S(2)}, u32[]{:S(2)}) %all-to-all-start.4) | async-done | bytes 524320 | tf_op jit(solution)/shard_map/all_to_all | solution.py:124
  170.0 1.1 broadcast_in_dim.10
  171.2 3.6 %all-to-all-start.3 = ((bf16[8,32,2048]{2,1,0:T(8,128)(2,1)}), bf16[8,32,2048]{2,1,0:T(8,128)(2,1)S(1)}, u32[]{:S(2)}, u32[]{:S(2)}) async-start(bf16[8,32,2048]{2,1,0:T(8,128)(2,1)} %broadcast_in_dim.10), calls=%async_computation.3 | async-start | bytes 2097152 | tf_op jit(solution)/shard_map/all_to_all | solution.py:124
  174.8 0.1 constant_dynamic-slice_fusion.8
  174.8 4.7 %collective-permute-start.5 = (bf16[256,256]{1,0:T(8,128)(2,1)S(1)}, bf16[256,256]{1,0:T(8,128)(2,1)S(1)}, u32[]{:S(2)}, u32[]{:S(2)}) collective-permute-start(bf16[256,256]{1,0:T(8,128)(2,1)S(1)} %get-tuple-element.69), channel_id=1, source_target_pairs={{0,1},{1,0},{2,3},{3,2},{4,5},{5,4},{6,7},{7,6},{8,9},{9,8},{10,11... | collective-permute-start | bytes 393224 | tf_op jit(solution)/shard_map/ppermute | solution.py:144
  179.6 2.9 %collective-permute-start.6 = (bf16[256,256]{1,0:T(8,128)(2,1)S(1)}, bf16[256,256]{1,0:T(8,128)(2,1)S(1)}, u32[]{:S(2)}, u32[]{:S(2)}) collective-permute-start(bf16[256,256]{1,0:T(8,128)(2,1)S(1)} %get-tuple-element.68), channel_id=1, source_target_pairs={{0,2},{1,3},{2,0},{3,1},{4,6},{5,7},{6,4},{7,5},{8,10},{9,11},{10,... | collective-permute-start | bytes 393224 | tf_op jit(solution)/shard_map/ppermute | solution.py:144
  182.5 2.6 %collective-permute-start.7 = (bf16[256,256]{1,0:T(8,128)(2,1)S(1)}, bf16[256,256]{1,0:T(8,128)(2,1)S(1)}, u32[]{:S(2)}, u32[]{:S(2)}) collective-permute-start(bf16[256,256]{1,0:T(8,128)(2,1)S(1)} %get-tuple-element.67), channel_id=1, source_target_pairs={{0,3},{1,2},{2,1},{3,0},{4,7},{5,6},{6,5},{7,4},{8,11},{9,10},{10,... | collective-permute-start | bytes 393224 | tf_op jit(solution)/shard_map/ppermute | solution.py:144
  185.1 0.0 copy-start.9
  185.1 0.6 copy-done.9
  185.7 0.9 collective-permute-done.6.refs_6_
  186.6 0.7 copy-done.11
  187.3 2.8 %collective-permute-done.7.refs_7_ = bf16[256,256]{1,0:T(8,128)(2,1)S(1)} collective-permute-done((bf16[256,256]{1,0:T(8,128)(2,1)S(1)}, bf16[256,256]{1,0:T(8,128)(2,1)S(1)}, u32[]{:S(2)}, u32[]{:S(2)}) %collective-permute-start.7) | collective-permute-done | bytes 131104 | tf_op jit(solution)/shard_map/ppermute | solution.py:144
  190.1 0.6 copy-done.13
  190.7 10.9 %all-to-all-done.3 = bf16[8,32,2048]{2,1,0:T(8,128)(2,1)S(1)} async-done(((bf16[8,32,2048]{2,1,0:T(8,128)(2,1)}), bf16[8,32,2048]{2,1,0:T(8,128)(2,1)S(1)}, u32[]{:S(2)}, u32[]{:S(2)}) %all-to-all-start.3) | async-done | bytes 1048608 | tf_op jit(solution)/shard_map/all_to_all | solution.py:124
  201.7 1.2 copy-done.1
  202.8 1.1 shard_map.113
  203.9 0.8 copy-done.4
  204.7 14.7 %all-to-all-start.5 = ((bf16[16,16,896]{2,1,0:T(8,128)(2,1)}), bf16[16,16,896]{2,1,0:T(8,128)(2,1)S(1)}, u32[]{:S(2)}, u32[]{:S(2)}) async-start(bf16[16,16,896]{2,1,0:T(8,128)(2,1)} %bitcast.41), calls=%async_computation.5 | async-start | bytes 917504 | tf_op jit(solution)/shard_map/all_to_all | solution.py:124
  219.4 0.1 constant_dynamic-slice_fusion.1
  219.5 0.0 copy-start.6
  219.5 0.0 copy-start.8
  219.6 3.1 %collective-permute-start.8 = (bf16[256,512]{1,0:T(8,128)(2,1)S(1)}, bf16[256,512]{1,0:T(8,128)(2,1)S(1)}, u32[]{:S(2)}, u32[]{:S(2)}) collective-permute-start(bf16[256,512]{1,0:T(8,128)(2,1)S(1)} %pad_maximum_fusion.1), channel_id=1, source_target_pairs={{0,1},{1,0},{2,3},{3,2},{4,5},{5,4},{6,7},{7,6},{8,9},{9,8},{10,11... | collective-permute-start | bytes 786440 | tf_op jit(solution)/shard_map/ppermute | solution.py:144
  222.7 3.1 %collective-permute-start.9 = (bf16[256,512]{1,0:T(8,128)(2,1)S(1)}, bf16[256,512]{1,0:T(8,128)(2,1)S(1)}, u32[]{:S(2)}, u32[]{:S(2)}) collective-permute-start(bf16[256,512]{1,0:T(8,128)(2,1)S(1)} %pad_maximum_fusion.2), channel_id=1, source_target_pairs={{0,2},{1,3},{2,0},{3,1},{4,6},{5,7},{6,4},{7,5},{8,10},{9,11},{10,... | collective-permute-start | bytes 786440 | tf_op jit(solution)/shard_map/ppermute | solution.py:144
  225.9 2.4 collective-permute-start.10
  228.3 2.8 %shard_map.116 = f32[448,256]{1,0:T(8,128)} custom-call(bf16[256,896]{1,0:T(8,128)(2,1)S(1)} %bitcast.38, bf16[256,896]{1,0:T(8,128)(2,1)S(1)} %copy-done.6, bf16[256,896]{1,0:T(8,128)(2,1)S(1)} %copy-done.8, bf16[256,896]{1,0:T(8,128)(2,1)} %collective-permute-done.3.refs_3_, bf16[256,256]{1,0:T(8,128)(2,1)S(1)} %get-tuple-element.55.refs_4_, ...), custom_call_target="tpu_custom_call" | custom-call | flops 2000000000 | bytes 5636096 | tf_op jit(solution)/shard_map/pallas_call | solution.py:33
  231.1 13.5 %collective-permute-done.9.refs_6_ = bf16[256,512]{1,0:T(8,128)(2,1)S(1)} collective-permute-done((bf16[256,512]{1,0:T(8,128)(2,1)S(1)}, bf16[256,512]{1,0:T(8,128)(2,1)S(1)}, u32[]{:S(2)}, u32[]{:S(2)}) %collective-permute-start.9) | collective-permute-done | bytes 262176 | tf_op jit(solution)/shard_map/ppermute | solution.py:144
  244.6 5.6 %collective-permute-done.10.refs_7_ = bf16[256,512]{1,0:T(8,128)(2,1)S(1)} collective-permute-done((bf16[256,512]{1,0:T(8,128)(2,1)S(1)}, bf16[256,512]{1,0:T(8,128)(2,1)S(1)}, u32[]{:S(2)}, u32[]{:S(2)}) %collective-permute-start.10) | collective-permute-done | bytes 262176 | tf_op jit(solution)/shard_map/ppermute | solution.py:144
  250.2 2.6 %shard_map.115 = (f32[448,256]{1,0:T(8,128)}, f32[448,256]{1,0:T(8,128)}) custom-call(bf16[256,896]{1,0:T(8,128)(2,1)S(1)} %bitcast.39, bf16[256,896]{1,0:T(8,128)(2,1)S(1)} %copy-done.6, bf16[256,896]{1,0:T(8,128)(2,1)S(1)} %copy-done.8, bf16[256,896]{1,0:T(8,128)(2,1)} %collective-permute-done.3.refs_3_, bf16[256,512]{1,0:T(8,128)(2,1)S(1)} %pad_maximum_fusion.refs_4_, ...), custom_call_target="tpu_custom_call" | custom-call | flops 2000000000 | bytes 7602176 | tf_op jit(solution)/shard_map/pallas_call | solution.py:33
  252.8 1.0 shard_map.114
  (48 shorter events, 0.2 us)
Async XLA Ops:
  2.1 0.8 copy-start.15
  3.0 0.8 copy-start.16
  5.1 0.6 copy-start.17
  5.1 15.2 %copy-start.23 = (bf16[1,448,256]{2,1,0:T(8,128)(2,1)S(1)}, bf16[1,448,256]{2,1,0:T(8,128)(2,1)}, u32[]{:S(2)}) copy-start(bf16[1,448,256]{2,1,0:T(8,128)(2,1)} %param.11) | copy-start | bytes 688132
  5.1 42.0 %copy-start.24 = (bf16[1,448,256]{2,1,0:T(8,128)(2,1)S(1)}, bf16[1,448,256]{2,1,0:T(8,128)(2,1)}, u32[]{:S(2)}) copy-start(bf16[1,448,256]{2,1,0:T(8,128)(2,1)} %param.12) | copy-start | bytes 688132
  5.7 50.8 %all-to-all-start = ((bf16[16,16,896]{2,1,0:T(8,128)(2,1)}), bf16[16,16,896]{2,1,0:T(8,128)(2,1)S(1)}, u32[]{:S(2)}, u32[]{:S(2)}) async-start(bf16[16,16,896]{2,1,0:T(8,128)(2,1)} %bitcast.4), calls=%async_computation | async-start | bytes 917504 | tf_op jit(solution)/shard_map/all_to_all | solution.py:124
  56.5 47.4 %copy-start.2 = (bf16[16,16,896]{2,1,0:T(8,128)(2,1)}, bf16[16,16,896]{2,1,0:T(8,128)(2,1)S(1)}, u32[]{:S(2)}) copy-start(bf16[16,16,896]{2,1,0:T(8,128)(2,1)S(1)} %all-to-all-done) | copy-start | bytes 1376260
  58.2 36.1 %all-to-all-start.1 = ((bf16[8,32,2048]{2,1,0:T(8,128)(2,1)}), bf16[8,32,2048]{2,1,0:T(8,128)(2,1)S(1)}, u32[]{:S(2)}, u32[]{:S(2)}) async-start(bf16[8,32,2048]{2,1,0:T(8,128)(2,1)} %bitcast.10), calls=%async_computation.1 | async-start | bytes 2097152 | tf_op jit(solution)/shard_map/all_to_all | solution.py:124
  75.9 0.9 copy-start
  94.3 1.0 copy-start.19
  95.3 25.8 %all-to-all-start.2 = ((bf16[8,32,1024]{2,1,0:T(8,128)(2,1)}), bf16[8,32,1024]{2,1,0:T(8,128)(2,1)}, u32[]{:S(2)}, u32[]{:S(2)}) async-start(bf16[8,32,1024]{2,1,0:T(8,128)(2,1)} %bitcast.12), calls=%async_computation.2 | async-start | bytes 1048576 | tf_op jit(solution)/shard_map/all_to_all | solution.py:124
  99.4 44.5 %collective-permute-start.1 = (bf16[256,896]{1,0:T(8,128)(2,1)S(1)}, bf16[256,896]{1,0:T(8,128)(2,1)S(1)}, u32[]{:S(2)}, u32[]{:S(2)}) collective-permute-start(bf16[256,896]{1,0:T(8,128)(2,1)S(1)} %bitcast.35), channel_id=1, source_target_pairs={{0,1},{1,0},{2,3},{3,2},{4,5},{5,4},{6,7},{7,6},{8,9},{9,8},{10,11... | collective-permute-start | bytes 1376264 | tf_op jit(solution)/shard_map/ppermute | solution.py:144
  101.8 42.1 %collective-permute-start.2 = (bf16[256,896]{1,0:T(8,128)(2,1)S(1)}, bf16[256,896]{1,0:T(8,128)(2,1)S(1)}, u32[]{:S(2)}, u32[]{:S(2)}) collective-permute-start(bf16[256,896]{1,0:T(8,128)(2,1)S(1)} %bitcast.36), channel_id=1, source_target_pairs={{0,2},{1,3},{2,0},{3,1},{4,6},{5,7},{6,4},{7,5},{8,10},{9,11},{10,... | collective-permute-start | bytes 1376264 | tf_op jit(solution)/shard_map/ppermute | solution.py:144
  103.9 41.4 %collective-permute-start.3 = (bf16[256,896]{1,0:T(8,128)(2,1)S(1)}, bf16[256,896]{1,0:T(8,128)(2,1)}, u32[]{:S(2)}, u32[]{:S(2)}) collective-permute-start(bf16[256,896]{1,0:T(8,128)(2,1)S(1)} %bitcast.37), channel_id=1, source_target_pairs={{0,3},{1,2},{2,1},{3,0},{4,7},{5,6},{6,5},{7,4},{8,11},{9,10},{10,... | collective-permute-start | bytes 1376264 | tf_op jit(solution)/shard_map/ppermute | solution.py:144
  109.4 33.5 %collective-permute-start = (bf16[32,2048]{1,0:T(8,128)(2,1)}, bf16[32,2048]{1,0:T(8,128)(2,1)}, u32[]{:S(2)}, u32[]{:S(2)}) collective-permute-start(bf16[32,2048]{1,0:T(8,128)(2,1)} %convert_element_type.28), channel_id=1, source_target_pairs={{0,64},{64,0},{1,65},{65,1},{2,66},{66,2},{3,67},{67,3},{4,68},{68... | collective-permute-start | bytes 393224 | tf_op jit(solution)/shard_map/ppermute | solution.py:134
  143.8 0.7 copy-start.20
  143.9 9.2 %copy-start.22 = (f32[32,1024]{1,0:T(8,128)S(1)}, f32[32,1024]{1,0:T(8,128)}, u32[]{:S(2)}) copy-start(f32[32,1024]{1,0:T(8,128)} %convert_reduce_fusion.1) | copy-start | bytes 393220
  143.9 22.9 %copy-start.5 = (bf16[256,896]{1,0:T(8,128)(2,1)}, bf16[256,896]{1,0:T(8,128)(2,1)S(1)}, u32[]{:S(2)}) copy-start(bf16[256,896]{1,0:T(8,128)(2,1)S(1)} %collective-permute-done.1.refs_1_) | copy-start | bytes 1376260
  144.6 0.8 copy-start.7
  145.3 21.4 %copy-start.21 = (f32[32,2048]{1,0:T(8,128)S(1)}, f32[32,2048]{1,0:T(8,128)}, u32[]{:S(2)}) copy-start(f32[32,2048]{1,0:T(8,128)} %copy-done.20) | copy-start | bytes 786436
  146.2 23.8 %all-to-all-start.4 = ((bf16[8,32,1024]{2,1,0:T(8,128)(2,1)}), bf16[8,32,1024]{2,1,0:T(8,128)(2,1)S(1)}, u32[]{:S(2)}, u32[]{:S(2)}) async-start(bf16[8,32,1024]{2,1,0:T(8,128)(2,1)} %broadcast_in_dim.22), calls=%async_computation.4 | async-start | bytes 1048576 | tf_op jit(solution)/shard_map/all_to_all | solution.py:124
  153.0 13.7 %collective-permute-start.4 = (bf16[32,1024]{1,0:T(8,128)(2,1)S(1)}, bf16[32,1024]{1,0:T(8,128)(2,1)S(1)}, u32[]{:S(2)}, u32[]{:S(2)}) collective-permute-start(bf16[32,1024]{1,0:T(8,128)(2,1)S(1)} %convert_element_type.32), channel_id=1, source_target_pairs={{0,64},{64,0},{1,65},{65,1},{2,66},{66,2},{3,67},{67,3},{4,68},{68... | collective-permute-start | bytes 196616 | tf_op jit(solution)/shard_map/ppermute | solution.py:134
  171.2 30.5 %all-to-all-start.3 = ((bf16[8,32,2048]{2,1,0:T(8,128)(2,1)}), bf16[8,32,2048]{2,1,0:T(8,128)(2,1)S(1)}, u32[]{:S(2)}, u32[]{:S(2)}) async-start(bf16[8,32,2048]{2,1,0:T(8,128)(2,1)} %broadcast_in_dim.10), calls=%async_computation.3 | async-start | bytes 2097152 | tf_op jit(solution)/shard_map/all_to_all | solution.py:124
  174.8 10.2 %collective-permute-start.5 = (bf16[256,256]{1,0:T(8,128)(2,1)S(1)}, bf16[256,256]{1,0:T(8,128)(2,1)S(1)}, u32[]{:S(2)}, u32[]{:S(2)}) collective-permute-start(bf16[256,256]{1,0:T(8,128)(2,1)S(1)} %get-tuple-element.69), channel_id=1, source_target_pairs={{0,1},{1,0},{2,3},{3,2},{4,5},{5,4},{6,7},{7,6},{8,9},{9,8},{10,11... | collective-permute-start | bytes 393224 | tf_op jit(solution)/shard_map/ppermute | solution.py:144
  179.6 7.0 %collective-permute-start.6 = (bf16[256,256]{1,0:T(8,128)(2,1)S(1)}, bf16[256,256]{1,0:T(8,128)(2,1)S(1)}, u32[]{:S(2)}, u32[]{:S(2)}) collective-permute-start(bf16[256,256]{1,0:T(8,128)(2,1)S(1)} %get-tuple-element.68), channel_id=1, source_target_pairs={{0,2},{1,3},{2,0},{3,1},{4,6},{5,7},{6,4},{7,5},{8,10},{9,11},{10,... | collective-permute-start | bytes 393224 | tf_op jit(solution)/shard_map/ppermute | solution.py:144
  182.5 7.6 %collective-permute-start.7 = (bf16[256,256]{1,0:T(8,128)(2,1)S(1)}, bf16[256,256]{1,0:T(8,128)(2,1)S(1)}, u32[]{:S(2)}, u32[]{:S(2)}) collective-permute-start(bf16[256,256]{1,0:T(8,128)(2,1)S(1)} %get-tuple-element.67), channel_id=1, source_target_pairs={{0,3},{1,2},{2,1},{3,0},{4,7},{5,6},{6,5},{7,4},{8,11},{9,10},{10,... | collective-permute-start | bytes 393224 | tf_op jit(solution)/shard_map/ppermute | solution.py:144
  185.1 0.7 copy-start.9
  186.6 0.7 copy-start.11
  190.1 0.6 copy-start.13
  201.7 1.2 copy-start.1
  203.9 0.8 copy-start.4
  204.7 48.1 %all-to-all-start.5 = ((bf16[16,16,896]{2,1,0:T(8,128)(2,1)}), bf16[16,16,896]{2,1,0:T(8,128)(2,1)S(1)}, u32[]{:S(2)}, u32[]{:S(2)}) async-start(bf16[16,16,896]{2,1,0:T(8,128)(2,1)} %bitcast.41), calls=%async_computation.5 | async-start | bytes 917504 | tf_op jit(solution)/shard_map/all_to_all | solution.py:124
  219.5 8.8 %copy-start.3 = (bf16[16,16,896]{2,1,0:T(8,128)(2,1)S(1)}, bf16[16,16,896]{2,1,0:T(8,128)(2,1)}, u32[]{:S(2)}) copy-start(bf16[16,16,896]{2,1,0:T(8,128)(2,1)} %copy-done.2) | copy-start | bytes 1376260
  219.5 8.8 %copy-start.6 = (bf16[256,896]{1,0:T(8,128)(2,1)S(1)}, bf16[256,896]{1,0:T(8,128)(2,1)}, u32[]{:S(2)}) copy-start(bf16[256,896]{1,0:T(8,128)(2,1)} %copy-done.5) | copy-start | bytes 1376260
  219.5 8.8 %copy-start.8 = (bf16[256,896]{1,0:T(8,128)(2,1)S(1)}, bf16[256,896]{1,0:T(8,128)(2,1)}, u32[]{:S(2)}) copy-start(bf16[256,896]{1,0:T(8,128)(2,1)} %copy-done.7) | copy-start | bytes 1376260
  219.6 8.8 %copy-start.10 = (bf16[256,256]{1,0:T(8,128)(2,1)S(1)}, bf16[256,256]{1,0:T(8,128)(2,1)}, u32[]{:S(2)}) copy-start(bf16[256,256]{1,0:T(8,128)(2,1)} %copy-done.9) | copy-start | bytes 393220
  219.6 8.7 %copy-start.12 = (bf16[256,256]{1,0:T(8,128)(2,1)S(1)}, bf16[256,256]{1,0:T(8,128)(2,1)}, u32[]{:S(2)}) copy-start(bf16[256,256]{1,0:T(8,128)(2,1)} %copy-done.11) | copy-start | bytes 393220
  219.6 8.7 %copy-start.14 = (bf16[256,256]{1,0:T(8,128)(2,1)S(1)}, bf16[256,256]{1,0:T(8,128)(2,1)}, u32[]{:S(2)}) copy-start(bf16[256,256]{1,0:T(8,128)(2,1)} %copy-done.13) | copy-start | bytes 393220
  219.6 11.5 %collective-permute-start.8 = (bf16[256,512]{1,0:T(8,128)(2,1)S(1)}, bf16[256,512]{1,0:T(8,128)(2,1)S(1)}, u32[]{:S(2)}, u32[]{:S(2)}) collective-permute-start(bf16[256,512]{1,0:T(8,128)(2,1)S(1)} %pad_maximum_fusion.1), channel_id=1, source_target_pairs={{0,1},{1,0},{2,3},{3,2},{4,5},{5,4},{6,7},{7,6},{8,9},{9,8},{10,11... | collective-permute-start | bytes 786440 | tf_op jit(solution)/shard_map/ppermute | solution.py:144
  222.7 21.9 %collective-permute-start.9 = (bf16[256,512]{1,0:T(8,128)(2,1)S(1)}, bf16[256,512]{1,0:T(8,128)(2,1)S(1)}, u32[]{:S(2)}, u32[]{:S(2)}) collective-permute-start(bf16[256,512]{1,0:T(8,128)(2,1)S(1)} %pad_maximum_fusion.2), channel_id=1, source_target_pairs={{0,2},{1,3},{2,0},{3,1},{4,6},{5,7},{6,4},{7,5},{8,10},{9,11},{10,... | collective-permute-start | bytes 786440 | tf_op jit(solution)/shard_map/ppermute | solution.py:144
  225.9 24.3 %collective-permute-start.10 = (bf16[256,512]{1,0:T(8,128)(2,1)S(1)}, bf16[256,512]{1,0:T(8,128)(2,1)S(1)}, u32[]{:S(2)}, u32[]{:S(2)}) collective-permute-start(bf16[256,512]{1,0:T(8,128)(2,1)S(1)} %pad_maximum_fusion.3), channel_id=1, source_target_pairs={{0,3},{1,2},{2,1},{3,0},{4,7},{5,6},{6,5},{7,4},{8,11},{9,10},{10,... | collective-permute-start | bytes 786440 | tf_op jit(solution)/shard_map/ppermute | solution.py:144
  231.1 21.7 %copy-start.18 = (bf16[256,128]{1,0:T(8,128)(2,1)S(1)}, bf16[256,128]{1,0:T(8,128)(2,1)}, u32[]{:S(2)}) copy-start(bf16[256,128]{1,0:T(8,128)(2,1)} %copy-done.17) | copy-start | bytes 196612

commit v4 on v3

v4 whole, which is shorter than its diff:
```python
import math

import jax
import jax.numpy as jnp
from jax import lax
from jax.experimental import pallas as pl
from jax.experimental.pallas import tpu as pltpu
from jax.sharding import Mesh, PartitionSpec as P

TOP = 2
CAP = 16
EXPERTS = 16
SLICES = 4
OWN = ("x", "zp")
SLICE = ("zb", "c")
EP = OWN + SLICE
GRP = ("y", "zh")

PLAIN = (((1,), (0,)), ((), ()))
LAST = (((1,), (1,)), ((), ()))
FIRST = (((0,), (0,)), ((), ()))
F32 = jnp.float32
BF = jnp.bfloat16


def dot(a, b, dims=PLAIN):
    return lax.dot_general(a, b, dims, preferred_element_type=F32)


def local(kernel, outs, *args, fetch=0):
    size = sum(a.size * a.dtype.itemsize for a in args)
    size += sum(math.prod(shape) * jnp.dtype(kind).itemsize for shape, kind in outs)
    stay, total = len(args) - fetch, len(args)

    def fetching(*refs):
        results = refs[total : total + len(outs)]
        held, sems = refs[total + len(outs) : -1], refs[-1]
        moves = [
            pltpu.make_async_copy(refs[stay + i], held[i], sems.at[i]) for i in range(fetch)
        ]
        for move in moves:
            move.start()
        for move in moves:
            move.wait()
        kernel(*refs[:stay], *held, *results)

    scratch = [pltpu.VMEM(a.shape, a.dtype) for a in args[stay:]]
    return pl.pallas_call(
        fetching if fetch else kernel,
        out_shape=[jax.ShapeDtypeStruct(shape, kind) for shape, kind in outs],
        in_specs=[pl.BlockSpec(memory_space=pltpu.VMEM)] * stay
        + [pl.BlockSpec(memory_space=pltpu.HBM)] * fetch,
        out_specs=[pl.BlockSpec(memory_space=pltpu.VMEM)] * len(outs),
        scratch_shapes=scratch + [pltpu.SemaphoreType.DMA((fetch,))] if fetch else (),
        compiler_params=pltpu.CompilerParams(vmem_limit_bytes=(56 if fetch else 16) * 2**20),
        cost_estimate=pl.CostEstimate(
            flops=2 * 10**9, bytes_accessed=2 * size, transcendentals=0
        ),
    )(*args)


def pair(ref):
    return jnp.concatenate([ref[0:1], ref[1:2]], axis=1)


def hits(ids_ref):
    ids = pair(ids_ref)
    count = ids.shape[1]
    across = jnp.broadcast_to(ids, (count, count))
    first = lax.broadcasted_iota(jnp.int32, (count, count), 0)
    second = lax.broadcasted_iota(jnp.int32, (count, count), 1)
    earlier = (across.T == across) & (first < second)
    rank = jnp.sum(jnp.where(earlier, 1.0, 0.0), axis=0, keepdims=True)
    target = ids * CAP + rank.astype(jnp.int32)
    return lax.broadcasted_iota(jnp.int32, (EXPERTS * CAP, count), 0) == target


def pack_kernel(ids_ref, weight_ref, tokens_ref, grad_ref, send_ref):
    hit = hits(ids_ref)
    slot_weight = jnp.sum(jnp.where(hit, pair(weight_ref), 0.0), axis=1, keepdims=True)
    place = jnp.where(hit, 1.0, 0.0).astype(BF)
    tokens = tokens_ref[...]
    grads = grad_ref[...]
    rows = dot(place, jnp.concatenate([tokens, tokens], axis=0))
    grad_rows = slot_weight * dot(place, jnp.concatenate([grads, grads], axis=0))
    send_ref[...] = jnp.concatenate([rows, grad_rows], axis=1).astype(BF)


def pre_kernel(rows_ref, *refs):
    out_ref = refs[-1]
    width, hs = refs[0].shape[0], refs[0].shape[1] // 2
    half = out_ref.shape[1] // 2
    rows = rows_ref[:, :width]
    for s in range(SLICES):
        both = dot(rows, refs[s][...]).astype(BF)
        out_ref[:, s * hs : (s + 1) * hs] = both[:, :hs]
        out_ref[:, half + s * hs : half + (s + 1) * hs] = both[:, hs:]


def act_kernel(rows_ref, *refs):
    out_ref = refs[-1]
    width, hs = refs[0].shape
    rows = rows_ref[:, width:]
    for s in range(SLICES):
        out_ref[:, s * hs : (s + 1) * hs] = dot(rows, refs[s][...]).astype(BF)


def sum_kernel(got_ref, sum_ref, round_ref):
    total = jnp.sum(got_ref[...].astype(F32), axis=0)
    sum_ref[...] = total
    round_ref[...] = total.astype(BF)


def hidden_kernel(part_ref, other_ref, hidden_ref):
    units = part_ref.shape[1] // 2
    pre = part_ref[...] + other_ref[...].astype(F32)
    gate_pre, up_pre = pre[:, :units], pre[:, units:]
    hidden = (gate_pre * jax.nn.sigmoid(gate_pre) * up_pre).astype(BF)
    hidden_ref[...] = jnp.broadcast_to(hidden[None], hidden_ref.shape)


def delta_kernel(part_ref, other_ref, act_ref, act_other_ref, delta_ref):
    units = act_ref.shape[1]
    pre = part_ref[...] + other_ref[...].astype(F32)
    act_grad = act_ref[...] + act_other_ref[...].astype(F32)
    gate_pre, up_pre = pre[:, :units], pre[:, units:]
    sig = jax.nn.sigmoid(gate_pre)
    gate_delta = act_grad * up_pre * sig * (1.0 + gate_pre * (1.0 - sig))
    up_delta = act_grad * gate_pre * sig
    shape = (delta_ref.shape[0],) + act_ref.shape
    delta_ref[:, :, :units] = jnp.broadcast_to(gate_delta.astype(BF)[None], shape)
    delta_ref[:, :, units:] = jnp.broadcast_to(up_delta.astype(BF)[None], shape)


def back_kernel(hidden_ref, deltas_ref, *refs):
    out_ref = refs[-1]
    in_refs, down_refs = refs[:SLICES], refs[SLICES:-1]
    hs = down_refs[0].shape[1]
    half = deltas_ref.shape[1] // 2
    out_rows = in_rows = 0.0
    for s in range(SLICES):
        here = slice(s * hs, (s + 1) * hs)
        there = slice(half + s * hs, half + (s + 1) * hs)
        out_rows += dot(hidden_ref[:, here], down_refs[s][...], LAST)
        both = jnp.concatenate([deltas_ref[:, here], deltas_ref[:, there]], axis=1)
        in_rows += dot(both, in_refs[s][...], LAST)
    out_ref[...] = jnp.concatenate([out_rows, in_rows], axis=1).astype(BF)


def down_kernel(factor, *refs):
    rows_refs, unit_refs, grad_ref = refs[:SLICES], refs[SLICES:-1], refs[-1]
    width = grad_ref.shape[0]
    total = 0.0
    for rows_ref, unit_ref in zip(rows_refs, unit_refs):
        total += dot(rows_ref[:, width:], unit_ref[...], FIRST)
    grad_ref[...] = total * factor


def in_kernel(factor, *refs):
    rows_refs, unit_refs, grad_refs = refs[:SLICES], refs[SLICES:-2], refs[-2:]
    width, hs = grad_refs[0].shape
    total = 0.0
    for rows_ref, unit_ref in zip(rows_refs, unit_refs):
        total += dot(rows_ref[:, :width], unit_ref[...], FIRST)
    grad_refs[0][...] = total[:, :hs] * factor
    grad_refs[1][...] = total[:, hs:] * factor


def home_kernel(ids_ref, weight_ref, back_ref, mixed_ref, grad_ref):
    tok_rows, width = mixed_ref.shape
    place = jnp.where(hits(ids_ref), 1.0, 0.0).astype(BF)
    row = pair(weight_ref)
    count = row.shape[1]
    weight = jnp.broadcast_to(row, (count, count)).T[:, :1]
    per = dot(place, back_ref[...], FIRST)
    per_out = per[:, :width] * weight
    per_in = per[:, width:]
    mixed_ref[...] = per_out[:tok_rows] + per_out[tok_rows:]
    grad_ref[...] = per_in[:tok_rows] + per_in[tok_rows:]


def swap(value, axis):
    return lax.all_to_all(value, axis, split_axis=0, concat_axis=0, tiled=True)


def sum_y(part):
    rows, cols = part.shape
    got = swap(part.reshape(8, rows // 8, cols), "y")
    shape = (rows // 8, cols)
    return local(sum_kernel, [(shape, F32), (shape, BF)], got)


def swap_pair(value, axis):
    return lax.ppermute(value, axis, [(0, 1), (1, 0)])


def gather_y(copies):
    count, rows, cols = copies.shape
    return swap(copies, "y").reshape(count * rows, cols)


def to_slice(value, step):
    return lax.ppermute(value, SLICE, [(i, i ^ step) for i in range(SLICES)])


def share(value):
    across = swap_pair(value, "zb")
    return [value, swap_pair(value, "c"), across, swap_pair(across, "c")]


def body(tokens, expert_ids, route_weight, out_grad, w_gate, w_up, w_down):
    tok_rows, width = tokens.shape
    hs = w_gate.shape[2]
    units = SLICES * hs
    slots = EXPERTS * CAP
    ids, weight = expert_ids.T, route_weight.T
    (send,) = local(
        pack_kernel, [((slots, 2 * width), BF)], ids, weight, tokens, out_grad, fetch=4
    )
    send, w_gate, w_up = lax.optimization_barrier((send, w_gate, w_up))
    rows = swap(send.reshape(EXPERTS, CAP, 2 * width), OWN).reshape(slots, 2 * width)
    w_in = share(jnp.concatenate([w_gate[0], w_up[0]], axis=1))
    (pre_local,) = local(pre_kernel, [((slots, 2 * units), BF)], rows, *w_in)
    pre_local, rows, w_down = lax.optimization_barrier((pre_local, rows, w_down))
    pre_part, pre_round = sum_y(pre_local)
    w_out = share(w_down[0].T)
    every = share(rows)
    (act_local,) = local(act_kernel, [((slots, units), BF)], rows, *w_out)
    act_local, every = lax.optimization_barrier((act_local, every))
    act_part, act_round = sum_y(act_local)

    pre_other = swap_pair(pre_round, "zh")
    copies = (8, slots // 8)
    (hidden,) = local(hidden_kernel, [(copies + (units,), BF)], pre_part, pre_other)
    hidden, act_round = lax.optimization_barrier((hidden, act_round))
    hidden = gather_y(hidden)
    act_other = swap_pair(act_round, "zh")
    (deltas,) = local(
        delta_kernel, [(copies + (2 * units,), BF)], pre_part, pre_other, act_part, act_other
    )
    deltas = gather_y(deltas)

    def of_slice(value, blocks):
        cut = [
            [value[:, (b * SLICES + s) * hs :][:, :hs] for b in range(blocks)]
            for s in range(SLICES)
        ]
        cut = [jnp.concatenate(part, axis=1) for part in cut]
        return cut[:1] + [to_slice(cut[step], step) for step in (1, 2, 3)]

    hidden_own = of_slice(hidden, 1)
    deltas, hidden, hidden_own = lax.optimization_barrier((deltas, hidden, hidden_own))
    (back,) = local(
        back_kernel, [((slots, 2 * width), BF)], hidden, deltas, *w_in, *w_out, fetch=10
    )
    back = swap(back.reshape(EXPERTS, CAP, 2 * width), OWN).reshape(slots, 2 * width)

    factor = 1.0 / math.sqrt(8 * tok_rows)

    def down(*refs):
        down_kernel(factor, *refs)

    def into(*refs):
        in_kernel(factor, *refs)

    one = ((width, hs), F32)
    (down_grad,) = local(down, [one], *every, *hidden_own)
    gate_grad, up_grad = local(into, [one, one], *every, *of_slice(deltas, 2))
    mixed, tokens_grad = local(home_kernel, [((tok_rows, width), F32)] * 2, ids, weight, back)
    return (mixed, tokens_grad, gate_grad[None], up_grad[None], down_grad.T[None])


def solution(mesh):
    fine = Mesh(mesh.devices.reshape(8, 2, 4, 4, 2, 2), GRP + EP)
    return jax.shard_map(
        body,
        mesh=fine,
        in_specs=(
            P(EP, GRP),
            P(EP, None),
            P(EP, None),
            P(EP, GRP),
            P(EP, GRP, None),
            P(EP, GRP, None),
            P(EP, None, GRP),
        ),
        out_specs=(
            P(EP, GRP),
            P(EP, GRP),
            P(EP, GRP, None),
            P(EP, GRP, None),
            P(EP, None, GRP),
        ),
        check_vma=False,
    )
```

time: 255 us -> 224 us (0.88)
  blocking collectives: 45.9 us -> 0 us
  starting transfers between devices: 91 us -> 123 us
  local copies, waits for them, and re-layouts: 13.3 us -> 2.83 us
  waiting for transfers between devices: 85.9 us -> 79.7 us
  other arithmetic: 5.01 us -> 0.11 us
  Pallas kernels: 11.7 us -> 16.1 us
    all_gather x3 -> x0, blocking collectives: 45.9 us -> none  [the longest x1 26.8 us: body(): all_gate = lax.all_gather(w_gate, SLICE, axis=0)]
    ppermute x2 -> x11, starting transfers between devices: 13.8 us -> 49.1 us  [swap_pair(): return lax.ppermute(value, axis, [(0, 1), (1, 0)])]
    all_to_all x6, waiting for transfers between devices: 31.5 us -> 23 us  [swap(): return lax.all_to_all(value, axis, split_axis=0, concat_axis=0, tiled=True)]
    unnamed x50 -> x30, local copies, waits for them, and re-layouts: 9.58 us -> 1.43 us
    ppermute x9 -> x6, starting transfers between devices: 26.6 us -> 21.7 us  [to_slice(): return lax.ppermute(value, SLICE, [(i, i ^ step) for i in range(SLICES)])]
    pallas_call x7 -> x11, Pallas kernels: 11.7 us -> 16.1 us  [local(): pl.pallas_call(fetching if fetch else kernel, out_shape=[jax.ShapeDtypeSt...]
    reduce_sum x2 -> x0, other arithmetic: 3.17 us -> none  [sum_y(): return jnp.sum(got.astype(F32), axis=0)]
    ppermute x2 -> x11, waiting for transfers between devices: 31.6 us -> 34.5 us  [swap_pair(): return lax.ppermute(value, axis, [(0, 1), (1, 0)])]
  transfers between devices with their start and end apart: 17 -> 23, of which waited for: 9 -> 13; matrix products, arithmetic and copies ran while one was open for 2% -> 1% of each run, Pallas kernels for 3% -> 3%
where the time goes in v4:
time: 224 us; the launch traced here: 223 us
  starting transfers between devices  123 us (55%)
  waiting for transfers between devices  79.7 us (36%)
  Pallas kernels  16.1 us (7%)
  local copies, waits for them, and re-layouts  2.83 us (1%)
    all_to_all x6, starting transfers between devices, swap(): return lax.all_to_all(value, axis, split_axis=0, concat_axis=0, tiled=True)  52.2 us
    ppermute x11, starting transfers between devices, swap_pair(): return lax.ppermute(value, axis, [(0, 1), (1, 0)])  49.1 us
    ppermute x11, waiting for transfers between devices, swap_pair(): return lax.ppermute(value, axis, [(0, 1), (1, 0)])  34.5 us
    all_to_all x6, waiting for transfers between devices, swap(): return lax.all_to_all(value, axis, split_axis=0, concat_axis=0, tiled=True)  23 us
    ppermute x6, waiting for transfers between devices, to_slice(): return lax.ppermute(value, SLICE, [(i, i ^ step) for i in range(SLICES)])  22.2 us
    ppermute x6, starting transfers between devices, to_slice(): return lax.ppermute(value, SLICE, [(i, i ^ step) for i in range(SLICES)])  21.7 us
    pallas_call x11, Pallas kernels, local(): pl.pallas_call(fetching if fetch else kernel, out_shape=[jax.ShapeDtypeSt...  16.1 us
  transfers between devices with their start and end apart: 23, of which 13 were waited for; matrix products, arithmetic and copies ran while one was open for 1% of the time, Pallas kernels for 3%

profile of v4, /device:TPU:129, one launch (start us, length us, event | category | flops | bytes accessed | tf_op | source)
XLA Modules:
  0.0 222.7 jit_solution(4639914076175833550)
XLA Ops:
  0.6 2.2 %shard_map.110 = bf16[256,896]{1,0:T(8,128)(2,1)} custom-call(s32[2,64]{1,0:T(2,128)} %bitcast.31, f32[2,64]{1,0:T(2,128)} %bitcast.33, bf16[64,448]{1,0:T(8,128)(2,1)} %refs_2_.1, bf16[64,448]{1,0:T(8,128)(2,1)} %refs_3_.1), custom_call_target="tpu_custom_call" | custom-call | flops 2000000000 | bytes 1148928 | tf_op jit(solution)/shard_map/pallas_call | solution.py:48
  2.9 0.0 copy-start.13
  2.9 0.0 copy-start.14
  2.9 14.7 %all-to-all-start = ((bf16[16,16,896]{2,1,0:T(8,128)(2,1)}), bf16[16,16,896]{2,1,0:T(8,128)(2,1)S(1)}, u32[]{:S(2)}, u32[]{:S(2)}) async-start(bf16[16,16,896]{2,1,0:T(8,128)(2,1)} %bitcast.38), calls=%async_computation | async-start | bytes 917504 | tf_op jit(solution)/shard_map/all_to_all | solution.py:183
  17.6 0.0 copy-start
  17.7 4.0 %collective-permute-start.1 = (bf16[448,512]{1,0:T(8,128)(2,1)S(1)}, bf16[448,512]{1,0:T(8,128)(2,1)S(1)}, u32[]{:S(2)}, u32[]{:S(2)}) collective-permute-start(bf16[448,512]{1,0:T(8,128)(2,1)S(1)} %pad_maximum_fusion.refs_0_.refs_2_), channel_id=1, source_target_pairs={{0,2},{2,0},{1,3},{3,1},{4,6},{6,4},{5,7},{7,5},{8,10},{10,8},{9,1... | collective-permute-start | bytes 1376264 | tf_op jit(solution)/shard_map/ppermute | solution.py:194
  21.7 3.4 %collective-permute-start = (bf16[448,512]{1,0:T(8,128)(2,1)S(1)}, bf16[448,512]{1,0:T(8,128)(2,1)S(1)}, u32[]{:S(2)}, u32[]{:S(2)}) collective-permute-start(bf16[448,512]{1,0:T(8,128)(2,1)S(1)} %pad_maximum_fusion.refs_0_.refs_2_), channel_id=1, source_target_pairs={{0,1},{1,0},{2,3},{3,2},{4,5},{5,4},{6,7},{7,6},{8,9},{9,8},{10,11... | collective-permute-start | bytes 1376264 | tf_op jit(solution)/shard_map/ppermute | solution.py:194
  25.1 21.9 %collective-permute-done.1.refs_2_.refs_4_ = bf16[448,512]{1,0:T(8,128)(2,1)S(1)} collective-permute-done((bf16[448,512]{1,0:T(8,128)(2,1)S(1)}, bf16[448,512]{1,0:T(8,128)(2,1)S(1)}, u32[]{:S(2)}, u32[]{:S(2)}) %collective-permute-start.1) | collective-permute-done | bytes 458784 | tf_op jit(solution)/shard_map/ppermute | solution.py:194
  47.0 3.5 %collective-permute-start.2 = (bf16[448,512]{1,0:T(8,128)(2,1)S(1)}, bf16[448,512]{1,0:T(8,128)(2,1)S(1)}, u32[]{:S(2)}, u32[]{:S(2)}) collective-permute-start(bf16[448,512]{1,0:T(8,128)(2,1)S(1)} %collective-permute-done.1.refs_2_.refs_4_), channel_id=1, source_target_pairs={{0,1},{1,0},{2,3},{3,2},{4,5},{5,4},{6,7},{7,6},{8,9},{9,8},{10,11... | collective-permute-start | bytes 1376264 | tf_op jit(solution)/shard_map/ppermute | solution.py:194
  50.5 0.0 collective-permute-done.refs_1_.refs_3_
  50.5 0.0 copy-start.2
  50.5 1.4 collective-permute-done.2.refs_3_.refs_5_
  51.9 0.0 all-to-all-done
  51.9 1.7 shard_map.111
  53.7 0.0 copy-start.4
  53.7 7.0 %all-to-all-start.1 = ((bf16[8,32,2048]{2,1,0:T(8,128)(2,1)}), bf16[8,32,2048]{2,1,0:T(8,128)(2,1)S(1)}, u32[]{:S(2)}, u32[]{:S(2)}) async-start(bf16[8,32,2048]{2,1,0:T(8,128)(2,1)} %bitcast.6), calls=%async_computation.1 | async-start | bytes 2097152 | tf_op jit(solution)/shard_map/all_to_all | solution.py:183
  60.6 1.9 collective-permute-start.8
  62.6 3.4 %collective-permute-start.5 = (bf16[448,256]{1,0:T(8,128)(2,1)S(1)}, bf16[448,256]{1,0:T(8,128)(2,1)S(1)}, u32[]{:S(2)}, u32[]{:S(2)}) collective-permute-start(bf16[448,256]{1,0:T(8,128)(2,1)S(1)} %bitcast.28), channel_id=1, source_target_pairs={{0,2},{2,0},{1,3},{3,1},{4,6},{6,4},{5,7},{7,5},{8,10},{10,8},{9,1... | collective-permute-start | bytes 688136 | tf_op jit(solution)/shard_map/ppermute | solution.py:194
  65.9 3.1 %collective-permute-start.7 = (bf16[256,896]{1,0:T(8,128)(2,1)S(1)}, bf16[256,896]{1,0:T(8,128)(2,1)S(1)}, u32[]{:S(2)}, u32[]{:S(2)}) collective-permute-start(bf16[256,896]{1,0:T(8,128)(2,1)S(1)} %bitcast.22), channel_id=1, source_target_pairs={{0,1},{1,0},{2,3},{3,2},{4,5},{5,4},{6,7},{7,6},{8,9},{9,8},{10,11... | collective-permute-start | bytes 1376264 | tf_op jit(solution)/shard_map/ppermute | solution.py:194
  69.1 4.9 %collective-permute-done.8.refs_2_ = bf16[256,896]{1,0:T(8,128)(2,1)S(1)} collective-permute-done((bf16[256,896]{1,0:T(8,128)(2,1)S(1)}, bf16[256,896]{1,0:T(8,128)(2,1)S(1)}, u32[]{:S(2)}, u32[]{:S(2)}) %collective-permute-start.8) | collective-permute-done | bytes 458784 | tf_op jit(solution)/shard_map/ppermute | solution.py:194
  73.9 4.5 %collective-permute-start.9 = (bf16[256,896]{1,0:T(8,128)(2,1)S(1)}, bf16[256,896]{1,0:T(8,128)(2,1)S(1)}, u32[]{:S(2)}, u32[]{:S(2)}) collective-permute-start(bf16[256,896]{1,0:T(8,128)(2,1)S(1)} %collective-permute-done.8.refs_2_), channel_id=1, source_target_pairs={{0,1},{1,0},{2,3},{3,2},{4,5},{5,4},{6,7},{7,6},{8,9},{9,8},{10,11... | collective-permute-start | bytes 1376264 | tf_op jit(solution)/shard_map/ppermute | solution.py:194
  78.5 1.9 collective-permute-start.4
  80.4 0.0 collective-permute-done.5.refs_2_.refs_8_
  80.4 2.4 %collective-permute-start.6 = (bf16[448,256]{1,0:T(8,128)(2,1)S(1)}, bf16[448,256]{1,0:T(8,128)(2,1)S(1)}, u32[]{:S(2)}, u32[]{:S(2)}) collective-permute-start(bf16[448,256]{1,0:T(8,128)(2,1)S(1)} %collective-permute-done.5.refs_2_.refs_8_), channel_id=1, source_target_pairs={{0,1},{1,0},{2,3},{3,2},{4,5},{5,4},{6,7},{7,6},{8,9},{9,8},{10,11... | collective-permute-start | bytes 688136 | tf_op jit(solution)/shard_map/ppermute | solution.py:194
  82.8 0.0 collective-permute-done.4.refs_1_.refs_7_
  82.9 1.1 collective-permute-done.6.refs_3_.refs_9_
  83.9 1.3 shard_map.113
  85.2 0.0 collective-permute-done.7.refs_1_
  85.3 4.6 %all-to-all-done.1.got_ref = bf16[8,32,2048]{2,1,0:T(8,128)(2,1)S(1)} async-done(((bf16[8,32,2048]{2,1,0:T(8,128)(2,1)}), bf16[8,32,2048]{2,1,0:T(8,128)(2,1)S(1)}, u32[]{:S(2)}, u32[]{:S(2)}) %all-to-all-start.1) | async-done | bytes 1048608 | tf_op jit(solution)/shard_map/all_to_all | solution.py:183
  89.9 3.5 %all-to-all-start.2 = ((bf16[8,32,1024]{2,1,0:T(8,128)(2,1)}), bf16[8,32,1024]{2,1,0:T(8,128)(2,1)S(1)}, u32[]{:S(2)}, u32[]{:S(2)}) async-start(bf16[8,32,1024]{2,1,0:T(8,128)(2,1)} %bitcast.10), calls=%async_computation.2 | async-start | bytes 1048576 | tf_op jit(solution)/shard_map/all_to_all | solution.py:183
  93.4 0.1 shard_map.112
  93.5 0.0 copy-start.10
  93.5 0.7 copy-done.10
  94.2 11.8 %collective-permute-start.3 = (bf16[32,2048]{1,0:T(8,128)(2,1)S(1)}, bf16[32,2048]{1,0:T(8,128)(2,1)S(1)}, u32[]{:S(2)}, u32[]{:S(2)}) collective-permute-start(bf16[32,2048]{1,0:T(8,128)(2,1)S(1)} %get-tuple-element.37), channel_id=1, source_target_pairs={{0,64},{64,0},{1,65},{65,1},{2,66},{66,2},{3,67},{67,3},{4,68},{68... | collective-permute-start | bytes 393224 | tf_op jit(solution)/shard_map/ppermute | solution.py:194
  106.1 5.2 %all-to-all-done.2.got_ref = bf16[8,32,1024]{2,1,0:T(8,128)(2,1)S(1)} async-done(((bf16[8,32,1024]{2,1,0:T(8,128)(2,1)}), bf16[8,32,1024]{2,1,0:T(8,128)(2,1)S(1)}, u32[]{:S(2)}, u32[]{:S(2)}) %all-to-all-start.2) | async-done | bytes 524320 | tf_op jit(solution)/shard_map/all_to_all | solution.py:183
  111.3 0.1 shard_map.114
  111.3 0.6 collective-permute-done.3.other_ref
  111.9 0.9 shard_map.115
  112.8 6.6 %all-to-all-start.4 = ((bf16[8,32,1024]{2,1,0:T(8,128)(2,1)}), bf16[8,32,1024]{2,1,0:T(8,128)(2,1)S(1)}, u32[]{:S(2)}, u32[]{:S(2)}) async-start(bf16[8,32,1024]{2,1,0:T(8,128)(2,1)} %shard_map.115), calls=%async_computation.4 | async-start | bytes 1048576 | tf_op jit(solution)/shard_map/all_to_all | solution.py:183
  119.4 9.1 %collective-permute-start.10 = (bf16[32,1024]{1,0:T(8,128)(2,1)S(1)}, bf16[32,1024]{1,0:T(8,128)(2,1)S(1)}, u32[]{:S(2)}, u32[]{:S(2)}) collective-permute-start(bf16[32,1024]{1,0:T(8,128)(2,1)S(1)} %get-tuple-element.43), channel_id=1, source_target_pairs={{0,64},{64,0},{1,65},{65,1},{2,66},{66,2},{3,67},{67,3},{4,68},{68... | collective-permute-start | bytes 196616 | tf_op jit(solution)/shard_map/ppermute | solution.py:194
  128.5 4.6 %collective-permute-done.10.act_other_ref = bf16[32,1024]{1,0:T(8,128)(2,1)S(1)} collective-permute-done((bf16[32,1024]{1,0:T(8,128)(2,1)S(1)}, bf16[32,1024]{1,0:T(8,128)(2,1)S(1)}, u32[]{:S(2)}, u32[]{:S(2)}) %collective-permute-start.10) | collective-permute-done | bytes 65568 | tf_op jit(solution)/shard_map/ppermute | solution.py:194
  133.1 1.1 shard_map.116
  134.2 2.0 all-to-all-done.4
  136.3 4.6 %all-to-all-start.3 = ((bf16[8,32,2048]{2,1,0:T(8,128)(2,1)}), bf16[8,32,2048]{2,1,0:T(8,128)(2,1)}, u32[]{:S(2)}, u32[]{:S(2)}) async-start(bf16[8,32,2048]{2,1,0:T(8,128)(2,1)} %shard_map.116), calls=%async_computation.3 | async-start | bytes 2097152 | tf_op jit(solution)/shard_map/all_to_all | solution.py:183
  140.9 9.0 %collective-permute-start.13 = (bf16[256,256]{1,0:T(8,128)(2,1)S(1)}, bf16[256,256]{1,0:T(8,128)(2,1)S(1)}, u32[]{:S(2)}, u32[]{:S(2)}) collective-permute-start(bf16[256,256]{1,0:T(8,128)(2,1)S(1)} %get-tuple-element.67), channel_id=1, source_target_pairs={{0,3},{1,2},{2,1},{3,0},{4,7},{5,6},{6,5},{7,4},{8,11},{9,10},{10,... | collective-permute-start | bytes 393224 | tf_op jit(solution)/shard_map/ppermute | solution.py:203
  150.0 1.9 collective-permute-start.12
  151.9 2.3 %collective-permute-start.11 = (bf16[256,256]{1,0:T(8,128)(2,1)S(1)}, bf16[256,256]{1,0:T(8,128)(2,1)S(1)}, u32[]{:S(2)}, u32[]{:S(2)}) collective-permute-start(bf16[256,256]{1,0:T(8,128)(2,1)S(1)} %get-tuple-element.69), channel_id=1, source_target_pairs={{0,1},{1,0},{2,3},{3,2},{4,5},{5,4},{6,7},{7,6},{8,9},{9,8},{10,11... | collective-permute-start | bytes 393224 | tf_op jit(solution)/shard_map/ppermute | solution.py:203
  154.2 0.0 collective-permute-done.13.refs_7_
  154.2 2.5 %collective-permute-done.12.refs_6_ = bf16[256,256]{1,0:T(8,128)(2,1)S(1)} collective-permute-done((bf16[256,256]{1,0:T(8,128)(2,1)S(1)}, bf16[256,256]{1,0:T(8,128)(2,1)S(1)}, u32[]{:S(2)}, u32[]{:S(2)}) %collective-permute-start.12) | collective-permute-done | bytes 131104 | tf_op jit(solution)/shard_map/ppermute | solution.py:203
  156.7 0.0 collective-permute-done.11.refs_5_
  156.7 11.2 %all-to-all-done.3 = bf16[8,32,2048]{2,1,0:T(8,128)(2,1)} async-done(((bf16[8,32,2048]{2,1,0:T(8,128)(2,1)}), bf16[8,32,2048]{2,1,0:T(8,128)(2,1)}, u32[]{:S(2)}, u32[]{:S(2)}) %all-to-all-start.3) | async-done | bytes 1048608 | tf_op jit(solution)/shard_map/all_to_all | solution.py:183
  168.0 4.1 %shard_map.117 = bf16[256,896]{1,0:T(8,128)(2,1)} custom-call(bf16[256,1024]{1,0:T(8,128)(2,1)} %bitcast.36, bf16[256,2048]{1,0:T(8,128)(2,1)} %bitcast.11.refs_1_, bf16[448,512]{1,0:T(8,128)(2,1)} %copy-done, bf16[448,512]{1,0:T(8,128)(2,1)} %copy-done.2, bf16[448,512]{1,0:T(8,128)(2,1)} %copy-done.1, bf16[448,512]{1,0:T(8,128)(2,1)} %copy-done.3, ...), custom_call_target="tpu_custom_call" | custom-call | flops 2000000000 | bytes 9568256 | tf_op jit(solution)/shard_map/pallas_call | solution.py:48
  172.1 15.8 %all-to-all-start.5 = ((bf16[16,16,896]{2,1,0:T(8,128)(2,1)}), bf16[16,16,896]{2,1,0:T(8,128)(2,1)S(1)}, u32[]{:S(2)}, u32[]{:S(2)}) async-start(bf16[16,16,896]{2,1,0:T(8,128)(2,1)} %bitcast.37), calls=%async_computation.5 | async-start | bytes 917504 | tf_op jit(solution)/shard_map/all_to_all | solution.py:183
  187.9 1.4 fusion
  189.2 3.0 %collective-permute-start.14 = (bf16[256,512]{1,0:T(8,128)(2,1)S(1)}, bf16[256,512]{1,0:T(8,128)(2,1)S(1)}, u32[]{:S(2)}, u32[]{:S(2)}) collective-permute-start(bf16[256,512]{1,0:T(8,128)(2,1)S(1)} %pad_maximum_fusion.2), channel_id=1, source_target_pairs={{0,1},{1,0},{2,3},{3,2},{4,5},{5,4},{6,7},{7,6},{8,9},{9,8},{10,11... | collective-permute-start | bytes 786440 | tf_op jit(solution)/shard_map/ppermute | solution.py:203
  192.2 1.9 collective-permute-start.15
  194.2 3.5 %collective-permute-start.16 = (bf16[256,512]{1,0:T(8,128)(2,1)S(1)}, bf16[256,512]{1,0:T(8,128)(2,1)S(1)}, u32[]{:S(2)}, u32[]{:S(2)}) collective-permute-start(bf16[256,512]{1,0:T(8,128)(2,1)S(1)} %pad_maximum_fusion.4), channel_id=1, source_target_pairs={{0,3},{1,2},{2,1},{3,0},{4,7},{5,6},{6,5},{7,4},{8,11},{9,10},{10,... | collective-permute-start | bytes 786440 | tf_op jit(solution)/shard_map/ppermute | solution.py:203
  197.8 1.8 shard_map.120
  199.5 0.0 collective-permute-done.14.refs_5_
  199.5 14.1 %collective-permute-done.15.refs_6_ = bf16[256,512]{1,0:T(8,128)(2,1)S(1)} collective-permute-done((bf16[256,512]{1,0:T(8,128)(2,1)S(1)}, bf16[256,512]{1,0:T(8,128)(2,1)S(1)}, u32[]{:S(2)}, u32[]{:S(2)}) %collective-permute-start.15) | collective-permute-done | bytes 262176 | tf_op jit(solution)/shard_map/ppermute | solution.py:203
  213.6 5.6 %collective-permute-done.16.refs_7_ = bf16[256,512]{1,0:T(8,128)(2,1)S(1)} collective-permute-done((bf16[256,512]{1,0:T(8,128)(2,1)S(1)}, bf16[256,512]{1,0:T(8,128)(2,1)S(1)}, u32[]{:S(2)}, u32[]{:S(2)}) %collective-permute-start.16) | collective-permute-done | bytes 262176 | tf_op jit(solution)/shard_map/ppermute | solution.py:203
  219.2 1.6 shard_map.119
  220.8 0.7 copy-done.8
  221.5 1.2 shard_map.118
  (30 shorter events, 0.2 us)
Async XLA Ops:
  2.9 14.7 %copy-start.13 = (bf16[1,448,256]{2,1,0:T(8,128)(2,1)S(1)}, bf16[1,448,256]{2,1,0:T(8,128)(2,1)}, u32[]{:S(2)}) copy-start(bf16[1,448,256]{2,1,0:T(8,128)(2,1)} %param.12) | copy-start | bytes 688132
  2.9 14.7 %copy-start.14 = (bf16[1,448,256]{2,1,0:T(8,128)(2,1)S(1)}, bf16[1,448,256]{2,1,0:T(8,128)(2,1)}, u32[]{:S(2)}) copy-start(bf16[1,448,256]{2,1,0:T(8,128)(2,1)} %param.11) | copy-start | bytes 688132
  2.9 49.0 %all-to-all-start = ((bf16[16,16,896]{2,1,0:T(8,128)(2,1)}), bf16[16,16,896]{2,1,0:T(8,128)(2,1)S(1)}, u32[]{:S(2)}, u32[]{:S(2)}) async-start(bf16[16,16,896]{2,1,0:T(8,128)(2,1)} %bitcast.38), calls=%async_computation | async-start | bytes 917504 | tf_op jit(solution)/shard_map/all_to_all | solution.py:183
  17.6 36.0 %copy-start = (bf16[448,512]{1,0:T(8,128)(2,1)}, bf16[448,512]{1,0:T(8,128)(2,1)S(1)}, u32[]{:S(2)}) copy-start(bf16[448,512]{1,0:T(8,128)(2,1)S(1)} %pad_maximum_fusion.refs_0_.refs_2_) | copy-start | bytes 1376260
  17.7 29.3 %collective-permute-start.1 = (bf16[448,512]{1,0:T(8,128)(2,1)S(1)}, bf16[448,512]{1,0:T(8,128)(2,1)S(1)}, u32[]{:S(2)}, u32[]{:S(2)}) collective-permute-start(bf16[448,512]{1,0:T(8,128)(2,1)S(1)} %pad_maximum_fusion.refs_0_.refs_2_), channel_id=1, source_target_pairs={{0,2},{2,0},{1,3},{3,1},{4,6},{6,4},{5,7},{7,5},{8,10},{10,8},{9,1... | collective-permute-start | bytes 1376264 | tf_op jit(solution)/shard_map/ppermute | solution.py:194
  21.7 28.9 %collective-permute-start = (bf16[448,512]{1,0:T(8,128)(2,1)S(1)}, bf16[448,512]{1,0:T(8,128)(2,1)S(1)}, u32[]{:S(2)}, u32[]{:S(2)}) collective-permute-start(bf16[448,512]{1,0:T(8,128)(2,1)S(1)} %pad_maximum_fusion.refs_0_.refs_2_), channel_id=1, source_target_pairs={{0,1},{1,0},{2,3},{3,2},{4,5},{5,4},{6,7},{7,6},{8,9},{9,8},{10,11... | collective-permute-start | bytes 1376264 | tf_op jit(solution)/shard_map/ppermute | solution.py:194
  47.0 6.6 %copy-start.1 = (bf16[448,512]{1,0:T(8,128)(2,1)}, bf16[448,512]{1,0:T(8,128)(2,1)S(1)}, u32[]{:S(2)}) copy-start(bf16[448,512]{1,0:T(8,128)(2,1)S(1)} %collective-permute-done.1.refs_2_.refs_4_) | copy-start | bytes 1376260
  47.0 4.9 %collective-permute-start.2 = (bf16[448,512]{1,0:T(8,128)(2,1)S(1)}, bf16[448,512]{1,0:T(8,128)(2,1)S(1)}, u32[]{:S(2)}, u32[]{:S(2)}) collective-permute-start(bf16[448,512]{1,0:T(8,128)(2,1)S(1)} %collective-permute-done.1.refs_2_.refs_4_), channel_id=1, source_target_pairs={{0,1},{1,0},{2,3},{3,2},{4,5},{5,4},{6,7},{7,6},{8,9},{9,8},{10,11... | collective-permute-start | bytes 1376264 | tf_op jit(solution)/shard_map/ppermute | solution.py:194
  50.5 3.1 %copy-start.2 = (bf16[448,512]{1,0:T(8,128)(2,1)}, bf16[448,512]{1,0:T(8,128)(2,1)S(1)}, u32[]{:S(2)}) copy-start(bf16[448,512]{1,0:T(8,128)(2,1)S(1)} %collective-permute-done.refs_1_.refs_3_) | copy-start | bytes 1376260
  51.9 1.7 copy-start.3
  53.7 8.9 %copy-start.4 = (bf16[1,256,448]{1,2,0:T(8,128)(2,1)S(1)}, bf16[1,256,448]{1,2,0:T(8,128)(2,1)}, u32[]{:S(2)}) copy-start(bf16[1,256,448]{1,2,0:T(8,128)(2,1)} %param.13) | copy-start | bytes 688132
  53.7 36.2 %all-to-all-start.1 = ((bf16[8,32,2048]{2,1,0:T(8,128)(2,1)}), bf16[8,32,2048]{2,1,0:T(8,128)(2,1)S(1)}, u32[]{:S(2)}, u32[]{:S(2)}) async-start(bf16[8,32,2048]{2,1,0:T(8,128)(2,1)} %bitcast.6), calls=%async_computation.1 | async-start | bytes 2097152 | tf_op jit(solution)/shard_map/all_to_all | solution.py:183
  60.6 13.3 %collective-permute-start.8 = (bf16[256,896]{1,0:T(8,128)(2,1)S(1)}, bf16[256,896]{1,0:T(8,128)(2,1)S(1)}, u32[]{:S(2)}, u32[]{:S(2)}) collective-permute-start(bf16[256,896]{1,0:T(8,128)(2,1)S(1)} %bitcast.21), channel_id=1, source_target_pairs={{0,2},{2,0},{1,3},{3,1},{4,6},{6,4},{5,7},{7,5},{8,10},{10,8},{9,1... | collective-permute-start | bytes 1376264 | tf_op jit(solution)/shard_map/ppermute | solution.py:194
  62.6 17.8 %collective-permute-start.5 = (bf16[448,256]{1,0:T(8,128)(2,1)S(1)}, bf16[448,256]{1,0:T(8,128)(2,1)S(1)}, u32[]{:S(2)}, u32[]{:S(2)}) collective-permute-start(bf16[448,256]{1,0:T(8,128)(2,1)S(1)} %bitcast.28), channel_id=1, source_target_pairs={{0,2},{2,0},{1,3},{3,1},{4,6},{6,4},{5,7},{7,5},{8,10},{10,8},{9,1... | collective-permute-start | bytes 688136 | tf_op jit(solution)/shard_map/ppermute | solution.py:194
  65.9 19.3 %collective-permute-start.7 = (bf16[256,896]{1,0:T(8,128)(2,1)S(1)}, bf16[256,896]{1,0:T(8,128)(2,1)S(1)}, u32[]{:S(2)}, u32[]{:S(2)}) collective-permute-start(bf16[256,896]{1,0:T(8,128)(2,1)S(1)} %bitcast.22), channel_id=1, source_target_pairs={{0,1},{1,0},{2,3},{3,2},{4,5},{5,4},{6,7},{7,6},{8,9},{9,8},{10,11... | collective-permute-start | bytes 1376264 | tf_op jit(solution)/shard_map/ppermute | solution.py:194
  73.9 11.3 %collective-permute-start.9 = (bf16[256,896]{1,0:T(8,128)(2,1)S(1)}, bf16[256,896]{1,0:T(8,128)(2,1)S(1)}, u32[]{:S(2)}, u32[]{:S(2)}) collective-permute-start(bf16[256,896]{1,0:T(8,128)(2,1)S(1)} %collective-permute-done.8.refs_2_), channel_id=1, source_target_pairs={{0,1},{1,0},{2,3},{3,2},{4,5},{5,4},{6,7},{7,6},{8,9},{9,8},{10,11... | collective-permute-start | bytes 1376264 | tf_op jit(solution)/shard_map/ppermute | solution.py:194
  78.5 4.4 %collective-permute-start.4 = (bf16[448,256]{1,0:T(8,128)(2,1)S(1)}, bf16[448,256]{1,0:T(8,128)(2,1)S(1)}, u32[]{:S(2)}, u32[]{:S(2)}) collective-permute-start(bf16[448,256]{1,0:T(8,128)(2,1)S(1)} %bitcast.29), channel_id=1, source_target_pairs={{0,1},{1,0},{2,3},{3,2},{4,5},{5,4},{6,7},{7,6},{8,9},{9,8},{10,11... | collective-permute-start | bytes 688136 | tf_op jit(solution)/shard_map/ppermute | solution.py:194
  80.4 4.8 %copy-start.5 = (bf16[448,256]{1,0:T(8,128)(2,1)}, bf16[448,256]{1,0:T(8,128)(2,1)S(1)}, u32[]{:S(2)}) copy-start(bf16[448,256]{1,0:T(8,128)(2,1)S(1)} %collective-permute-done.5.refs_2_.refs_8_) | copy-start | bytes 688132
  80.4 3.5 %collective-permute-start.6 = (bf16[448,256]{1,0:T(8,128)(2,1)S(1)}, bf16[448,256]{1,0:T(8,128)(2,1)S(1)}, u32[]{:S(2)}, u32[]{:S(2)}) collective-permute-start(bf16[448,256]{1,0:T(8,128)(2,1)S(1)} %collective-permute-done.5.refs_2_.refs_8_), channel_id=1, source_target_pairs={{0,1},{1,0},{2,3},{3,2},{4,5},{5,4},{6,7},{7,6},{8,9},{9,8},{10,11... | collective-permute-start | bytes 688136 | tf_op jit(solution)/shard_map/ppermute | solution.py:194
  82.9 2.4 %copy-start.6 = (bf16[448,256]{1,0:T(8,128)(2,1)}, bf16[448,256]{1,0:T(8,128)(2,1)S(1)}, u32[]{:S(2)}) copy-start(bf16[448,256]{1,0:T(8,128)(2,1)S(1)} %collective-permute-done.4.refs_1_.refs_7_) | copy-start | bytes 688132
  83.9 1.3 copy-start.7
  89.9 21.4 %all-to-all-start.2 = ((bf16[8,32,1024]{2,1,0:T(8,128)(2,1)}), bf16[8,32,1024]{2,1,0:T(8,128)(2,1)S(1)}, u32[]{:S(2)}, u32[]{:S(2)}) async-start(bf16[8,32,1024]{2,1,0:T(8,128)(2,1)} %bitcast.10), calls=%async_computation.2 | async-start | bytes 1048576 | tf_op jit(solution)/shard_map/all_to_all | solution.py:183
  93.5 0.7 copy-start.10
  94.2 17.7 %copy-start.11 = (f32[32,2048]{1,0:T(8,128)S(1)}, f32[32,2048]{1,0:T(8,128)}, u32[]{:S(2)}) copy-start(f32[32,2048]{1,0:T(8,128)} %copy-done.10) | copy-start | bytes 786436
  94.2 17.7 %collective-permute-start.3 = (bf16[32,2048]{1,0:T(8,128)(2,1)S(1)}, bf16[32,2048]{1,0:T(8,128)(2,1)S(1)}, u32[]{:S(2)}, u32[]{:S(2)}) collective-permute-start(bf16[32,2048]{1,0:T(8,128)(2,1)S(1)} %get-tuple-element.37), channel_id=1, source_target_pairs={{0,64},{64,0},{1,65},{65,1},{2,66},{66,2},{3,67},{67,3},{4,68},{68... | collective-permute-start | bytes 393224 | tf_op jit(solution)/shard_map/ppermute | solution.py:194
  112.8 23.5 %all-to-all-start.4 = ((bf16[8,32,1024]{2,1,0:T(8,128)(2,1)}), bf16[8,32,1024]{2,1,0:T(8,128)(2,1)S(1)}, u32[]{:S(2)}, u32[]{:S(2)}) async-start(bf16[8,32,1024]{2,1,0:T(8,128)(2,1)} %shard_map.115), calls=%async_computation.4 | async-start | bytes 1048576 | tf_op jit(solution)/shard_map/all_to_all | solution.py:183
  119.4 13.7 %collective-permute-start.10 = (bf16[32,1024]{1,0:T(8,128)(2,1)S(1)}, bf16[32,1024]{1,0:T(8,128)(2,1)S(1)}, u32[]{:S(2)}, u32[]{:S(2)}) collective-permute-start(bf16[32,1024]{1,0:T(8,128)(2,1)S(1)} %get-tuple-element.43), channel_id=1, source_target_pairs={{0,64},{64,0},{1,65},{65,1},{2,66},{66,2},{3,67},{67,3},{4,68},{68... | collective-permute-start | bytes 196616 | tf_op jit(solution)/shard_map/ppermute | solution.py:194
  136.3 4.6 %copy-start.12 = (bf16[8,32,1024]{2,1,0:T(8,128)(2,1)}, bf16[8,32,1024]{2,1,0:T(8,128)(2,1)S(1)}, u32[]{:S(2)}) copy-start(bf16[8,32,1024]{2,1,0:T(8,128)(2,1)S(1)} %all-to-all-done.4) | copy-start | bytes 1572868
  136.3 31.7 %all-to-all-start.3 = ((bf16[8,32,2048]{2,1,0:T(8,128)(2,1)}), bf16[8,32,2048]{2,1,0:T(8,128)(2,1)}, u32[]{:S(2)}, u32[]{:S(2)}) async-start(bf16[8,32,2048]{2,1,0:T(8,128)(2,1)} %shard_map.116), calls=%async_computation.3 | async-start | bytes 2097152 | tf_op jit(solution)/shard_map/all_to_all | solution.py:183
  140.9 13.3 %collective-permute-start.13 = (bf16[256,256]{1,0:T(8,128)(2,1)S(1)}, bf16[256,256]{1,0:T(8,128)(2,1)S(1)}, u32[]{:S(2)}, u32[]{:S(2)}) collective-permute-start(bf16[256,256]{1,0:T(8,128)(2,1)S(1)} %get-tuple-element.67), channel_id=1, source_target_pairs={{0,3},{1,2},{2,1},{3,0},{4,7},{5,6},{6,5},{7,4},{8,11},{9,10},{10,... | collective-permute-start | bytes 393224 | tf_op jit(solution)/shard_map/ppermute | solution.py:203
  150.0 6.7 %collective-permute-start.12 = (bf16[256,256]{1,0:T(8,128)(2,1)S(1)}, bf16[256,256]{1,0:T(8,128)(2,1)S(1)}, u32[]{:S(2)}, u32[]{:S(2)}) collective-permute-start(bf16[256,256]{1,0:T(8,128)(2,1)S(1)} %get-tuple-element.68), channel_id=1, source_target_pairs={{0,2},{1,3},{2,0},{3,1},{4,6},{5,7},{6,4},{7,5},{8,10},{9,11},{10,... | collective-permute-start | bytes 393224 | tf_op jit(solution)/shard_map/ppermute | solution.py:203
  151.9 4.8 %collective-permute-start.11 = (bf16[256,256]{1,0:T(8,128)(2,1)S(1)}, bf16[256,256]{1,0:T(8,128)(2,1)S(1)}, u32[]{:S(2)}, u32[]{:S(2)}) collective-permute-start(bf16[256,256]{1,0:T(8,128)(2,1)S(1)} %get-tuple-element.69), channel_id=1, source_target_pairs={{0,1},{1,0},{2,3},{3,2},{4,5},{5,4},{6,7},{7,6},{8,9},{9,8},{10,11... | collective-permute-start | bytes 393224 | tf_op jit(solution)/shard_map/ppermute | solution.py:203
  172.1 48.8 %all-to-all-start.5 = ((bf16[16,16,896]{2,1,0:T(8,128)(2,1)}), bf16[16,16,896]{2,1,0:T(8,128)(2,1)S(1)}, u32[]{:S(2)}, u32[]{:S(2)}) async-start(bf16[16,16,896]{2,1,0:T(8,128)(2,1)} %bitcast.37), calls=%async_computation.5 | async-start | bytes 917504 | tf_op jit(solution)/shard_map/all_to_all | solution.py:183
  189.2 10.3 %collective-permute-start.14 = (bf16[256,512]{1,0:T(8,128)(2,1)S(1)}, bf16[256,512]{1,0:T(8,128)(2,1)S(1)}, u32[]{:S(2)}, u32[]{:S(2)}) collective-permute-start(bf16[256,512]{1,0:T(8,128)(2,1)S(1)} %pad_maximum_fusion.2), channel_id=1, source_target_pairs={{0,1},{1,0},{2,3},{3,2},{4,5},{5,4},{6,7},{7,6},{8,9},{9,8},{10,11... | collective-permute-start | bytes 786440 | tf_op jit(solution)/shard_map/ppermute | solution.py:203
  192.2 21.4 %collective-permute-start.15 = (bf16[256,512]{1,0:T(8,128)(2,1)S(1)}, bf16[256,512]{1,0:T(8,128)(2,1)S(1)}, u32[]{:S(2)}, u32[]{:S(2)}) collective-permute-start(bf16[256,512]{1,0:T(8,128)(2,1)S(1)} %pad_maximum_fusion.3), channel_id=1, source_target_pairs={{0,2},{1,3},{2,0},{3,1},{4,6},{5,7},{6,4},{7,5},{8,10},{9,11},{10,... | collective-permute-start | bytes 786440 | tf_op jit(solution)/shard_map/ppermute | solution.py:203
  194.2 25.0 %collective-permute-start.16 = (bf16[256,512]{1,0:T(8,128)(2,1)S(1)}, bf16[256,512]{1,0:T(8,128)(2,1)S(1)}, u32[]{:S(2)}, u32[]{:S(2)}) collective-permute-start(bf16[256,512]{1,0:T(8,128)(2,1)S(1)} %pad_maximum_fusion.4), channel_id=1, source_target_pairs={{0,3},{1,2},{2,1},{3,0},{4,7},{5,6},{6,5},{7,4},{8,11},{9,10},{10,... | collective-permute-start | bytes 786440 | tf_op jit(solution)/shard_map/ppermute | solution.py:203
  219.2 1.6 copy-start.9
  220.8 0.7 copy-start.8

commit v5 on v4

--- a/solution.py
+++ b/solution.py
@@ -27,7 +27,7 @@
     return lax.dot_general(a, b, dims, preferred_element_type=F32)
 
 
-def local(kernel, outs, *args, fetch=0):
+def local(kernel, outs, *args, fetch=0, scalars=0):
     size = sum(a.size * a.dtype.itemsize for a in args)
     size += sum(math.prod(shape) * jnp.dtype(kind).itemsize for shape, kind in outs)
     stay, total = len(args) - fetch, len(args)
@@ -48,7 +48,8 @@
     return pl.pallas_call(
         fetching if fetch else kernel,
         out_shape=[jax.ShapeDtypeStruct(shape, kind) for shape, kind in outs],
-        in_specs=[pl.BlockSpec(memory_space=pltpu.VMEM)] * stay
+        in_specs=[pl.BlockSpec(memory_space=pltpu.SMEM)] * scalars
+        + [pl.BlockSpec(memory_space=pltpu.VMEM)] * (stay - scalars)
         + [pl.BlockSpec(memory_space=pltpu.HBM)] * fetch,
         out_specs=[pl.BlockSpec(memory_space=pltpu.VMEM)] * len(outs),
         scratch_shapes=scratch + [pltpu.SemaphoreType.DMA((fetch,))] if fetch else (),
@@ -63,7 +64,7 @@
     return jnp.concatenate([ref[0:1], ref[1:2]], axis=1)
 
 
-def hits(ids_ref):
+def hits(ids_ref, owner):
     ids = pair(ids_ref)
     count = ids.shape[1]
     across = jnp.broadcast_to(ids, (count, count))
@@ -71,12 +72,16 @@
     second = lax.broadcasted_iota(jnp.int32, (count, count), 1)
     earlier = (across.T == across) & (first < second)
     rank = jnp.sum(jnp.where(earlier, 1.0, 0.0), axis=0, keepdims=True)
-    target = ids * CAP + rank.astype(jnp.int32)
-    return lax.broadcasted_iota(jnp.int32, (EXPERTS * CAP, count), 0) == target
+    slot = lax.broadcasted_iota(jnp.int32, (EXPERTS * CAP, count), 0)
+    return (owner(slot // CAP) == ids) & (slot % CAP == rank.astype(jnp.int32))
+
+
+def places(ids_ref, owner):
+    return jnp.where(hits(ids_ref, owner), 1.0, 0.0).astype(BF)
 
 
 def pack_kernel(ids_ref, weight_ref, tokens_ref, grad_ref, send_ref):
-    hit = hits(ids_ref)
+    hit = hits(ids_ref, lambda block: block)
     slot_weight = jnp.sum(jnp.where(hit, pair(weight_ref), 0.0), axis=1, keepdims=True)
     place = jnp.where(hit, 1.0, 0.0).astype(BF)
     tokens = tokens_ref[...]
@@ -132,19 +137,30 @@
     delta_ref[:, :, units:] = jnp.broadcast_to(up_delta.astype(BF)[None], shape)
 
 
-def back_kernel(hidden_ref, deltas_ref, *refs):
+def out_kernel(here_ref, hidden_ref, *refs):
     out_ref = refs[-1]
-    in_refs, down_refs = refs[:SLICES], refs[SLICES:-1]
-    hs = down_refs[0].shape[1]
+    hs = refs[0].shape[1]
+    rows = 0.0
+    for s in range(SLICES):
+        rows += dot(hidden_ref[:, s * hs : (s + 1) * hs], refs[s][...], LAST)
+    rows = rows.astype(BF)
+    for e in range(EXPERTS):
+        block = ((e // 4) ^ here_ref[0]) * 4 + ((e % 4) ^ here_ref[1])
+        to = pl.multiple_of(block * CAP, CAP)
+        out_ref[pl.ds(to, CAP), :] = rows[e * CAP : (e + 1) * CAP]
+
+
+def back_kernel(deltas_ref, *refs):
+    out_ref = refs[-1]
+    hs = refs[0].shape[1] // 2
     half = deltas_ref.shape[1] // 2
-    out_rows = in_rows = 0.0
+    in_rows = 0.0
     for s in range(SLICES):
         here = slice(s * hs, (s + 1) * hs)
         there = slice(half + s * hs, half + (s + 1) * hs)
-        out_rows += dot(hidden_ref[:, here], down_refs[s][...], LAST)
         both = jnp.concatenate([deltas_ref[:, here], deltas_ref[:, there]], axis=1)
-        in_rows += dot(both, in_refs[s][...], LAST)
-    out_ref[...] = jnp.concatenate([out_rows, in_rows], axis=1).astype(BF)
+        in_rows += dot(both, refs[s][...], LAST)
+    out_ref[...] = in_rows.astype(BF)
 
 
 def down_kernel(factor, *refs):
@@ -166,17 +182,25 @@
     grad_refs[1][...] = total[:, hs:] * factor
 
 
-def home_kernel(ids_ref, weight_ref, back_ref, mixed_ref, grad_ref):
-    tok_rows, width = mixed_ref.shape
-    place = jnp.where(hits(ids_ref), 1.0, 0.0).astype(BF)
+def mixed_kernel(here_ref, ids_ref, weight_ref, *refs):
+    back_refs, mixed_ref = refs[:-1], refs[-1]
+    tok_rows = mixed_ref.shape[0]
+
+    def owner(block):
+        return ((block % 4) ^ here_ref[0]) * 4 + ((block // 4) ^ here_ref[1])
+
     row = pair(weight_ref)
     count = row.shape[1]
     weight = jnp.broadcast_to(row, (count, count)).T[:, :1]
-    per = dot(place, back_ref[...], FIRST)
-    per_out = per[:, :width] * weight
-    per_in = per[:, width:]
-    mixed_ref[...] = per_out[:tok_rows] + per_out[tok_rows:]
-    grad_ref[...] = per_in[:tok_rows] + per_in[tok_rows:]
+    back = jnp.concatenate([ref[...] for ref in back_refs], axis=0)
+    per = dot(places(ids_ref, owner), back, FIRST) * weight
+    mixed_ref[...] = per[:tok_rows] + per[tok_rows:]
+
+
+def grad_kernel(ids_ref, back_ref, grad_ref):
+    tok_rows = grad_ref.shape[0]
+    per = dot(places(ids_ref, lambda block: block), back_ref[...], FIRST)
+    grad_ref[...] = per[:tok_rows] + per[tok_rows:]
 
 
 def swap(value, axis):
@@ -197,6 +221,10 @@
 def gather_y(copies):
     count, rows, cols = copies.shape
     return swap(copies, "y").reshape(count * rows, cols)
+
+
+def step_to(value, axis, step):
+    return lax.ppermute(value, axis, [(i, i ^ step) for i in range(4)])
 
 
 def to_slice(value, step):
@@ -248,12 +276,21 @@
         cut = [jnp.concatenate(part, axis=1) for part in cut]
         return cut[:1] + [to_slice(cut[step], step) for step in (1, 2, 3)]
 
+    here = jnp.stack([lax.axis_index("x"), lax.axis_index("zp")]).astype(jnp.int32)
+    (out_rows,) = local(
+        out_kernel, [((slots, width), BF)], here, hidden, *w_out, fetch=4, scalars=1
+    )
+    out_rows = out_rows.reshape(4, 4, CAP, width)
+    along = [out_rows[0]] + [step_to(out_rows[step], "x", step) for step in (1, 2, 3)]
+    along = [jnp.stack([part[step] for part in along]) for step in range(4)]
     hidden_own = of_slice(hidden, 1)
-    deltas, hidden, hidden_own = lax.optimization_barrier((deltas, hidden, hidden_own))
-    (back,) = local(
-        back_kernel, [((slots, 2 * width), BF)], hidden, deltas, *w_in, *w_out, fetch=10
-    )
-    back = swap(back.reshape(EXPERTS, CAP, 2 * width), OWN).reshape(slots, 2 * width)
+    home = along[:1] + [step_to(along[step], "zp", step) for step in (1, 2, 3)]
+    home = [part.reshape(4 * CAP, width) for part in home]
+    deltas, home, hidden_own = lax.optimization_barrier((deltas, home, hidden_own))
+
+    (back,) = local(back_kernel, [((slots, width), BF)], deltas, *w_in, fetch=5)
+    back, deltas = lax.optimization_barrier((back, deltas))
+    back = swap(back.reshape(EXPERTS, CAP, width), OWN).reshape(slots, width)
 
     factor = 1.0 / math.sqrt(8 * tok_rows)
 
@@ -266,7 +303,9 @@
     one = ((width, hs), F32)
     (down_grad,) = local(down, [one], *every, *hidden_own)
     gate_grad, up_grad = local(into, [one, one], *every, *of_slice(deltas, 2))
-    mixed, tokens_grad = local(home_kernel, [((tok_rows, width), F32)] * 2, ids, weight, back)
+    result = [((tok_rows, width), F32)]
+    (mixed,) = local(mixed_kernel, result, here, ids, weight, *home, scalars=1)
+    (tokens_grad,) = local(grad_kernel, result, ids, back)
     return (mixed, tokens_grad, gate_grad[None], up_grad[None], down_grad.T[None])
 
 

time: 224 us -> 232 us (1.036)
  the two profiles are of different devices: /device:TPU:129 before, /device:TPU:1 now
where the time goes in v5:
time: 232 us; the launch traced here: 230 us
  starting transfers between devices  164 us (71%)
  waiting for transfers between devices  38.5 us (17%)
  Pallas kernels  20.3 us (9%)
  local copies, waits for them, and re-layouts  4.69 us (2%)
    ppermute x11, starting transfers between devices, swap_pair(): return lax.ppermute(value, axis, [(0, 1), (1, 0)])  59.4 us
    all_to_all x6, starting transfers between devices, swap(): return lax.all_to_all(value, axis, split_axis=0, concat_axis=0, tiled=True)  46.1 us
    ppermute x6, starting transfers between devices, step_to(): return lax.ppermute(value, axis, [(i, i ^ step) for i in range(4)])  35.5 us
    ppermute x6, starting transfers between devices, to_slice(): return lax.ppermute(value, SLICE, [(i, i ^ step) for i in range(SLICES)])  23.2 us
    pallas_call x13, Pallas kernels, local(): pl.pallas_call(fetching if fetch else kernel, out_shape=[jax.ShapeDtypeSt...  20.3 us
    ppermute x11, waiting for transfers between devices, swap_pair(): return lax.ppermute(value, axis, [(0, 1), (1, 0)])  15.9 us
    ppermute x6, waiting for transfers between devices, step_to(): return lax.ppermute(value, axis, [(i, i ^ step) for i in range(4)])  7.81 us
    ppermute x6, waiting for transfers between devices, to_slice(): return lax.ppermute(value, SLICE, [(i, i ^ step) for i in range(SLICES)])  7.57 us
  transfers between devices with their start and end apart: 29, of which 12 were waited for; matrix products, arithmetic and copies ran while one was open for 2% of the time, Pallas kernels for 5%

profile of v5, /device:TPU:1, one launch (start us, length us, event | category | flops | bytes accessed | tf_op | source)
XLA Modules:
  0.0 229.8 jit_solution(7388454896581319698)
XLA Ops:
  0.6 2.2 shard_map.110
  2.9 0.0 copy-start.16
  2.9 17.2 %all-to-all-start = ((bf16[16,16,896]{2,1,0:T(8,128)(2,1)}), bf16[16,16,896]{2,1,0:T(8,128)(2,1)S(1)}, u32[]{:S(2)}, u32[]{:S(2)}) async-start(bf16[16,16,896]{2,1,0:T(8,128)(2,1)} %bitcast.59), calls=%async_computation | async-start | bytes 917504 | tf_op jit(solution)/shard_map/all_to_all | solution.py:207
  20.1 0.0 copy-start
  20.1 4.0 %collective-permute-start.1 = (bf16[448,512]{1,0:T(8,128)(2,1)S(1)}, bf16[448,512]{1,0:T(8,128)(2,1)S(1)}, u32[]{:S(2)}, u32[]{:S(2)}) collective-permute-start(bf16[448,512]{1,0:T(8,128)(2,1)S(1)} %pad_maximum_fusion.refs_0_.refs_1_), channel_id=1, source_target_pairs={{0,2},{2,0},{1,3},{3,1},{4,6},{6,4},{5,7},{7,5},{8,10},{10,8},{9,1... | collective-permute-start | bytes 1376264 | tf_op jit(solution)/shard_map/ppermute | solution.py:218
  24.1 3.1 %collective-permute-start = (bf16[448,512]{1,0:T(8,128)(2,1)S(1)}, bf16[448,512]{1,0:T(8,128)(2,1)S(1)}, u32[]{:S(2)}, u32[]{:S(2)}) collective-permute-start(bf16[448,512]{1,0:T(8,128)(2,1)S(1)} %pad_maximum_fusion.refs_0_.refs_1_), channel_id=1, source_target_pairs={{0,1},{1,0},{2,3},{3,2},{4,5},{5,4},{6,7},{7,6},{8,9},{9,8},{10,11... | collective-permute-start | bytes 1376264 | tf_op jit(solution)/shard_map/ppermute | solution.py:218
  27.3 10.0 %collective-permute-done.1.refs_2_.refs_3_ = bf16[448,512]{1,0:T(8,128)(2,1)S(1)} collective-permute-done((bf16[448,512]{1,0:T(8,128)(2,1)S(1)}, bf16[448,512]{1,0:T(8,128)(2,1)S(1)}, u32[]{:S(2)}, u32[]{:S(2)}) %collective-permute-start.1) | collective-permute-done | bytes 458784 | tf_op jit(solution)/shard_map/ppermute | solution.py:218
  37.3 3.3 %collective-permute-start.2 = (bf16[448,512]{1,0:T(8,128)(2,1)S(1)}, bf16[448,512]{1,0:T(8,128)(2,1)S(1)}, u32[]{:S(2)}, u32[]{:S(2)}) collective-permute-start(bf16[448,512]{1,0:T(8,128)(2,1)S(1)} %collective-permute-done.1.refs_2_.refs_3_), channel_id=1, source_target_pairs={{0,1},{1,0},{2,3},{3,2},{4,5},{5,4},{6,7},{7,6},{8,9},{9,8},{10,11... | collective-permute-start | bytes 1376264 | tf_op jit(solution)/shard_map/ppermute | solution.py:218
  40.5 0.0 copy-start.2
  40.5 1.4 collective-permute-done.2.refs_3_.refs_4_
  42.0 1.5 all-to-all-done
  43.5 1.7 shard_map.111
  45.3 7.0 %all-to-all-start.1 = ((bf16[8,32,2048]{2,1,0:T(8,128)(2,1)}), bf16[8,32,2048]{2,1,0:T(8,128)(2,1)S(1)}, u32[]{:S(2)}, u32[]{:S(2)}) async-start(bf16[8,32,2048]{2,1,0:T(8,128)(2,1)} %bitcast.8), calls=%async_computation.1 | async-start | bytes 2097152 | tf_op jit(solution)/shard_map/all_to_all | solution.py:207
  52.2 6.5 %collective-permute-start.8 = (bf16[256,896]{1,0:T(8,128)(2,1)S(1)}, bf16[256,896]{1,0:T(8,128)(2,1)S(1)}, u32[]{:S(2)}, u32[]{:S(2)}) collective-permute-start(bf16[256,896]{1,0:T(8,128)(2,1)S(1)} %bitcast.38), channel_id=1, source_target_pairs={{0,2},{2,0},{1,3},{3,1},{4,6},{6,4},{5,7},{7,5},{8,10},{10,8},{9,1... | collective-permute-start | bytes 1376264 | tf_op jit(solution)/shard_map/ppermute | solution.py:218
  58.8 1.9 collective-permute-start.5
  60.7 5.2 %collective-permute-start.7 = (bf16[256,896]{1,0:T(8,128)(2,1)S(1)}, bf16[256,896]{1,0:T(8,128)(2,1)S(1)}, u32[]{:S(2)}, u32[]{:S(2)}) collective-permute-start(bf16[256,896]{1,0:T(8,128)(2,1)S(1)} %bitcast.39), channel_id=1, source_target_pairs={{0,1},{1,0},{2,3},{3,2},{4,5},{5,4},{6,7},{7,6},{8,9},{9,8},{10,11... | collective-permute-start | bytes 1376264 | tf_op jit(solution)/shard_map/ppermute | solution.py:218
  65.9 1.7 collective-permute-done.8.refs_2_
  67.6 7.0 %collective-permute-start.9 = (bf16[256,896]{1,0:T(8,128)(2,1)S(1)}, bf16[256,896]{1,0:T(8,128)(2,1)S(1)}, u32[]{:S(2)}, u32[]{:S(2)}) collective-permute-start(bf16[256,896]{1,0:T(8,128)(2,1)S(1)} %collective-permute-done.8.refs_2_), channel_id=1, source_target_pairs={{0,1},{1,0},{2,3},{3,2},{4,5},{5,4},{6,7},{7,6},{8,9},{9,8},{10,11... | collective-permute-start | bytes 1376264 | tf_op jit(solution)/shard_map/ppermute | solution.py:218
  74.6 1.9 collective-permute-start.4
  76.5 2.4 %collective-permute-start.6 = (bf16[448,256]{1,0:T(8,128)(2,1)S(1)}, bf16[448,256]{1,0:T(8,128)(2,1)S(1)}, u32[]{:S(2)}, u32[]{:S(2)}) collective-permute-start(bf16[448,256]{1,0:T(8,128)(2,1)S(1)} %collective-permute-done.5.refs_2_.refs_4_), channel_id=1, source_target_pairs={{0,1},{1,0},{2,3},{3,2},{4,5},{5,4},{6,7},{7,6},{8,9},{9,8},{10,11... | collective-permute-start | bytes 688136 | tf_op jit(solution)/shard_map/ppermute | solution.py:218
  79.0 1.1 collective-permute-done.6.refs_3_.refs_5_
  80.1 1.3 shard_map.113
  81.4 6.7 %all-to-all-start.2 = ((bf16[8,32,1024]{2,1,0:T(8,128)(2,1)}), bf16[8,32,1024]{2,1,0:T(8,128)(2,1)S(1)}, u32[]{:S(2)}, u32[]{:S(2)}) async-start(bf16[8,32,1024]{2,1,0:T(8,128)(2,1)} %bitcast.12), calls=%async_computation.2 | async-start | bytes 1048576 | tf_op jit(solution)/shard_map/all_to_all | solution.py:207
  88.0 0.1 shard_map.112
  88.2 0.0 copy-start.11
  88.2 0.7 copy-done.11
  88.9 12.5 %collective-permute-start.3 = (bf16[32,2048]{1,0:T(8,128)(2,1)S(1)}, bf16[32,2048]{1,0:T(8,128)(2,1)S(1)}, u32[]{:S(2)}, u32[]{:S(2)}) collective-permute-start(bf16[32,2048]{1,0:T(8,128)(2,1)S(1)} %get-tuple-element.40), channel_id=1, source_target_pairs={{0,64},{64,0},{1,65},{65,1},{2,66},{66,2},{3,67},{67,3},{4,68},{68... | collective-permute-start | bytes 393224 | tf_op jit(solution)/shard_map/ppermute | solution.py:218
  101.4 4.6 %all-to-all-done.2.got_ref = bf16[8,32,1024]{2,1,0:T(8,128)(2,1)S(1)} async-done(((bf16[8,32,1024]{2,1,0:T(8,128)(2,1)}), bf16[8,32,1024]{2,1,0:T(8,128)(2,1)S(1)}, u32[]{:S(2)}, u32[]{:S(2)}) %all-to-all-start.2) | async-done | bytes 524320 | tf_op jit(solution)/shard_map/all_to_all | solution.py:207
  106.0 0.1 shard_map.114
  106.1 0.9 shard_map.115
  106.9 4.9 %all-to-all-start.4 = ((bf16[8,32,1024]{2,1,0:T(8,128)(2,1)}), bf16[8,32,1024]{2,1,0:T(8,128)(2,1)S(1)}, u32[]{:S(2)}, u32[]{:S(2)}) async-start(bf16[8,32,1024]{2,1,0:T(8,128)(2,1)} %shard_map.115), calls=%async_computation.4 | async-start | bytes 1048576 | tf_op jit(solution)/shard_map/all_to_all | solution.py:207
  111.8 11.6 %collective-permute-start.10 = (bf16[32,1024]{1,0:T(8,128)(2,1)S(1)}, bf16[32,1024]{1,0:T(8,128)(2,1)S(1)}, u32[]{:S(2)}, u32[]{:S(2)}) collective-permute-start(bf16[32,1024]{1,0:T(8,128)(2,1)S(1)} %get-tuple-element.46), channel_id=1, source_target_pairs={{0,64},{64,0},{1,65},{65,1},{2,66},{66,2},{3,67},{67,3},{4,68},{68... | collective-permute-start | bytes 196616 | tf_op jit(solution)/shard_map/ppermute | solution.py:218
  123.4 0.6 pad_add_fusion.refs_0_.here_ref
  124.0 1.7 collective-permute-done.10.act_other_ref
  125.8 1.1 shard_map.116
  126.9 1.1 all-to-all-done.4
  128.0 0.8 copy-done.13
  128.8 5.5 %all-to-all-start.3 = ((bf16[8,32,2048]{2,1,0:T(8,128)(2,1)}), bf16[8,32,2048]{2,1,0:T(8,128)(2,1)}, u32[]{:S(2)}, u32[]{:S(2)}) async-start(bf16[8,32,2048]{2,1,0:T(8,128)(2,1)} %shard_map.116), calls=%async_computation.3 | async-start | bytes 2097152 | tf_op jit(solution)/shard_map/all_to_all | solution.py:207
  134.2 3.6 %shard_map.117 = bf16[256,448]{1,0:T(8,128)(2,1)} custom-call(s32[2]{0:T(128)} %pad_add_fusion.refs_0_.here_ref, bf16[256,1024]{1,0:T(8,128)(2,1)} %bitcast.57, bf16[448,256]{1,0:T(8,128)(2,1)} %bitcast.45, bf16[448,256]{1,0:T(8,128)(2,1)} %copy-done.6, bf16[448,256]{1,0:T(8,128)(2,1)} %copy-done.5, bf16[448,256]{1,0:T(8,128)(2,1)} %copy-done.7), custom_call_target="tpu_custom_call" | custom-call | flops 2000000000 | bytes 3342352 | tf_op jit(solution)/shard_map/pallas_call | solution.py:48
  137.8 0.9 fusion.2
  138.8 4.3 %collective-permute-start.13 = (bf16[4,16,448]{2,1,0:T(8,128)(2,1)S(1)}, bf16[4,16,448]{2,1,0:T(8,128)(2,1)S(1)}, u32[]{:S(2)}, u32[]{:S(2)}) collective-permute-start(bf16[4,16,448]{2,1,0:T(8,128)(2,1)S(1)} %bitcast.65), channel_id=1, source_target_pairs={{0,48},{16,32},{32,16},{48,0},{1,49},{17,33},{33,17},{49,1},{2,50}... | collective-permute-start | bytes 172040 | tf_op jit(solution)/shard_map/ppermute | solution.py:227
  143.1 0.8 slice_bitcast_fusion
  143.9 1.9 collective-permute-start.11
  145.8 3.4 %collective-permute-start.12 = (bf16[4,16,448]{2,1,0:T(8,128)(2,1)S(1)}, bf16[4,16,448]{2,1,0:T(8,128)(2,1)S(1)}, u32[]{:S(2)}, u32[]{:S(2)}) collective-permute-start(bf16[4,16,448]{2,1,0:T(8,128)(2,1)S(1)} %bitcast.63), channel_id=1, source_target_pairs={{0,32},{16,48},{32,0},{48,16},{1,33},{17,49},{33,1},{49,17},{2,34}... | collective-permute-start | bytes 172040 | tf_op jit(solution)/shard_map/ppermute | solution.py:227
  149.2 7.1 %collective-permute-start.19 = (bf16[256,256]{1,0:T(8,128)(2,1)S(1)}, bf16[256,256]{1,0:T(8,128)(2,1)S(1)}, u32[]{:S(2)}, u32[]{:S(2)}) collective-permute-start(bf16[256,256]{1,0:T(8,128)(2,1)S(1)} %get-tuple-element.73), channel_id=1, source_target_pairs={{0,3},{1,2},{2,1},{3,0},{4,7},{5,6},{6,5},{7,4},{8,11},{9,10},{10,... | collective-permute-start | bytes 393224 | tf_op jit(solution)/shard_map/ppermute | solution.py:231
  156.3 3.6 %collective-permute-start.18 = (bf16[256,256]{1,0:T(8,128)(2,1)S(1)}, bf16[256,256]{1,0:T(8,128)(2,1)S(1)}, u32[]{:S(2)}, u32[]{:S(2)}) collective-permute-start(bf16[256,256]{1,0:T(8,128)(2,1)S(1)} %get-tuple-element.74), channel_id=1, source_target_pairs={{0,2},{1,3},{2,0},{3,1},{4,6},{5,7},{6,4},{7,5},{8,10},{9,11},{10,... | collective-permute-start | bytes 393224 | tf_op jit(solution)/shard_map/ppermute | solution.py:231
  159.9 1.9 collective-permute-start.17
  161.9 15.6 %collective-permute-start.14 = (bf16[4,16,448]{2,1,0:T(8,128)(2,1)S(1)}, bf16[4,16,448]{2,1,0:T(8,128)(2,1)S(1)}, u32[]{:S(2)}, u32[]{:S(2)}) collective-permute-start(bf16[4,16,448]{2,1,0:T(8,128)(2,1)S(1)} %pad_maximum_fusion.6), channel_id=1, source_target_pairs={{0,4},{4,0},{8,12},{12,8},{1,5},{5,1},{9,13},{13,9},{2,6},{6,2},{1... | collective-permute-start | bytes 172040 | tf_op jit(solution)/shard_map/ppermute | solution.py:227
  177.6 5.2 %collective-permute-start.15 = (bf16[4,16,448]{2,1,0:T(8,128)(2,1)S(1)}, bf16[4,16,448]{2,1,0:T(8,128)(2,1)S(1)}, u32[]{:S(2)}, u32[]{:S(2)}) collective-permute-start(bf16[4,16,448]{2,1,0:T(8,128)(2,1)S(1)} %pad_maximum_fusion.7), channel_id=1, source_target_pairs={{0,8},{4,12},{8,0},{12,4},{1,9},{5,13},{9,1},{13,5},{2,10},{6,14},... | collective-permute-start | bytes 172040 | tf_op jit(solution)/shard_map/ppermute | solution.py:227
  182.9 5.1 %collective-permute-start.16 = (bf16[4,16,448]{2,1,0:T(8,128)(2,1)S(1)}, bf16[4,16,448]{2,1,0:T(8,128)(2,1)S(1)}, u32[]{:S(2)}, u32[]{:S(2)}) collective-permute-start(bf16[4,16,448]{2,1,0:T(8,128)(2,1)S(1)} %pad_maximum_fusion.8), channel_id=1, source_target_pairs={{0,12},{4,8},{8,4},{12,0},{1,13},{5,9},{9,5},{13,1},{2,14},{6,10},... | collective-permute-start | bytes 172040 | tf_op jit(solution)/shard_map/ppermute | solution.py:227
  188.0 0.5 collective-permute-done.15
  188.5 7.3 %collective-permute-done.16 = bf16[4,16,448]{2,1,0:T(8,128)(2,1)S(1)} collective-permute-done((bf16[4,16,448]{2,1,0:T(8,128)(2,1)S(1)}, bf16[4,16,448]{2,1,0:T(8,128)(2,1)S(1)}, u32[]{:S(2)}, u32[]{:S(2)}) %collective-permute-start.16) | collective-permute-done | bytes 57376 | tf_op jit(solution)/shard_map/ppermute | solution.py:227
  195.8 3.2 %shard_map.119 = bf16[256,448]{1,0:T(8,128)(2,1)} custom-call(bf16[256,2048]{1,0:T(8,128)(2,1)} %bitcast.13.refs_0_, bf16[448,512]{1,0:T(8,128)(2,1)} %copy-done, bf16[448,512]{1,0:T(8,128)(2,1)} %copy-done.2, bf16[448,512]{1,0:T(8,128)(2,1)} %copy-done.1, bf16[448,512]{1,0:T(8,128)(2,1)} %copy-done.3), custom_call_target="tpu_custom_call" | custom-call | flops 2000000000 | bytes 6225920 | tf_op jit(solution)/shard_map/pallas_call | solution.py:48
  199.0 4.9 %all-to-all-start.5 = ((bf16[16,16,448]{2,1,0:T(8,128)(2,1)}), bf16[16,16,448]{2,1,0:T(8,128)(2,1)S(1)}, u32[]{:S(2)}, u32[]{:S(2)}) async-start(bf16[16,16,448]{2,1,0:T(8,128)(2,1)} %bitcast.60), calls=%async_computation.5 | async-start | bytes 524288 | tf_op jit(solution)/shard_map/all_to_all | solution.py:207
  204.0 1.4 fusion
  205.4 3.5 %collective-permute-start.20 = (bf16[256,512]{1,0:T(8,128)(2,1)S(1)}, bf16[256,512]{1,0:T(8,128)(2,1)S(1)}, u32[]{:S(2)}, u32[]{:S(2)}) collective-permute-start(bf16[256,512]{1,0:T(8,128)(2,1)S(1)} %pad_maximum_fusion.2), channel_id=1, source_target_pairs={{0,1},{1,0},{2,3},{3,2},{4,5},{5,4},{6,7},{7,6},{8,9},{9,8},{10,11... | collective-permute-start | bytes 786440 | tf_op jit(solution)/shard_map/ppermute | solution.py:231
  208.9 5.2 %collective-permute-start.21 = (bf16[256,512]{1,0:T(8,128)(2,1)S(1)}, bf16[256,512]{1,0:T(8,128)(2,1)S(1)}, u32[]{:S(2)}, u32[]{:S(2)}) collective-permute-start(bf16[256,512]{1,0:T(8,128)(2,1)S(1)} %pad_maximum_fusion.3), channel_id=1, source_target_pairs={{0,2},{1,3},{2,0},{3,1},{4,6},{5,7},{6,4},{7,5},{8,10},{9,11},{10,... | collective-permute-start | bytes 786440 | tf_op jit(solution)/shard_map/ppermute | solution.py:231
  214.2 1.9 collective-permute-start.22
  216.1 1.7 shard_map.118
  217.8 1.8 shard_map.122
  219.6 1.9 collective-permute-done.21.refs_6_
  221.5 5.6 %collective-permute-done.22.refs_7_ = bf16[256,512]{1,0:T(8,128)(2,1)S(1)} collective-permute-done((bf16[256,512]{1,0:T(8,128)(2,1)S(1)}, bf16[256,512]{1,0:T(8,128)(2,1)S(1)}, u32[]{:S(2)}, u32[]{:S(2)}) %collective-permute-start.22) | collective-permute-done | bytes 262176 | tf_op jit(solution)/shard_map/ppermute | solution.py:231
  227.1 1.6 shard_map.121
  228.7 1.1 shard_map.120
  (58 shorter events, 0.3 us)
Async XLA Ops:
  2.9 17.2 %copy-start.15 = (bf16[1,448,256]{2,1,0:T(8,128)(2,1)S(1)}, bf16[1,448,256]{2,1,0:T(8,128)(2,1)}, u32[]{:S(2)}) copy-start(bf16[1,448,256]{2,1,0:T(8,128)(2,1)} %param.12) | copy-start | bytes 688132
  2.9 17.2 %copy-start.16 = (bf16[1,448,256]{2,1,0:T(8,128)(2,1)S(1)}, bf16[1,448,256]{2,1,0:T(8,128)(2,1)}, u32[]{:S(2)}) copy-start(bf16[1,448,256]{2,1,0:T(8,128)(2,1)} %param.11) | copy-start | bytes 688132
  2.9 40.6 %all-to-all-start = ((bf16[16,16,896]{2,1,0:T(8,128)(2,1)}), bf16[16,16,896]{2,1,0:T(8,128)(2,1)S(1)}, u32[]{:S(2)}, u32[]{:S(2)}) async-start(bf16[16,16,896]{2,1,0:T(8,128)(2,1)} %bitcast.59), calls=%async_computation | async-start | bytes 917504 | tf_op jit(solution)/shard_map/all_to_all | solution.py:207
  20.1 25.1 %copy-start = (bf16[448,512]{1,0:T(8,128)(2,1)}, bf16[448,512]{1,0:T(8,128)(2,1)S(1)}, u32[]{:S(2)}) copy-start(bf16[448,512]{1,0:T(8,128)(2,1)S(1)} %pad_maximum_fusion.refs_0_.refs_1_) | copy-start | bytes 1376260
  20.1 17.1 %collective-permute-start.1 = (bf16[448,512]{1,0:T(8,128)(2,1)S(1)}, bf16[448,512]{1,0:T(8,128)(2,1)S(1)}, u32[]{:S(2)}, u32[]{:S(2)}) collective-permute-start(bf16[448,512]{1,0:T(8,128)(2,1)S(1)} %pad_maximum_fusion.refs_0_.refs_1_), channel_id=1, source_target_pairs={{0,2},{2,0},{1,3},{3,1},{4,6},{6,4},{5,7},{7,5},{8,10},{10,8},{9,1... | collective-permute-start | bytes 1376264 | tf_op jit(solution)/shard_map/ppermute | solution.py:218
  24.1 16.4 %collective-permute-start = (bf16[448,512]{1,0:T(8,128)(2,1)S(1)}, bf16[448,512]{1,0:T(8,128)(2,1)S(1)}, u32[]{:S(2)}, u32[]{:S(2)}) collective-permute-start(bf16[448,512]{1,0:T(8,128)(2,1)S(1)} %pad_maximum_fusion.refs_0_.refs_1_), channel_id=1, source_target_pairs={{0,1},{1,0},{2,3},{3,2},{4,5},{5,4},{6,7},{7,6},{8,9},{9,8},{10,11... | collective-permute-start | bytes 1376264 | tf_op jit(solution)/shard_map/ppermute | solution.py:218
  37.3 8.0 %copy-start.1 = (bf16[448,512]{1,0:T(8,128)(2,1)}, bf16[448,512]{1,0:T(8,128)(2,1)S(1)}, u32[]{:S(2)}) copy-start(bf16[448,512]{1,0:T(8,128)(2,1)S(1)} %collective-permute-done.1.refs_2_.refs_3_) | copy-start | bytes 1376260
  37.3 4.7 %collective-permute-start.2 = (bf16[448,512]{1,0:T(8,128)(2,1)S(1)}, bf16[448,512]{1,0:T(8,128)(2,1)S(1)}, u32[]{:S(2)}, u32[]{:S(2)}) collective-permute-start(bf16[448,512]{1,0:T(8,128)(2,1)S(1)} %collective-permute-done.1.refs_2_.refs_3_), channel_id=1, source_target_pairs={{0,1},{1,0},{2,3},{3,2},{4,5},{5,4},{6,7},{7,6},{8,9},{9,8},{10,11... | collective-permute-start | bytes 1376264 | tf_op jit(solution)/shard_map/ppermute | solution.py:218
  40.5 4.7 %copy-start.2 = (bf16[448,512]{1,0:T(8,128)(2,1)}, bf16[448,512]{1,0:T(8,128)(2,1)S(1)}, u32[]{:S(2)}) copy-start(bf16[448,512]{1,0:T(8,128)(2,1)S(1)} %collective-permute-done.refs_1_.refs_2_) | copy-start | bytes 1376260
  41.9 3.3 %copy-start.3 = (bf16[448,512]{1,0:T(8,128)(2,1)}, bf16[448,512]{1,0:T(8,128)(2,1)S(1)}, u32[]{:S(2)}) copy-start(bf16[448,512]{1,0:T(8,128)(2,1)S(1)} %collective-permute-done.2.refs_3_.refs_4_) | copy-start | bytes 1376260
  45.2 13.5 %copy-start.4 = (bf16[1,256,448]{1,2,0:T(8,128)(2,1)S(1)}, bf16[1,256,448]{1,2,0:T(8,128)(2,1)}, u32[]{:S(2)}) copy-start(bf16[1,256,448]{1,2,0:T(8,128)(2,1)} %param.13) | copy-start | bytes 688132
  45.3 36.1 %all-to-all-start.1 = ((bf16[8,32,2048]{2,1,0:T(8,128)(2,1)}), bf16[8,32,2048]{2,1,0:T(8,128)(2,1)S(1)}, u32[]{:S(2)}, u32[]{:S(2)}) async-start(bf16[8,32,2048]{2,1,0:T(8,128)(2,1)} %bitcast.8), calls=%async_computation.1 | async-start | bytes 2097152 | tf_op jit(solution)/shard_map/all_to_all | solution.py:207
  52.2 15.4 %collective-permute-start.8 = (bf16[256,896]{1,0:T(8,128)(2,1)S(1)}, bf16[256,896]{1,0:T(8,128)(2,1)S(1)}, u32[]{:S(2)}, u32[]{:S(2)}) collective-permute-start(bf16[256,896]{1,0:T(8,128)(2,1)S(1)} %bitcast.38), channel_id=1, source_target_pairs={{0,2},{2,0},{1,3},{3,1},{4,6},{6,4},{5,7},{7,5},{8,10},{10,8},{9,1... | collective-permute-start | bytes 1376264 | tf_op jit(solution)/shard_map/ppermute | solution.py:218
  58.8 17.7 %collective-permute-start.5 = (bf16[448,256]{1,0:T(8,128)(2,1)S(1)}, bf16[448,256]{1,0:T(8,128)(2,1)S(1)}, u32[]{:S(2)}, u32[]{:S(2)}) collective-permute-start(bf16[448,256]{1,0:T(8,128)(2,1)S(1)} %bitcast.46), channel_id=1, source_target_pairs={{0,2},{2,0},{1,3},{3,1},{4,6},{6,4},{5,7},{7,5},{8,10},{10,8},{9,1... | collective-permute-start | bytes 688136 | tf_op jit(solution)/shard_map/ppermute | solution.py:218
  60.7 20.6 %collective-permute-start.7 = (bf16[256,896]{1,0:T(8,128)(2,1)S(1)}, bf16[256,896]{1,0:T(8,128)(2,1)S(1)}, u32[]{:S(2)}, u32[]{:S(2)}) collective-permute-start(bf16[256,896]{1,0:T(8,128)(2,1)S(1)} %bitcast.39), channel_id=1, source_target_pairs={{0,1},{1,0},{2,3},{3,2},{4,5},{5,4},{6,7},{7,6},{8,9},{9,8},{10,11... | collective-permute-start | bytes 1376264 | tf_op jit(solution)/shard_map/ppermute | solution.py:218
  67.6 13.7 %collective-permute-start.9 = (bf16[256,896]{1,0:T(8,128)(2,1)S(1)}, bf16[256,896]{1,0:T(8,128)(2,1)S(1)}, u32[]{:S(2)}, u32[]{:S(2)}) collective-permute-start(bf16[256,896]{1,0:T(8,128)(2,1)S(1)} %collective-permute-done.8.refs_2_), channel_id=1, source_target_pairs={{0,1},{1,0},{2,3},{3,2},{4,5},{5,4},{6,7},{7,6},{8,9},{9,8},{10,11... | collective-permute-start | bytes 1376264 | tf_op jit(solution)/shard_map/ppermute | solution.py:218
  74.6 4.4 %collective-permute-start.4 = (bf16[448,256]{1,0:T(8,128)(2,1)S(1)}, bf16[448,256]{1,0:T(8,128)(2,1)S(1)}, u32[]{:S(2)}, u32[]{:S(2)}) collective-permute-start(bf16[448,256]{1,0:T(8,128)(2,1)S(1)} %bitcast.47), channel_id=1, source_target_pairs={{0,1},{1,0},{2,3},{3,2},{4,5},{5,4},{6,7},{7,6},{8,9},{9,8},{10,11... | collective-permute-start | bytes 688136 | tf_op jit(solution)/shard_map/ppermute | solution.py:218
  76.5 4.8 %copy-start.5 = (bf16[448,256]{1,0:T(8,128)(2,1)}, bf16[448,256]{1,0:T(8,128)(2,1)S(1)}, u32[]{:S(2)}) copy-start(bf16[448,256]{1,0:T(8,128)(2,1)S(1)} %collective-permute-done.5.refs_2_.refs_4_) | copy-start | bytes 688132
  76.5 3.5 %collective-permute-start.6 = (bf16[448,256]{1,0:T(8,128)(2,1)S(1)}, bf16[448,256]{1,0:T(8,128)(2,1)S(1)}, u32[]{:S(2)}, u32[]{:S(2)}) collective-permute-start(bf16[448,256]{1,0:T(8,128)(2,1)S(1)} %collective-permute-done.5.refs_2_.refs_4_), channel_id=1, source_target_pairs={{0,1},{1,0},{2,3},{3,2},{4,5},{5,4},{6,7},{7,6},{8,9},{9,8},{10,11... | collective-permute-start | bytes 688136 | tf_op jit(solution)/shard_map/ppermute | solution.py:218
  79.0 2.4 %copy-start.6 = (bf16[448,256]{1,0:T(8,128)(2,1)}, bf16[448,256]{1,0:T(8,128)(2,1)S(1)}, u32[]{:S(2)}) copy-start(bf16[448,256]{1,0:T(8,128)(2,1)S(1)} %collective-permute-done.4.refs_1_.refs_3_) | copy-start | bytes 688132
  80.0 1.3 copy-start.7
  81.4 24.6 %all-to-all-start.2 = ((bf16[8,32,1024]{2,1,0:T(8,128)(2,1)}), bf16[8,32,1024]{2,1,0:T(8,128)(2,1)S(1)}, u32[]{:S(2)}, u32[]{:S(2)}) async-start(bf16[8,32,1024]{2,1,0:T(8,128)(2,1)} %bitcast.12), calls=%async_computation.2 | async-start | bytes 1048576 | tf_op jit(solution)/shard_map/all_to_all | solution.py:207
  88.2 0.7 copy-start.11
  88.9 17.2 %copy-start.12 = (f32[32,2048]{1,0:T(8,128)S(1)}, f32[32,2048]{1,0:T(8,128)}, u32[]{:S(2)}) copy-start(f32[32,2048]{1,0:T(8,128)} %copy-done.11) | copy-start | bytes 786436
  88.9 17.2 %collective-permute-start.3 = (bf16[32,2048]{1,0:T(8,128)(2,1)S(1)}, bf16[32,2048]{1,0:T(8,128)(2,1)S(1)}, u32[]{:S(2)}, u32[]{:S(2)}) collective-permute-start(bf16[32,2048]{1,0:T(8,128)(2,1)S(1)} %get-tuple-element.40), channel_id=1, source_target_pairs={{0,64},{64,0},{1,65},{65,1},{2,66},{66,2},{3,67},{67,3},{4,68},{68... | collective-permute-start | bytes 393224 | tf_op jit(solution)/shard_map/ppermute | solution.py:218
  106.9 21.0 %all-to-all-start.4 = ((bf16[8,32,1024]{2,1,0:T(8,128)(2,1)}), bf16[8,32,1024]{2,1,0:T(8,128)(2,1)S(1)}, u32[]{:S(2)}, u32[]{:S(2)}) async-start(bf16[8,32,1024]{2,1,0:T(8,128)(2,1)} %shard_map.115), calls=%async_computation.4 | async-start | bytes 1048576 | tf_op jit(solution)/shard_map/all_to_all | solution.py:207
  111.8 13.9 %collective-permute-start.10 = (bf16[32,1024]{1,0:T(8,128)(2,1)S(1)}, bf16[32,1024]{1,0:T(8,128)(2,1)S(1)}, u32[]{:S(2)}, u32[]{:S(2)}) collective-permute-start(bf16[32,1024]{1,0:T(8,128)(2,1)S(1)} %get-tuple-element.46), channel_id=1, source_target_pairs={{0,64},{64,0},{1,65},{65,1},{2,66},{66,2},{3,67},{67,3},{4,68},{68... | collective-permute-start | bytes 196616 | tf_op jit(solution)/shard_map/ppermute | solution.py:218
  128.0 0.8 copy-start.13
  128.8 67.0 %all-to-all-start.3 = ((bf16[8,32,2048]{2,1,0:T(8,128)(2,1)}), bf16[8,32,2048]{2,1,0:T(8,128)(2,1)}, u32[]{:S(2)}, u32[]{:S(2)}) async-start(bf16[8,32,2048]{2,1,0:T(8,128)(2,1)} %shard_map.116), calls=%async_computation.3 | async-start | bytes 2097152 | tf_op jit(solution)/shard_map/all_to_all | solution.py:207
  134.2 8.8 %copy-start.14 = (bf16[8,32,1024]{2,1,0:T(8,128)(2,1)S(1)}, bf16[8,32,1024]{2,1,0:T(8,128)(2,1)}, u32[]{:S(2)}) copy-start(bf16[8,32,1024]{2,1,0:T(8,128)(2,1)} %copy-done.13) | copy-start | bytes 1572868
  138.8 21.1 %collective-permute-start.13 = (bf16[4,16,448]{2,1,0:T(8,128)(2,1)S(1)}, bf16[4,16,448]{2,1,0:T(8,128)(2,1)S(1)}, u32[]{:S(2)}, u32[]{:S(2)}) collective-permute-start(bf16[4,16,448]{2,1,0:T(8,128)(2,1)S(1)} %bitcast.65), channel_id=1, source_target_pairs={{0,48},{16,32},{32,16},{48,0},{1,49},{17,33},{33,17},{49,1},{2,50}... | collective-permute-start | bytes 172040 | tf_op jit(solution)/shard_map/ppermute | solution.py:227
  143.9 18.0 %collective-permute-start.11 = (bf16[4,16,448]{2,1,0:T(8,128)(2,1)S(1)}, bf16[4,16,448]{2,1,0:T(8,128)(2,1)S(1)}, u32[]{:S(2)}, u32[]{:S(2)}) collective-permute-start(bf16[4,16,448]{2,1,0:T(8,128)(2,1)S(1)} %bitcast.64), channel_id=1, source_target_pairs={{0,16},{16,0},{32,48},{48,32},{1,17},{17,1},{33,49},{49,33},{2,18}... | collective-permute-start | bytes 172040 | tf_op jit(solution)/shard_map/ppermute | solution.py:227
  145.8 16.1 %collective-permute-start.12 = (bf16[4,16,448]{2,1,0:T(8,128)(2,1)S(1)}, bf16[4,16,448]{2,1,0:T(8,128)(2,1)S(1)}, u32[]{:S(2)}, u32[]{:S(2)}) collective-permute-start(bf16[4,16,448]{2,1,0:T(8,128)(2,1)S(1)} %bitcast.63), channel_id=1, source_target_pairs={{0,32},{16,48},{32,0},{48,16},{1,33},{17,49},{33,1},{49,17},{2,34}... | collective-permute-start | bytes 172040 | tf_op jit(solution)/shard_map/ppermute | solution.py:227
  149.2 46.6 %collective-permute-start.19 = (bf16[256,256]{1,0:T(8,128)(2,1)S(1)}, bf16[256,256]{1,0:T(8,128)(2,1)S(1)}, u32[]{:S(2)}, u32[]{:S(2)}) collective-permute-start(bf16[256,256]{1,0:T(8,128)(2,1)S(1)} %get-tuple-element.73), channel_id=1, source_target_pairs={{0,3},{1,2},{2,1},{3,0},{4,7},{5,6},{6,5},{7,4},{8,11},{9,10},{10,... | collective-permute-start | bytes 393224 | tf_op jit(solution)/shard_map/ppermute | solution.py:231
  156.3 39.4 %collective-permute-start.18 = (bf16[256,256]{1,0:T(8,128)(2,1)S(1)}, bf16[256,256]{1,0:T(8,128)(2,1)S(1)}, u32[]{:S(2)}, u32[]{:S(2)}) collective-permute-start(bf16[256,256]{1,0:T(8,128)(2,1)S(1)} %get-tuple-element.74), channel_id=1, source_target_pairs={{0,2},{1,3},{2,0},{3,1},{4,6},{5,7},{6,4},{7,5},{8,10},{9,11},{10,... | collective-permute-start | bytes 393224 | tf_op jit(solution)/shard_map/ppermute | solution.py:231
  159.9 35.9 %collective-permute-start.17 = (bf16[256,256]{1,0:T(8,128)(2,1)S(1)}, bf16[256,256]{1,0:T(8,128)(2,1)S(1)}, u32[]{:S(2)}, u32[]{:S(2)}) collective-permute-start(bf16[256,256]{1,0:T(8,128)(2,1)S(1)} %get-tuple-element.75), channel_id=1, source_target_pairs={{0,1},{1,0},{2,3},{3,2},{4,5},{5,4},{6,7},{7,6},{8,9},{9,8},{10,11... | collective-permute-start | bytes 393224 | tf_op jit(solution)/shard_map/ppermute | solution.py:231
  161.9 20.9 %collective-permute-start.14 = (bf16[4,16,448]{2,1,0:T(8,128)(2,1)S(1)}, bf16[4,16,448]{2,1,0:T(8,128)(2,1)S(1)}, u32[]{:S(2)}, u32[]{:S(2)}) collective-permute-start(bf16[4,16,448]{2,1,0:T(8,128)(2,1)S(1)} %pad_maximum_fusion.6), channel_id=1, source_target_pairs={{0,4},{4,0},{8,12},{12,8},{1,5},{5,1},{9,13},{13,9},{2,6},{6,2},{1... | collective-permute-start | bytes 172040 | tf_op jit(solution)/shard_map/ppermute | solution.py:227
  177.6 10.9 %collective-permute-start.15 = (bf16[4,16,448]{2,1,0:T(8,128)(2,1)S(1)}, bf16[4,16,448]{2,1,0:T(8,128)(2,1)S(1)}, u32[]{:S(2)}, u32[]{:S(2)}) collective-permute-start(bf16[4,16,448]{2,1,0:T(8,128)(2,1)S(1)} %pad_maximum_fusion.7), channel_id=1, source_target_pairs={{0,8},{4,12},{8,0},{12,4},{1,9},{5,13},{9,1},{13,5},{2,10},{6,14},... | collective-permute-start | bytes 172040 | tf_op jit(solution)/shard_map/ppermute | solution.py:227
  182.9 12.9 %collective-permute-start.16 = (bf16[4,16,448]{2,1,0:T(8,128)(2,1)S(1)}, bf16[4,16,448]{2,1,0:T(8,128)(2,1)S(1)}, u32[]{:S(2)}, u32[]{:S(2)}) collective-permute-start(bf16[4,16,448]{2,1,0:T(8,128)(2,1)S(1)} %pad_maximum_fusion.8), channel_id=1, source_target_pairs={{0,12},{4,8},{8,4},{12,0},{1,13},{5,9},{9,5},{13,1},{2,14},{6,10},... | collective-permute-start | bytes 172040 | tf_op jit(solution)/shard_map/ppermute | solution.py:227
  199.0 29.7 %all-to-all-start.5 = ((bf16[16,16,448]{2,1,0:T(8,128)(2,1)}), bf16[16,16,448]{2,1,0:T(8,128)(2,1)S(1)}, u32[]{:S(2)}, u32[]{:S(2)}) async-start(bf16[16,16,448]{2,1,0:T(8,128)(2,1)} %bitcast.60), calls=%async_computation.5 | async-start | bytes 524288 | tf_op jit(solution)/shard_map/all_to_all | solution.py:207
  205.4 14.2 %collective-permute-start.20 = (bf16[256,512]{1,0:T(8,128)(2,1)S(1)}, bf16[256,512]{1,0:T(8,128)(2,1)S(1)}, u32[]{:S(2)}, u32[]{:S(2)}) collective-permute-start(bf16[256,512]{1,0:T(8,128)(2,1)S(1)} %pad_maximum_fusion.2), channel_id=1, source_target_pairs={{0,1},{1,0},{2,3},{3,2},{4,5},{5,4},{6,7},{7,6},{8,9},{9,8},{10,11... | collective-permute-start | bytes 786440 | tf_op jit(solution)/shard_map/ppermute | solution.py:231
  208.9 12.6 %collective-permute-start.21 = (bf16[256,512]{1,0:T(8,128)(2,1)S(1)}, bf16[256,512]{1,0:T(8,128)(2,1)S(1)}, u32[]{:S(2)}, u32[]{:S(2)}) collective-permute-start(bf16[256,512]{1,0:T(8,128)(2,1)S(1)} %pad_maximum_fusion.3), channel_id=1, source_target_pairs={{0,2},{1,3},{2,0},{3,1},{4,6},{5,7},{6,4},{7,5},{8,10},{9,11},{10,... | collective-permute-start | bytes 786440 | tf_op jit(solution)/shard_map/ppermute | solution.py:231
  214.1 2.0 copy-start.8
  214.1 2.0 copy-start.9
  214.1 2.0 copy-start.10
  214.2 13.0 %collective-permute-start.22 = (bf16[256,512]{1,0:T(8,128)(2,1)S(1)}, bf16[256,512]{1,0:T(8,128)(2,1)S(1)}, u32[]{:S(2)}, u32[]{:S(2)}) collective-permute-start(bf16[256,512]{1,0:T(8,128)(2,1)S(1)} %pad_maximum_fusion.4), channel_id=1, source_target_pairs={{0,3},{1,2},{2,1},{3,0},{4,7},{5,6},{6,5},{7,4},{8,11},{9,10},{10,... | collective-permute-start | bytes 786440 | tf_op jit(solution)/shard_map/ppermute | solution.py:231

commit v6 on v4

--- a/solution.py
+++ b/solution.py
@@ -147,23 +147,27 @@
     out_ref[...] = jnp.concatenate([out_rows, in_rows], axis=1).astype(BF)
 
 
-def down_kernel(factor, *refs):
-    rows_refs, unit_refs, grad_ref = refs[:SLICES], refs[SLICES:-1], refs[-1]
-    width = grad_ref.shape[0]
-    total = 0.0
-    for rows_ref, unit_ref in zip(rows_refs, unit_refs):
-        total += dot(rows_ref[:, width:], unit_ref[...], FIRST)
-    grad_ref[...] = total * factor
-
-
-def in_kernel(factor, *refs):
-    rows_refs, unit_refs, grad_refs = refs[:SLICES], refs[SLICES:-2], refs[-2:]
-    width, hs = grad_refs[0].shape
-    total = 0.0
-    for rows_ref, unit_ref in zip(rows_refs, unit_refs):
-        total += dot(rows_ref[:, :width], unit_ref[...], FIRST)
-    grad_refs[0][...] = total[:, :hs] * factor
-    grad_refs[1][...] = total[:, hs:] * factor
+def down_kernel(rows_ref, next_ref, own_ref, got_ref, keep_ref, away_ref):
+    width, hs = keep_ref.shape
+    rows, following = rows_ref[:, width:], next_ref[:, width:]
+    for step, out_ref in ((0, keep_ref), (2, away_ref)):
+        there = slice(step // 2 * hs, (step // 2 + 1) * hs)
+        total = dot(rows, own_ref[:, step * hs : (step + 1) * hs], FIRST)
+        total += dot(following, got_ref[:, there], FIRST)
+        out_ref[...] = total.astype(out_ref.dtype)
+
+
+def in_kernel(rows_ref, next_ref, own_ref, got_ref, keep_ref, away_ref):
+    width, hs = keep_ref.shape[0], keep_ref.shape[1] // 2
+    half = own_ref.shape[1] // 2
+    rows, following = rows_ref[:, :width], next_ref[:, :width]
+    for step, out_ref in ((0, keep_ref), (2, away_ref)):
+        for side in (0, 1):
+            here = slice(side * half + step * hs, side * half + (step + 1) * hs)
+            there = slice((step + side) * hs, (step + side + 1) * hs)
+            total = dot(rows, own_ref[:, here], FIRST)
+            total += dot(following, got_ref[:, there], FIRST)
+            out_ref[:, side * hs : (side + 1) * hs] = total.astype(out_ref.dtype)
 
 
 def home_kernel(ids_ref, weight_ref, back_ref, mixed_ref, grad_ref):
@@ -199,10 +203,6 @@
     return swap(copies, "y").reshape(count * rows, cols)
 
 
-def to_slice(value, step):
-    return lax.ppermute(value, SLICE, [(i, i ^ step) for i in range(SLICES)])
-
-
 def share(value):
     across = swap_pair(value, "zb")
     return [value, swap_pair(value, "c"), across, swap_pair(across, "c")]
@@ -224,15 +224,14 @@
     pre_local, rows, w_down = lax.optimization_barrier((pre_local, rows, w_down))
     pre_part, pre_round = sum_y(pre_local)
     w_out = share(w_down[0].T)
-    every = share(rows)
+    rows_next = swap_pair(rows, "c")
     (act_local,) = local(act_kernel, [((slots, units), BF)], rows, *w_out)
-    act_local, every = lax.optimization_barrier((act_local, every))
     act_part, act_round = sum_y(act_local)
 
     pre_other = swap_pair(pre_round, "zh")
     copies = (8, slots // 8)
     (hidden,) = local(hidden_kernel, [(copies + (units,), BF)], pre_part, pre_other)
-    hidden, act_round = lax.optimization_barrier((hidden, act_round))
+    hidden, act_round, rows_next = lax.optimization_barrier((hidden, act_round, rows_next))
     hidden = gather_y(hidden)
     act_other = swap_pair(act_round, "zh")
     (deltas,) = local(
@@ -240,32 +239,34 @@
     )
     deltas = gather_y(deltas)
 
-    def of_slice(value, blocks):
+    def to_next(value):
+        sides = value.shape[1] // units
         cut = [
-            [value[:, (b * SLICES + s) * hs :][:, :hs] for b in range(blocks)]
-            for s in range(SLICES)
+            value[:, side * units + step * hs :][:, :hs] for step in (1, 3) for side in range(sides)
         ]
-        cut = [jnp.concatenate(part, axis=1) for part in cut]
-        return cut[:1] + [to_slice(cut[step], step) for step in (1, 2, 3)]
-
-    hidden_own = of_slice(hidden, 1)
-    deltas, hidden, hidden_own = lax.optimization_barrier((deltas, hidden, hidden_own))
+        return swap_pair(jnp.concatenate(cut, axis=1), "c")
+
+    shape = (width, hs)
+    down_keep, down_away = local(
+        down_kernel, [(shape, F32), (shape, BF)], rows, rows_next, hidden, to_next(hidden)
+    )
+    down_got = swap_pair(down_away, "zb")
+    deltas, hidden, down_got = lax.optimization_barrier((deltas, hidden, down_got))
+    deltas_got = to_next(deltas)
     (back,) = local(
         back_kernel, [((slots, 2 * width), BF)], hidden, deltas, *w_in, *w_out, fetch=10
     )
+    back, deltas_got = lax.optimization_barrier((back, deltas_got))
     back = swap(back.reshape(EXPERTS, CAP, 2 * width), OWN).reshape(slots, 2 * width)
 
+    shape = (width, 2 * hs)
+    in_keep, in_away = local(
+        in_kernel, [(shape, F32), (shape, BF)], rows, rows_next, deltas, deltas_got
+    )
     factor = 1.0 / math.sqrt(8 * tok_rows)
-
-    def down(*refs):
-        down_kernel(factor, *refs)
-
-    def into(*refs):
-        in_kernel(factor, *refs)
-
-    one = ((width, hs), F32)
-    (down_grad,) = local(down, [one], *every, *hidden_own)
-    gate_grad, up_grad = local(into, [one, one], *every, *of_slice(deltas, 2))
+    in_grad = (in_keep + swap_pair(in_away, "zb").astype(F32)) * factor
+    gate_grad, up_grad = in_grad[:, :hs], in_grad[:, hs:]
+    down_grad = (down_keep + down_got.astype(F32)) * factor
     mixed, tokens_grad = local(home_kernel, [((tok_rows, width), F32)] * 2, ids, weight, back)
     return (mixed, tokens_grad, gate_grad[None], up_grad[None], down_grad.T[None])
 

time: 224 us -> 225 us (level)
  the two profiles are of different devices: /device:TPU:129 before, /device:TPU:1 now
where the time goes in v6:
time: 225 us; the launch traced here: 222 us
  starting transfers between devices  135 us (60%)
  waiting for transfers between devices  67.9 us (30%)
  Pallas kernels  14.2 us (6%)
  local copies, waits for them, and re-layouts  3.38 us (2%)
    ppermute x13, starting transfers between devices, swap_pair(): return lax.ppermute(value, axis, [(0, 1), (1, 0)])  74.7 us
    all_to_all x6, starting transfers between devices, swap(): return lax.all_to_all(value, axis, split_axis=0, concat_axis=0, tiled=True)  60.1 us
    ppermute x13, waiting for transfers between devices, swap_pair(): return lax.ppermute(value, axis, [(0, 1), (1, 0)])  43.9 us
    all_to_all x6, waiting for transfers between devices, swap(): return lax.all_to_all(value, axis, split_axis=0, concat_axis=0, tiled=True)  23.9 us
    pallas_call x11, Pallas kernels, local(): pl.pallas_call(fetching if fetch else kernel, out_shape=[jax.ShapeDtypeSt...  14.2 us
  transfers between devices with their start and end apart: 19, of which 14 were waited for; matrix products, arithmetic and copies ran while one was open for 1% of the time, Pallas kernels for 4%

profile of v6, /device:TPU:1, one launch (start us, length us, event | category | flops | bytes accessed | tf_op | source)
XLA Modules:
  0.0 222.3 jit_solution(10124130844394956590)
XLA Ops:
  0.6 2.2 %shard_map.110 = bf16[256,896]{1,0:T(8,128)(2,1)} custom-call(s32[2,64]{1,0:T(2,128)} %bitcast.39, f32[2,64]{1,0:T(2,128)} %bitcast.41, bf16[64,448]{1,0:T(8,128)(2,1)} %refs_2_.1, bf16[64,448]{1,0:T(8,128)(2,1)} %refs_3_.1), custom_call_target="tpu_custom_call" | custom-call | flops 2000000000 | bytes 1148928 | tf_op jit(solution)/shard_map/pallas_call | solution.py:48
  2.9 0.0 copy-start.13
  2.9 0.0 copy-start.14
  2.9 17.2 %all-to-all-start = ((bf16[16,16,896]{2,1,0:T(8,128)(2,1)}), bf16[16,16,896]{2,1,0:T(8,128)(2,1)S(1)}, u32[]{:S(2)}, u32[]{:S(2)}) async-start(bf16[16,16,896]{2,1,0:T(8,128)(2,1)} %bitcast.44), calls=%async_computation | async-start | bytes 917504 | tf_op jit(solution)/shard_map/all_to_all | solution.py:187
  20.1 0.0 copy-start.3
  20.1 4.0 %collective-permute-start.1 = (bf16[448,512]{1,0:T(8,128)(2,1)S(1)}, bf16[448,512]{1,0:T(8,128)(2,1)S(1)}, u32[]{:S(2)}, u32[]{:S(2)}) collective-permute-start(bf16[448,512]{1,0:T(8,128)(2,1)S(1)} %pad_maximum_fusion.1.refs_0_.refs_2_), channel_id=1, source_target_pairs={{0,2},{2,0},{1,3},{3,1},{4,6},{6,4},{5,7},{7,5},{8,10},{10,8},{9,1... | collective-permute-start | bytes 1376264 | tf_op jit(solution)/shard_map/ppermute | solution.py:198
  24.1 3.1 %collective-permute-start = (bf16[448,512]{1,0:T(8,128)(2,1)S(1)}, bf16[448,512]{1,0:T(8,128)(2,1)S(1)}, u32[]{:S(2)}, u32[]{:S(2)}) collective-permute-start(bf16[448,512]{1,0:T(8,128)(2,1)S(1)} %pad_maximum_fusion.1.refs_0_.refs_2_), channel_id=1, source_target_pairs={{0,1},{1,0},{2,3},{3,2},{4,5},{5,4},{6,7},{7,6},{8,9},{9,8},{10,11... | collective-permute-start | bytes 1376264 | tf_op jit(solution)/shard_map/ppermute | solution.py:198
  27.3 10.0 %collective-permute-done.1.refs_2_.refs_4_ = bf16[448,512]{1,0:T(8,128)(2,1)S(1)} collective-permute-done((bf16[448,512]{1,0:T(8,128)(2,1)S(1)}, bf16[448,512]{1,0:T(8,128)(2,1)S(1)}, u32[]{:S(2)}, u32[]{:S(2)}) %collective-permute-start.1) | collective-permute-done | bytes 458784 | tf_op jit(solution)/shard_map/ppermute | solution.py:198
  37.2 3.3 %collective-permute-start.2 = (bf16[448,512]{1,0:T(8,128)(2,1)S(1)}, bf16[448,512]{1,0:T(8,128)(2,1)S(1)}, u32[]{:S(2)}, u32[]{:S(2)}) collective-permute-start(bf16[448,512]{1,0:T(8,128)(2,1)S(1)} %collective-permute-done.1.refs_2_.refs_4_), channel_id=1, source_target_pairs={{0,1},{1,0},{2,3},{3,2},{4,5},{5,4},{6,7},{7,6},{8,9},{9,8},{10,11... | collective-permute-start | bytes 1376264 | tf_op jit(solution)/shard_map/ppermute | solution.py:198
  40.5 0.0 collective-permute-done.refs_1_.refs_3_
  40.5 0.0 copy-start.5
  40.5 1.4 collective-permute-done.2.refs_3_.refs_5_
  42.0 1.6 all-to-all-done
  43.5 1.7 shard_map.111
  45.2 0.0 copy-done.3
  45.2 0.0 copy-done.5
  45.2 0.0 copy-start.7
  45.2 7.0 %all-to-all-start.1 = ((bf16[8,32,2048]{2,1,0:T(8,128)(2,1)}), bf16[8,32,2048]{2,1,0:T(8,128)(2,1)S(1)}, u32[]{:S(2)}, u32[]{:S(2)}) async-start(bf16[8,32,2048]{2,1,0:T(8,128)(2,1)} %bitcast.6), calls=%async_computation.1 | async-start | bytes 2097152 | tf_op jit(solution)/shard_map/all_to_all | solution.py:187
  52.2 6.5 %collective-permute-start.5 = (bf16[448,256]{1,0:T(8,128)(2,1)S(1)}, bf16[448,256]{1,0:T(8,128)(2,1)S(1)}, u32[]{:S(2)}, u32[]{:S(2)}) collective-permute-start(bf16[448,256]{1,0:T(8,128)(2,1)S(1)} %bitcast.36), channel_id=1, source_target_pairs={{0,2},{2,0},{1,3},{3,1},{4,6},{6,4},{5,7},{7,5},{8,10},{10,8},{9,1... | collective-permute-start | bytes 688136 | tf_op jit(solution)/shard_map/ppermute | solution.py:198
  58.8 3.2 %collective-permute-start.4 = (bf16[448,256]{1,0:T(8,128)(2,1)S(1)}, bf16[448,256]{1,0:T(8,128)(2,1)S(1)}, u32[]{:S(2)}, u32[]{:S(2)}) collective-permute-start(bf16[448,256]{1,0:T(8,128)(2,1)S(1)} %bitcast.37), channel_id=1, source_target_pairs={{0,1},{1,0},{2,3},{3,2},{4,5},{5,4},{6,7},{7,6},{8,9},{9,8},{10,11... | collective-permute-start | bytes 688136 | tf_op jit(solution)/shard_map/ppermute | solution.py:198
  61.9 0.7 collective-permute-done.5.refs_2_.refs_8_
  62.7 5.2 %collective-permute-start.6 = (bf16[448,256]{1,0:T(8,128)(2,1)S(1)}, bf16[448,256]{1,0:T(8,128)(2,1)S(1)}, u32[]{:S(2)}, u32[]{:S(2)}) collective-permute-start(bf16[448,256]{1,0:T(8,128)(2,1)S(1)} %collective-permute-done.5.refs_2_.refs_8_), channel_id=1, source_target_pairs={{0,1},{1,0},{2,3},{3,2},{4,5},{5,4},{6,7},{7,6},{8,9},{9,8},{10,11... | collective-permute-start | bytes 688136 | tf_op jit(solution)/shard_map/ppermute | solution.py:198
  67.9 0.0 collective-permute-done.4.refs_1_.refs_7_
  67.9 1.1 collective-permute-done.6.refs_3_.refs_9_
  69.0 1.3 shard_map.113
  70.3 0.7 copy-done.9
  71.0 0.7 copy-done.10
  71.7 5.6 %all-to-all-done.1.got_ref = bf16[8,32,2048]{2,1,0:T(8,128)(2,1)S(1)} async-done(((bf16[8,32,2048]{2,1,0:T(8,128)(2,1)}), bf16[8,32,2048]{2,1,0:T(8,128)(2,1)S(1)}, u32[]{:S(2)}, u32[]{:S(2)}) %all-to-all-start.1) | async-done | bytes 1048608 | tf_op jit(solution)/shard_map/all_to_all | solution.py:187
  77.3 3.5 %all-to-all-start.2 = ((bf16[8,32,1024]{2,1,0:T(8,128)(2,1)}), bf16[8,32,1024]{2,1,0:T(8,128)(2,1)S(1)}, u32[]{:S(2)}, u32[]{:S(2)}) async-start(bf16[8,32,1024]{2,1,0:T(8,128)(2,1)} %bitcast.10), calls=%async_computation.2 | async-start | bytes 1048576 | tf_op jit(solution)/shard_map/all_to_all | solution.py:187
  80.8 6.5 %collective-permute-start.7 = (bf16[256,896]{1,0:T(8,128)(2,1)S(1)}, bf16[256,896]{1,0:T(8,128)(2,1)S(1)}, u32[]{:S(2)}, u32[]{:S(2)}) collective-permute-start(bf16[256,896]{1,0:T(8,128)(2,1)S(1)} %bitcast.31), channel_id=1, source_target_pairs={{0,1},{1,0},{2,3},{3,2},{4,5},{5,4},{6,7},{7,6},{8,9},{9,8},{10,11... | collective-permute-start | bytes 1376264 | tf_op jit(solution)/shard_map/ppermute | solution.py:198
  87.4 0.1 shard_map.112
  87.5 15.5 %collective-permute-start.3 = (bf16[32,2048]{1,0:T(8,128)(2,1)S(1)}, bf16[32,2048]{1,0:T(8,128)(2,1)S(1)}, u32[]{:S(2)}, u32[]{:S(2)}) collective-permute-start(bf16[32,2048]{1,0:T(8,128)(2,1)S(1)} %get-tuple-element.34), channel_id=1, source_target_pairs={{0,64},{64,0},{1,65},{65,1},{2,66},{66,2},{3,67},{67,3},{4,68},{68... | collective-permute-start | bytes 393224 | tf_op jit(solution)/shard_map/ppermute | solution.py:198
  103.0 0.0 all-to-all-done.2.got_ref
  103.0 0.1 shard_map.114
  103.1 3.8 %collective-permute-done.3.other_ref = bf16[32,2048]{1,0:T(8,128)(2,1)S(1)} collective-permute-done((bf16[32,2048]{1,0:T(8,128)(2,1)S(1)}, bf16[32,2048]{1,0:T(8,128)(2,1)S(1)}, u32[]{:S(2)}, u32[]{:S(2)}) %collective-permute-start.3) | collective-permute-done | bytes 131104 | tf_op jit(solution)/shard_map/ppermute | solution.py:198
  106.9 0.9 shard_map.115
  107.7 0.0 collective-permute-done.7.next_ref
  107.7 6.8 %all-to-all-start.4 = ((bf16[8,32,1024]{2,1,0:T(8,128)(2,1)}), bf16[8,32,1024]{2,1,0:T(8,128)(2,1)S(1)}, u32[]{:S(2)}, u32[]{:S(2)}) async-start(bf16[8,32,1024]{2,1,0:T(8,128)(2,1)} %shard_map.115), calls=%async_computation.4 | async-start | bytes 1048576 | tf_op jit(solution)/shard_map/all_to_all | solution.py:187
  114.6 11.9 %collective-permute-start.8 = (bf16[32,1024]{1,0:T(8,128)(2,1)S(1)}, bf16[32,1024]{1,0:T(8,128)(2,1)S(1)}, u32[]{:S(2)}, u32[]{:S(2)}) collective-permute-start(bf16[32,1024]{1,0:T(8,128)(2,1)S(1)} %get-tuple-element.39), channel_id=1, source_target_pairs={{0,64},{64,0},{1,65},{65,1},{2,66},{66,2},{3,67},{67,3},{4,68},{68... | collective-permute-start | bytes 196616 | tf_op jit(solution)/shard_map/ppermute | solution.py:198
  126.4 1.8 collective-permute-done.8.act_other_ref
  128.3 1.1 shard_map.116
  129.4 3.1 %all-to-all-done.4 = bf16[8,32,1024]{2,1,0:T(8,128)(2,1)S(1)} async-done(((bf16[8,32,1024]{2,1,0:T(8,128)(2,1)}), bf16[8,32,1024]{2,1,0:T(8,128)(2,1)S(1)}, u32[]{:S(2)}, u32[]{:S(2)}) %all-to-all-start.4) | async-done | bytes 524320 | tf_op jit(solution)/shard_map/all_to_all | solution.py:187
  132.5 3.6 %all-to-all-start.3 = ((bf16[8,32,2048]{2,1,0:T(8,128)(2,1)}), bf16[8,32,2048]{2,1,0:T(8,128)(2,1)S(1)}, u32[]{:S(2)}, u32[]{:S(2)}) async-start(bf16[8,32,2048]{2,1,0:T(8,128)(2,1)} %shard_map.116), calls=%async_computation.3 | async-start | bytes 2097152 | tf_op jit(solution)/shard_map/all_to_all | solution.py:187
  136.2 5.8 %collective-permute-start.9 = (bf16[256,512]{1,0:T(8,128)(2,1)S(1)}, bf16[256,512]{1,0:T(8,128)(2,1)S(1)}, u32[]{:S(2)}, u32[]{:S(2)}) collective-permute-start(bf16[256,512]{1,0:T(8,128)(2,1)S(1)} %pad_maximum_fusion.2), channel_id=1, source_target_pairs={{0,1},{1,0},{2,3},{3,2},{4,5},{5,4},{6,7},{7,6},{8,9},{9,8},{10,11... | collective-permute-start | bytes 786440 | tf_op jit(solution)/shard_map/ppermute | solution.py:198
  141.9 1.1 collective-permute-done.9.got_ref
  143.1 0.7 shard_map.117
  143.8 1.9 collective-permute-start.10
  145.7 6.8 %collective-permute-done.10 = bf16[448,256]{1,0:T(8,128)(2,1)S(1)} collective-permute-done((bf16[448,256]{1,0:T(8,128)(2,1)S(1)}, bf16[448,256]{1,0:T(8,128)(2,1)S(1)}, u32[]{:S(2)}, u32[]{:S(2)}) %collective-permute-start.10) | collective-permute-done | bytes 229408 | tf_op jit(solution)/shard_map/ppermute | solution.py:198
  152.5 9.3 %all-to-all-done.3 = bf16[8,32,2048]{2,1,0:T(8,128)(2,1)S(1)} async-done(((bf16[8,32,2048]{2,1,0:T(8,128)(2,1)}), bf16[8,32,2048]{2,1,0:T(8,128)(2,1)S(1)}, u32[]{:S(2)}, u32[]{:S(2)}) %all-to-all-start.3) | async-done | bytes 1048608 | tf_op jit(solution)/shard_map/all_to_all | solution.py:187
  161.9 0.1 pad_maximum_fusion
  162.0 0.9 copy-done
  162.8 5.8 %collective-permute-start.11 = (bf16[256,1024]{1,0:T(8,128)(2,1)S(1)}, bf16[256,1024]{1,0:T(8,128)(2,1)S(1)}, u32[]{:S(2)}, u32[]{:S(2)}) collective-permute-start(bf16[256,1024]{1,0:T(8,128)(2,1)S(1)} %pad_maximum_fusion), channel_id=1, source_target_pairs={{0,1},{1,0},{2,3},{3,2},{4,5},{5,4},{6,7},{7,6},{8,9},{9,8},{10,11... | collective-permute-start | bytes 1572872 | tf_op jit(solution)/shard_map/ppermute | solution.py:198
  168.7 4.2 %shard_map.118 = bf16[256,896]{1,0:T(8,128)(2,1)} custom-call(bf16[256,1024]{1,0:T(8,128)(2,1)} %bitcast.28, bf16[256,2048]{1,0:T(8,128)(2,1)} %bitcast.24, bf16[448,512]{1,0:T(8,128)(2,1)} %copy-done.3, bf16[448,512]{1,0:T(8,128)(2,1)} %copy-done.5, bf16[448,512]{1,0:T(8,128)(2,1)} %copy-done.4, bf16[448,512]{1,0:T(8,128)(2,1)} %copy-done.6, ...), custom_call_target="tpu_custom_call" | custom-call | flops 2000000000 | bytes 9568256 | tf_op jit(solution)/shard_map/pallas_call | solution.py:48
  172.9 0.0 collective-permute-done.11.got_ref
  172.9 22.1 %all-to-all-start.5 = ((bf16[16,16,896]{2,1,0:T(8,128)(2,1)}), bf16[16,16,896]{2,1,0:T(8,128)(2,1)S(1)}, u32[]{:S(2)}, u32[]{:S(2)}) async-start(bf16[16,16,896]{2,1,0:T(8,128)(2,1)} %bitcast.43), calls=%async_computation.5 | async-start | bytes 917504 | tf_op jit(solution)/shard_map/all_to_all | solution.py:187
  195.1 0.7 shard_map.120
  195.7 1.9 collective-permute-start.12
  197.7 0.8 multiply_bitcast_fusion
  198.5 17.2 %collective-permute-done.12 = bf16[448,512]{1,0:T(8,128)(2,1)S(1)} collective-permute-done((bf16[448,512]{1,0:T(8,128)(2,1)S(1)}, bf16[448,512]{1,0:T(8,128)(2,1)S(1)}, u32[]{:S(2)}, u32[]{:S(2)}) %collective-permute-start.12) | collective-permute-done | bytes 458784 | tf_op jit(solution)/shard_map/ppermute | solution.py:198
  215.7 0.1 add_multiply_fusion
  215.9 0.0 copy-start.12
  215.9 1.0 slice_bitcast_fusion
  216.9 4.2 %all-to-all-done.5 = bf16[16,16,896]{2,1,0:T(8,128)(2,1)S(1)} async-done(((bf16[16,16,896]{2,1,0:T(8,128)(2,1)}), bf16[16,16,896]{2,1,0:T(8,128)(2,1)S(1)}, u32[]{:S(2)}, u32[]{:S(2)}) %all-to-all-start.5) | async-done | bytes 458784 | tf_op jit(solution)/shard_map/all_to_all | solution.py:187
  221.1 1.2 shard_map.119
  (27 shorter events, 0.1 us)
Async XLA Ops:
  2.9 17.2 %copy-start.13 = (bf16[1,448,256]{2,1,0:T(8,128)(2,1)S(1)}, bf16[1,448,256]{2,1,0:T(8,128)(2,1)}, u32[]{:S(2)}) copy-start(bf16[1,448,256]{2,1,0:T(8,128)(2,1)} %param.12) | copy-start | bytes 688132
  2.9 17.2 %copy-start.14 = (bf16[1,448,256]{2,1,0:T(8,128)(2,1)S(1)}, bf16[1,448,256]{2,1,0:T(8,128)(2,1)}, u32[]{:S(2)}) copy-start(bf16[1,448,256]{2,1,0:T(8,128)(2,1)} %param.11) | copy-start | bytes 688132
  2.9 40.6 %all-to-all-start = ((bf16[16,16,896]{2,1,0:T(8,128)(2,1)}), bf16[16,16,896]{2,1,0:T(8,128)(2,1)S(1)}, u32[]{:S(2)}, u32[]{:S(2)}) async-start(bf16[16,16,896]{2,1,0:T(8,128)(2,1)} %bitcast.44), calls=%async_computation | async-start | bytes 917504 | tf_op jit(solution)/shard_map/all_to_all | solution.py:187
  20.1 25.1 %copy-start.3 = (bf16[448,512]{1,0:T(8,128)(2,1)}, bf16[448,512]{1,0:T(8,128)(2,1)S(1)}, u32[]{:S(2)}) copy-start(bf16[448,512]{1,0:T(8,128)(2,1)S(1)} %pad_maximum_fusion.1.refs_0_.refs_2_) | copy-start | bytes 1376260
  20.1 17.1 %collective-permute-start.1 = (bf16[448,512]{1,0:T(8,128)(2,1)S(1)}, bf16[448,512]{1,0:T(8,128)(2,1)S(1)}, u32[]{:S(2)}, u32[]{:S(2)}) collective-permute-start(bf16[448,512]{1,0:T(8,128)(2,1)S(1)} %pad_maximum_fusion.1.refs_0_.refs_2_), channel_id=1, source_target_pairs={{0,2},{2,0},{1,3},{3,1},{4,6},{6,4},{5,7},{7,5},{8,10},{10,8},{9,1... | collective-permute-start | bytes 1376264 | tf_op jit(solution)/shard_map/ppermute | solution.py:198
  24.1 16.4 %collective-permute-start = (bf16[448,512]{1,0:T(8,128)(2,1)S(1)}, bf16[448,512]{1,0:T(8,128)(2,1)S(1)}, u32[]{:S(2)}, u32[]{:S(2)}) collective-permute-start(bf16[448,512]{1,0:T(8,128)(2,1)S(1)} %pad_maximum_fusion.1.refs_0_.refs_2_), channel_id=1, source_target_pairs={{0,1},{1,0},{2,3},{3,2},{4,5},{5,4},{6,7},{7,6},{8,9},{9,8},{10,11... | collective-permute-start | bytes 1376264 | tf_op jit(solution)/shard_map/ppermute | solution.py:198
  37.2 8.0 %copy-start.4 = (bf16[448,512]{1,0:T(8,128)(2,1)}, bf16[448,512]{1,0:T(8,128)(2,1)S(1)}, u32[]{:S(2)}) copy-start(bf16[448,512]{1,0:T(8,128)(2,1)S(1)} %collective-permute-done.1.refs_2_.refs_4_) | copy-start | bytes 1376260
  37.2 4.7 %collective-permute-start.2 = (bf16[448,512]{1,0:T(8,128)(2,1)S(1)}, bf16[448,512]{1,0:T(8,128)(2,1)S(1)}, u32[]{:S(2)}, u32[]{:S(2)}) collective-permute-start(bf16[448,512]{1,0:T(8,128)(2,1)S(1)} %collective-permute-done.1.refs_2_.refs_4_), channel_id=1, source_target_pairs={{0,1},{1,0},{2,3},{3,2},{4,5},{5,4},{6,7},{7,6},{8,9},{9,8},{10,11... | collective-permute-start | bytes 1376264 | tf_op jit(solution)/shard_map/ppermute | solution.py:198
  40.5 4.7 %copy-start.5 = (bf16[448,512]{1,0:T(8,128)(2,1)}, bf16[448,512]{1,0:T(8,128)(2,1)S(1)}, u32[]{:S(2)}) copy-start(bf16[448,512]{1,0:T(8,128)(2,1)S(1)} %collective-permute-done.refs_1_.refs_3_) | copy-start | bytes 1376260
  41.9 3.3 %copy-start.6 = (bf16[448,512]{1,0:T(8,128)(2,1)}, bf16[448,512]{1,0:T(8,128)(2,1)S(1)}, u32[]{:S(2)}) copy-start(bf16[448,512]{1,0:T(8,128)(2,1)S(1)} %collective-permute-done.2.refs_3_.refs_5_) | copy-start | bytes 1376260
  45.2 7.0 %copy-start.7 = (bf16[1,256,448]{1,2,0:T(8,128)(2,1)S(1)}, bf16[1,256,448]{1,2,0:T(8,128)(2,1)}, u32[]{:S(2)}) copy-start(bf16[1,256,448]{1,2,0:T(8,128)(2,1)} %param.13) | copy-start | bytes 688132
  45.2 32.1 %all-to-all-start.1 = ((bf16[8,32,2048]{2,1,0:T(8,128)(2,1)}), bf16[8,32,2048]{2,1,0:T(8,128)(2,1)S(1)}, u32[]{:S(2)}, u32[]{:S(2)}) async-start(bf16[8,32,2048]{2,1,0:T(8,128)(2,1)} %bitcast.6), calls=%async_computation.1 | async-start | bytes 2097152 | tf_op jit(solution)/shard_map/all_to_all | solution.py:187
  52.2 10.5 %collective-permute-start.5 = (bf16[448,256]{1,0:T(8,128)(2,1)S(1)}, bf16[448,256]{1,0:T(8,128)(2,1)S(1)}, u32[]{:S(2)}, u32[]{:S(2)}) collective-permute-start(bf16[448,256]{1,0:T(8,128)(2,1)S(1)} %bitcast.36), channel_id=1, source_target_pairs={{0,2},{2,0},{1,3},{3,1},{4,6},{6,4},{5,7},{7,5},{8,10},{10,8},{9,1... | collective-permute-start | bytes 688136 | tf_op jit(solution)/shard_map/ppermute | solution.py:198
  58.8 9.1 %collective-permute-start.4 = (bf16[448,256]{1,0:T(8,128)(2,1)S(1)}, bf16[448,256]{1,0:T(8,128)(2,1)S(1)}, u32[]{:S(2)}, u32[]{:S(2)}) collective-permute-start(bf16[448,256]{1,0:T(8,128)(2,1)S(1)} %bitcast.37), channel_id=1, source_target_pairs={{0,1},{1,0},{2,3},{3,2},{4,5},{5,4},{6,7},{7,6},{8,9},{9,8},{10,11... | collective-permute-start | bytes 688136 | tf_op jit(solution)/shard_map/ppermute | solution.py:198
  62.7 7.6 %copy-start.8 = (bf16[448,256]{1,0:T(8,128)(2,1)}, bf16[448,256]{1,0:T(8,128)(2,1)S(1)}, u32[]{:S(2)}) copy-start(bf16[448,256]{1,0:T(8,128)(2,1)S(1)} %collective-permute-done.5.refs_2_.refs_8_) | copy-start | bytes 688132
  62.7 6.3 %collective-permute-start.6 = (bf16[448,256]{1,0:T(8,128)(2,1)S(1)}, bf16[448,256]{1,0:T(8,128)(2,1)S(1)}, u32[]{:S(2)}, u32[]{:S(2)}) collective-permute-start(bf16[448,256]{1,0:T(8,128)(2,1)S(1)} %collective-permute-done.5.refs_2_.refs_8_), channel_id=1, source_target_pairs={{0,1},{1,0},{2,3},{3,2},{4,5},{5,4},{6,7},{7,6},{8,9},{9,8},{10,11... | collective-permute-start | bytes 688136 | tf_op jit(solution)/shard_map/ppermute | solution.py:198
  70.3 0.7 copy-start.9
  71.0 0.7 copy-start.10
  77.3 25.7 %all-to-all-start.2 = ((bf16[8,32,1024]{2,1,0:T(8,128)(2,1)}), bf16[8,32,1024]{2,1,0:T(8,128)(2,1)S(1)}, u32[]{:S(2)}, u32[]{:S(2)}) async-start(bf16[8,32,1024]{2,1,0:T(8,128)(2,1)} %bitcast.10), calls=%async_computation.2 | async-start | bytes 1048576 | tf_op jit(solution)/shard_map/all_to_all | solution.py:187
  80.8 26.9 %collective-permute-start.7 = (bf16[256,896]{1,0:T(8,128)(2,1)S(1)}, bf16[256,896]{1,0:T(8,128)(2,1)S(1)}, u32[]{:S(2)}, u32[]{:S(2)}) collective-permute-start(bf16[256,896]{1,0:T(8,128)(2,1)S(1)} %bitcast.31), channel_id=1, source_target_pairs={{0,1},{1,0},{2,3},{3,2},{4,5},{5,4},{6,7},{7,6},{8,9},{9,8},{10,11... | collective-permute-start | bytes 1376264 | tf_op jit(solution)/shard_map/ppermute | solution.py:198
  87.5 19.4 %collective-permute-start.3 = (bf16[32,2048]{1,0:T(8,128)(2,1)S(1)}, bf16[32,2048]{1,0:T(8,128)(2,1)S(1)}, u32[]{:S(2)}, u32[]{:S(2)}) collective-permute-start(bf16[32,2048]{1,0:T(8,128)(2,1)S(1)} %get-tuple-element.34), channel_id=1, source_target_pairs={{0,64},{64,0},{1,65},{65,1},{2,66},{66,2},{3,67},{67,3},{4,68},{68... | collective-permute-start | bytes 393224 | tf_op jit(solution)/shard_map/ppermute | solution.py:198
  107.7 24.8 %all-to-all-start.4 = ((bf16[8,32,1024]{2,1,0:T(8,128)(2,1)}), bf16[8,32,1024]{2,1,0:T(8,128)(2,1)S(1)}, u32[]{:S(2)}, u32[]{:S(2)}) async-start(bf16[8,32,1024]{2,1,0:T(8,128)(2,1)} %shard_map.115), calls=%async_computation.4 | async-start | bytes 1048576 | tf_op jit(solution)/shard_map/all_to_all | solution.py:187
  114.6 13.7 %collective-permute-start.8 = (bf16[32,1024]{1,0:T(8,128)(2,1)S(1)}, bf16[32,1024]{1,0:T(8,128)(2,1)S(1)}, u32[]{:S(2)}, u32[]{:S(2)}) collective-permute-start(bf16[32,1024]{1,0:T(8,128)(2,1)S(1)} %get-tuple-element.39), channel_id=1, source_target_pairs={{0,64},{64,0},{1,65},{65,1},{2,66},{66,2},{3,67},{67,3},{4,68},{68... | collective-permute-start | bytes 196616 | tf_op jit(solution)/shard_map/ppermute | solution.py:198
  132.5 10.5 %copy-start.2 = (bf16[8,32,1024]{2,1,0:T(8,128)(2,1)}, bf16[8,32,1024]{2,1,0:T(8,128)(2,1)S(1)}, u32[]{:S(2)}) copy-start(bf16[8,32,1024]{2,1,0:T(8,128)(2,1)S(1)} %all-to-all-done.4) | copy-start | bytes 1572868
  132.5 29.3 %all-to-all-start.3 = ((bf16[8,32,2048]{2,1,0:T(8,128)(2,1)}), bf16[8,32,2048]{2,1,0:T(8,128)(2,1)S(1)}, u32[]{:S(2)}, u32[]{:S(2)}) async-start(bf16[8,32,2048]{2,1,0:T(8,128)(2,1)} %shard_map.116), calls=%async_computation.3 | async-start | bytes 2097152 | tf_op jit(solution)/shard_map/all_to_all | solution.py:187
  136.2 6.9 %collective-permute-start.9 = (bf16[256,512]{1,0:T(8,128)(2,1)S(1)}, bf16[256,512]{1,0:T(8,128)(2,1)S(1)}, u32[]{:S(2)}, u32[]{:S(2)}) collective-permute-start(bf16[256,512]{1,0:T(8,128)(2,1)S(1)} %pad_maximum_fusion.2), channel_id=1, source_target_pairs={{0,1},{1,0},{2,3},{3,2},{4,5},{5,4},{6,7},{7,6},{8,9},{9,8},{10,11... | collective-permute-start | bytes 786440 | tf_op jit(solution)/shard_map/ppermute | solution.py:198
  143.8 8.7 %collective-permute-start.10 = (bf16[448,256]{1,0:T(8,128)(2,1)S(1)}, bf16[448,256]{1,0:T(8,128)(2,1)S(1)}, u32[]{:S(2)}, u32[]{:S(2)}) collective-permute-start(bf16[448,256]{1,0:T(8,128)(2,1)S(1)} %get-tuple-element.42), channel_id=1, source_target_pairs={{0,2},{2,0},{1,3},{3,1},{4,6},{6,4},{5,7},{7,5},{8,10},{10,8},{9,1... | collective-permute-start | bytes 688136 | tf_op jit(solution)/shard_map/ppermute | solution.py:198
  152.5 9.3 %copy-start.15 = (bf16[448,256]{1,0:T(8,128)(2,1)}, bf16[448,256]{1,0:T(8,128)(2,1)S(1)}, u32[]{:S(2)}) copy-start(bf16[448,256]{1,0:T(8,128)(2,1)S(1)} %collective-permute-done.10) | copy-start | bytes 688132
  161.8 1.0 copy-start
  162.8 10.1 %collective-permute-start.11 = (bf16[256,1024]{1,0:T(8,128)(2,1)S(1)}, bf16[256,1024]{1,0:T(8,128)(2,1)S(1)}, u32[]{:S(2)}, u32[]{:S(2)}) collective-permute-start(bf16[256,1024]{1,0:T(8,128)(2,1)S(1)} %pad_maximum_fusion), channel_id=1, source_target_pairs={{0,1},{1,0},{2,3},{3,2},{4,5},{5,4},{6,7},{7,6},{8,9},{9,8},{10,11... | collective-permute-start | bytes 1572872 | tf_op jit(solution)/shard_map/ppermute | solution.py:198
  168.7 26.3 %copy-start.1 = (bf16[8,32,2048]{2,1,0:T(8,128)(2,1)S(1)}, bf16[8,32,2048]{2,1,0:T(8,128)(2,1)}, u32[]{:S(2)}) copy-start(bf16[8,32,2048]{2,1,0:T(8,128)(2,1)} %copy-done) | copy-start | bytes 3145732
  172.9 48.2 %all-to-all-start.5 = ((bf16[16,16,896]{2,1,0:T(8,128)(2,1)}), bf16[16,16,896]{2,1,0:T(8,128)(2,1)S(1)}, u32[]{:S(2)}, u32[]{:S(2)}) async-start(bf16[16,16,896]{2,1,0:T(8,128)(2,1)} %bitcast.43), calls=%async_computation.5 | async-start | bytes 917504 | tf_op jit(solution)/shard_map/all_to_all | solution.py:187
  195.0 2.6 %copy-start.16 = (bf16[448,256]{1,0:T(8,128)(2,1)S(1)}, bf16[448,256]{1,0:T(8,128)(2,1)}, u32[]{:S(2)}) copy-start(bf16[448,256]{1,0:T(8,128)(2,1)} %copy-done.15) | copy-start | bytes 688132
  195.7 20.0 %collective-permute-start.12 = (bf16[448,512]{1,0:T(8,128)(2,1)S(1)}, bf16[448,512]{1,0:T(8,128)(2,1)S(1)}, u32[]{:S(2)}, u32[]{:S(2)}) collective-permute-start(bf16[448,512]{1,0:T(8,128)(2,1)S(1)} %get-tuple-element.50), channel_id=1, source_target_pairs={{0,2},{2,0},{1,3},{3,1},{4,6},{6,4},{5,7},{7,5},{8,10},{10,8},{9,1... | collective-permute-start | bytes 1376264 | tf_op jit(solution)/shard_map/ppermute | solution.py:198
  215.9 5.2 %copy-start.12 = (f32[64,2]{0,1:T(2,128)S(1)}, f32[64,2]{0,1:T(2,128)}, u32[]{:S(2)}) copy-start(f32[64,2]{0,1:T(2,128)} %param.9) | copy-start | bytes 1540
  216.9 4.2 %copy-start.11 = (s32[64,2]{0,1:T(2,128)S(1)}, s32[64,2]{0,1:T(2,128)}, u32[]{:S(2)}) copy-start(s32[64,2]{0,1:T(2,128)} %param.8) | copy-start | bytes 1540

commit v7 on v6

--- a/solution.py
+++ b/solution.py
@@ -157,7 +157,7 @@
         out_ref[...] = total.astype(out_ref.dtype)
 
 
-def in_kernel(rows_ref, next_ref, own_ref, got_ref, keep_ref, away_ref):
+def in_kernel(factor, rows_ref, next_ref, own_ref, got_ref, keep_ref, away_ref):
     width, hs = keep_ref.shape[0], keep_ref.shape[1] // 2
     half = own_ref.shape[1] // 2
     rows, following = rows_ref[:, :width], next_ref[:, :width]
@@ -167,17 +167,27 @@
             there = slice((step + side) * hs, (step + side + 1) * hs)
             total = dot(rows, own_ref[:, here], FIRST)
             total += dot(following, got_ref[:, there], FIRST)
-            out_ref[:, side * hs : (side + 1) * hs] = total.astype(out_ref.dtype)
-
-
-def home_kernel(ids_ref, weight_ref, back_ref, mixed_ref, grad_ref):
-    tok_rows, width = mixed_ref.shape
-    place = jnp.where(hits(ids_ref), 1.0, 0.0).astype(BF)
+            out_ref[:, side * hs : (side + 1) * hs] = (total * factor).astype(out_ref.dtype)
+
+
+def join_kernel(keep_ref, got_ref, *grad_refs):
+    total = keep_ref[...] + got_ref[...].astype(F32)
+    hs = grad_refs[0].shape[1]
+    for side, grad_ref in enumerate(grad_refs):
+        grad_ref[...] = total[:, side * hs : (side + 1) * hs]
+
+
+def place_kernel(ids_ref, weight_ref, place_ref, column_ref):
+    place_ref[...] = jnp.where(hits(ids_ref), 1.0, 0.0).astype(BF)
     row = pair(weight_ref)
     count = row.shape[1]
-    weight = jnp.broadcast_to(row, (count, count)).T[:, :1]
-    per = dot(place, back_ref[...], FIRST)
-    per_out = per[:, :width] * weight
+    column_ref[...] = jnp.broadcast_to(row, (count, count)).T
+
+
+def home_kernel(place_ref, weight_ref, back_ref, mixed_ref, grad_ref):
+    tok_rows, width = mixed_ref.shape
+    per = dot(place_ref[...], back_ref[...], FIRST)
+    per_out = per[:, :width] * weight_ref[:, :1]
     per_in = per[:, width:]
     mixed_ref[...] = per_out[:tok_rows] + per_out[tok_rows:]
     grad_ref[...] = per_in[:tok_rows] + per_in[tok_rows:]
@@ -226,12 +236,13 @@
     w_out = share(w_down[0].T)
     rows_next = swap_pair(rows, "c")
     (act_local,) = local(act_kernel, [((slots, units), BF)], rows, *w_out)
+    act_local, rows_next = lax.optimization_barrier((act_local, rows_next))
     act_part, act_round = sum_y(act_local)
 
     pre_other = swap_pair(pre_round, "zh")
     copies = (8, slots // 8)
     (hidden,) = local(hidden_kernel, [(copies + (units,), BF)], pre_part, pre_other)
-    hidden, act_round, rows_next = lax.optimization_barrier((hidden, act_round, rows_next))
+    hidden, act_round = lax.optimization_barrier((hidden, act_round))
     hidden = gather_y(hidden)
     act_other = swap_pair(act_round, "zh")
     (deltas,) = local(
@@ -254,20 +265,29 @@
     deltas, hidden, down_got = lax.optimization_barrier((deltas, hidden, down_got))
     deltas_got = to_next(deltas)
     (back,) = local(
-        back_kernel, [((slots, 2 * width), BF)], hidden, deltas, *w_in, *w_out, fetch=10
-    )
-    back, deltas_got = lax.optimization_barrier((back, deltas_got))
+        back_kernel, [((slots, 2 * width), BF)], hidden, deltas, *w_in, *w_out
+    )
+    back, deltas_got, ids, weight = lax.optimization_barrier((back, deltas_got, ids, weight))
+    count = TOP * tok_rows
+    place, column = local(
+        place_kernel, [((slots, count), BF), ((count, count), F32)], ids, weight
+    )
     back = swap(back.reshape(EXPERTS, CAP, 2 * width), OWN).reshape(slots, 2 * width)
+
+    factor = 1.0 / math.sqrt(8 * tok_rows)
+
+    def into(*refs):
+        in_kernel(factor, *refs)
 
     shape = (width, 2 * hs)
     in_keep, in_away = local(
-        in_kernel, [(shape, F32), (shape, BF)], rows, rows_next, deltas, deltas_got
-    )
-    factor = 1.0 / math.sqrt(8 * tok_rows)
-    in_grad = (in_keep + swap_pair(in_away, "zb").astype(F32)) * factor
-    gate_grad, up_grad = in_grad[:, :hs], in_grad[:, hs:]
+        into, [(shape, F32), (shape, BF)], rows, rows_next, deltas, deltas_got
+    )
+    gate_grad, up_grad = local(
+        join_kernel, [((width, hs), F32)] * 2, in_keep, swap_pair(in_away, "zb")
+    )
     down_grad = (down_keep + down_got.astype(F32)) * factor
-    mixed, tokens_grad = local(home_kernel, [((tok_rows, width), F32)] * 2, ids, weight, back)
+    mixed, tokens_grad = local(home_kernel, [((tok_rows, width), F32)] * 2, place, column, back)
     return (mixed, tokens_grad, gate_grad[None], up_grad[None], down_grad.T[None])
 
 

time: 225 us -> 219 us (0.973)
  waiting for transfers between devices: 67.9 us -> 61.6 us
  starting transfers between devices: 135 us -> 138 us
    all_to_all x6, waiting for transfers between devices: 23.9 us -> 19.9 us  [swap(): return lax.all_to_all(value, axis, split_axis=0, concat_axis=0, tiled=True)]
    all_to_all x6, starting transfers between devices: 60.1 us -> 63.7 us  [swap(): return lax.all_to_all(value, axis, split_axis=0, concat_axis=0, tiled=True)]
    pallas_call x11 -> x13, Pallas kernels: 14.2 us -> 12.8 us  [local(): pl.pallas_call(fetching if fetch else kernel, out_shape=[jax.ShapeDtypeSt...]
  transfers between devices with their start and end apart: 19 -> 19, of which waited for: 14 -> 12; matrix products, arithmetic and copies ran while one was open for 1% -> 1% of each run, Pallas kernels for 4% -> 3%
where the time goes in v7:
time: 219 us; the launch traced here: 217 us
  starting transfers between devices  138 us (63%)
  waiting for transfers between devices  61.6 us (28%)
  Pallas kernels  12.8 us (6%)
    ppermute x13, starting transfers between devices, swap_pair(): return lax.ppermute(value, axis, [(0, 1), (1, 0)])  74 us
    all_to_all x6, starting transfers between devices, swap(): return lax.all_to_all(value, axis, split_axis=0, concat_axis=0, tiled=True)  63.7 us
    ppermute x13, waiting for transfers between devices, swap_pair(): return lax.ppermute(value, axis, [(0, 1), (1, 0)])  41.7 us
    all_to_all x6, waiting for transfers between devices, swap(): return lax.all_to_all(value, axis, split_axis=0, concat_axis=0, tiled=True)  19.9 us
    pallas_call x13, Pallas kernels, local(): pl.pallas_call(fetching if fetch else kernel, out_shape=[jax.ShapeDtypeSt...  12.8 us
  transfers between devices with their start and end apart: 19, of which 12 were waited for; matrix products, arithmetic and copies ran while one was open for 1% of the time, Pallas kernels for 3%

profile of v7, /device:TPU:1, one launch (start us, length us, event | category | flops | bytes accessed | tf_op | source)
XLA Modules:
  0.0 216.8 jit_solution(2144064975659339985)
XLA Ops:
  0.6 2.2 %shard_map.110 = bf16[256,896]{1,0:T(8,128)(2,1)} custom-call(s32[2,64]{1,0:T(2,128)} %bitcast.37, f32[2,64]{1,0:T(2,128)} %bitcast.39, bf16[64,448]{1,0:T(8,128)(2,1)} %refs_2_.1, bf16[64,448]{1,0:T(8,128)(2,1)} %refs_3_.1), custom_call_target="tpu_custom_call" | custom-call | flops 2000000000 | bytes 1148928 | tf_op jit(solution)/shard_map/pallas_call | solution.py:48
  2.9 0.0 copy-start.20
  2.9 0.0 copy-start.21
  2.9 17.2 %all-to-all-start = ((bf16[16,16,896]{2,1,0:T(8,128)(2,1)}), bf16[16,16,896]{2,1,0:T(8,128)(2,1)S(1)}, u32[]{:S(2)}, u32[]{:S(2)}) async-start(bf16[16,16,896]{2,1,0:T(8,128)(2,1)} %bitcast.41), calls=%async_computation | async-start | bytes 917504 | tf_op jit(solution)/shard_map/all_to_all | solution.py:197
  20.1 4.0 %collective-permute-start.1 = (bf16[448,512]{1,0:T(8,128)(2,1)S(1)}, bf16[448,512]{1,0:T(8,128)(2,1)S(1)}, u32[]{:S(2)}, u32[]{:S(2)}) collective-permute-start(bf16[448,512]{1,0:T(8,128)(2,1)S(1)} %pad_maximum_fusion.1.refs_0_), channel_id=1, source_target_pairs={{0,2},{2,0},{1,3},{3,1},{4,6},{6,4},{5,7},{7,5},{8,10},{10,8},{9,1... | collective-permute-start | bytes 1376264 | tf_op jit(solution)/shard_map/ppermute | solution.py:208
  24.1 3.1 %collective-permute-start = (bf16[448,512]{1,0:T(8,128)(2,1)S(1)}, bf16[448,512]{1,0:T(8,128)(2,1)S(1)}, u32[]{:S(2)}, u32[]{:S(2)}) collective-permute-start(bf16[448,512]{1,0:T(8,128)(2,1)S(1)} %pad_maximum_fusion.1.refs_0_), channel_id=1, source_target_pairs={{0,1},{1,0},{2,3},{3,2},{4,5},{5,4},{6,7},{7,6},{8,9},{9,8},{10,11... | collective-permute-start | bytes 1376264 | tf_op jit(solution)/shard_map/ppermute | solution.py:208
  27.3 10.0 %collective-permute-done.1.refs_2_ = bf16[448,512]{1,0:T(8,128)(2,1)S(1)} collective-permute-done((bf16[448,512]{1,0:T(8,128)(2,1)S(1)}, bf16[448,512]{1,0:T(8,128)(2,1)S(1)}, u32[]{:S(2)}, u32[]{:S(2)}) %collective-permute-start.1) | collective-permute-done | bytes 458784 | tf_op jit(solution)/shard_map/ppermute | solution.py:208
  37.3 3.3 %collective-permute-start.2 = (bf16[448,512]{1,0:T(8,128)(2,1)S(1)}, bf16[448,512]{1,0:T(8,128)(2,1)S(1)}, u32[]{:S(2)}, u32[]{:S(2)}) collective-permute-start(bf16[448,512]{1,0:T(8,128)(2,1)S(1)} %collective-permute-done.1.refs_2_), channel_id=1, source_target_pairs={{0,1},{1,0},{2,3},{3,2},{4,5},{5,4},{6,7},{7,6},{8,9},{9,8},{10,11... | collective-permute-start | bytes 1376264 | tf_op jit(solution)/shard_map/ppermute | solution.py:208
  40.5 0.0 collective-permute-done.refs_1_
  40.5 0.0 copy-start.2
  40.5 1.4 collective-permute-done.2.refs_3_
  42.0 1.6 all-to-all-done
  43.5 1.7 shard_map.111
  45.2 0.0 copy-done.2
  45.2 7.0 %all-to-all-start.1 = ((bf16[8,32,2048]{2,1,0:T(8,128)(2,1)}), bf16[8,32,2048]{2,1,0:T(8,128)(2,1)S(1)}, u32[]{:S(2)}, u32[]{:S(2)}) async-start(bf16[8,32,2048]{2,1,0:T(8,128)(2,1)} %bitcast.6), calls=%async_computation.1 | async-start | bytes 2097152 | tf_op jit(solution)/shard_map/all_to_all | solution.py:197
  52.2 6.5 %collective-permute-start.5 = (bf16[448,256]{1,0:T(8,128)(2,1)S(1)}, bf16[448,256]{1,0:T(8,128)(2,1)S(1)}, u32[]{:S(2)}, u32[]{:S(2)}) collective-permute-start(bf16[448,256]{1,0:T(8,128)(2,1)S(1)} %bitcast.33), channel_id=1, source_target_pairs={{0,2},{2,0},{1,3},{3,1},{4,6},{6,4},{5,7},{7,5},{8,10},{10,8},{9,1... | collective-permute-start | bytes 688136 | tf_op jit(solution)/shard_map/ppermute | solution.py:208
  58.8 3.2 %collective-permute-start.7 = (bf16[256,896]{1,0:T(8,128)(2,1)S(1)}, bf16[256,896]{1,0:T(8,128)(2,1)S(1)}, u32[]{:S(2)}, u32[]{:S(2)}) collective-permute-start(bf16[256,896]{1,0:T(8,128)(2,1)S(1)} %bitcast.28), channel_id=1, source_target_pairs={{0,1},{1,0},{2,3},{3,2},{4,5},{5,4},{6,7},{7,6},{8,9},{9,8},{10,11... | collective-permute-start | bytes 1376264 | tf_op jit(solution)/shard_map/ppermute | solution.py:208
  61.9 1.9 collective-permute-start.4
  63.9 0.0 collective-permute-done.5.refs_2_.refs_6_
  63.9 4.0 %collective-permute-start.6 = (bf16[448,256]{1,0:T(8,128)(2,1)S(1)}, bf16[448,256]{1,0:T(8,128)(2,1)S(1)}, u32[]{:S(2)}, u32[]{:S(2)}) collective-permute-start(bf16[448,256]{1,0:T(8,128)(2,1)S(1)} %collective-permute-done.5.refs_2_.refs_6_), channel_id=1, source_target_pairs={{0,1},{1,0},{2,3},{3,2},{4,5},{5,4},{6,7},{7,6},{8,9},{9,8},{10,11... | collective-permute-start | bytes 688136 | tf_op jit(solution)/shard_map/ppermute | solution.py:208
  67.9 0.0 collective-permute-done.4.refs_1_.refs_5_
  67.9 1.1 collective-permute-done.6.refs_3_.refs_7_
  69.0 1.3 shard_map.113
  70.3 0.0 collective-permute-done.7.next_ref.refs_1_
  70.3 0.0 copy-start.6
  70.3 7.0 %all-to-all-done.1.got_ref = bf16[8,32,2048]{2,1,0:T(8,128)(2,1)S(1)} async-done(((bf16[8,32,2048]{2,1,0:T(8,128)(2,1)}), bf16[8,32,2048]{2,1,0:T(8,128)(2,1)S(1)}, u32[]{:S(2)}, u32[]{:S(2)}) %all-to-all-start.1) | async-done | bytes 1048608 | tf_op jit(solution)/shard_map/all_to_all | solution.py:197
  77.3 3.5 %all-to-all-start.2 = ((bf16[8,32,1024]{2,1,0:T(8,128)(2,1)}), bf16[8,32,1024]{2,1,0:T(8,128)(2,1)S(1)}, u32[]{:S(2)}, u32[]{:S(2)}) async-start(bf16[8,32,1024]{2,1,0:T(8,128)(2,1)} %bitcast.10), calls=%async_computation.2 | async-start | bytes 1048576 | tf_op jit(solution)/shard_map/all_to_all | solution.py:197
  80.8 0.1 shard_map.112
  81.0 0.7 copy-done.18
  81.7 17.8 %collective-permute-start.3 = (bf16[32,2048]{1,0:T(8,128)(2,1)S(1)}, bf16[32,2048]{1,0:T(8,128)(2,1)S(1)}, u32[]{:S(2)}, u32[]{:S(2)}) collective-permute-start(bf16[32,2048]{1,0:T(8,128)(2,1)S(1)} %get-tuple-element.41), channel_id=1, source_target_pairs={{0,64},{64,0},{1,65},{65,1},{2,66},{66,2},{3,67},{67,3},{4,68},{68... | collective-permute-start | bytes 393224 | tf_op jit(solution)/shard_map/ppermute | solution.py:208
  99.4 0.0 all-to-all-done.2.got_ref
  99.4 0.1 shard_map.114
  99.5 2.3 %collective-permute-done.3.other_ref = bf16[32,2048]{1,0:T(8,128)(2,1)S(1)} collective-permute-done((bf16[32,2048]{1,0:T(8,128)(2,1)S(1)}, bf16[32,2048]{1,0:T(8,128)(2,1)S(1)}, u32[]{:S(2)}, u32[]{:S(2)}) %collective-permute-start.3) | collective-permute-done | bytes 131104 | tf_op jit(solution)/shard_map/ppermute | solution.py:208
  101.9 0.9 shard_map.115
  102.7 6.6 %all-to-all-start.4 = ((bf16[8,32,1024]{2,1,0:T(8,128)(2,1)}), bf16[8,32,1024]{2,1,0:T(8,128)(2,1)S(1)}, u32[]{:S(2)}, u32[]{:S(2)}) async-start(bf16[8,32,1024]{2,1,0:T(8,128)(2,1)} %shard_map.115), calls=%async_computation.4 | async-start | bytes 1048576 | tf_op jit(solution)/shard_map/all_to_all | solution.py:197
  109.3 13.7 %collective-permute-start.8 = (bf16[32,1024]{1,0:T(8,128)(2,1)S(1)}, bf16[32,1024]{1,0:T(8,128)(2,1)S(1)}, u32[]{:S(2)}, u32[]{:S(2)}) collective-permute-start(bf16[32,1024]{1,0:T(8,128)(2,1)S(1)} %get-tuple-element.47), channel_id=1, source_target_pairs={{0,64},{64,0},{1,65},{65,1},{2,66},{66,2},{3,67},{67,3},{4,68},{68... | collective-permute-start | bytes 196616 | tf_op jit(solution)/shard_map/ppermute | solution.py:208
  123.0 2.7 %collective-permute-done.8.act_other_ref = bf16[32,1024]{1,0:T(8,128)(2,1)S(1)} collective-permute-done((bf16[32,1024]{1,0:T(8,128)(2,1)S(1)}, bf16[32,1024]{1,0:T(8,128)(2,1)S(1)}, u32[]{:S(2)}, u32[]{:S(2)}) %collective-permute-start.8) | collective-permute-done | bytes 65568 | tf_op jit(solution)/shard_map/ppermute | solution.py:208
  125.7 1.1 shard_map.116
  126.8 0.0 all-to-all-done.4
  126.8 6.6 %all-to-all-start.3 = ((bf16[8,32,2048]{2,1,0:T(8,128)(2,1)}), bf16[8,32,2048]{2,1,0:T(8,128)(2,1)S(1)}, u32[]{:S(2)}, u32[]{:S(2)}) async-start(bf16[8,32,2048]{2,1,0:T(8,128)(2,1)} %shard_map.116), calls=%async_computation.3 | async-start | bytes 2097152 | tf_op jit(solution)/shard_map/all_to_all | solution.py:197
  133.4 6.2 %collective-permute-start.9 = (bf16[256,512]{1,0:T(8,128)(2,1)S(1)}, bf16[256,512]{1,0:T(8,128)(2,1)S(1)}, u32[]{:S(2)}, u32[]{:S(2)}) collective-permute-start(bf16[256,512]{1,0:T(8,128)(2,1)S(1)} %pad_maximum_fusion.2), channel_id=1, source_target_pairs={{0,1},{1,0},{2,3},{3,2},{4,5},{5,4},{6,7},{7,6},{8,9},{9,8},{10,11... | collective-permute-start | bytes 786440 | tf_op jit(solution)/shard_map/ppermute | solution.py:208
  139.7 1.1 collective-permute-done.9.got_ref
  140.8 0.7 shard_map.117
  141.5 2.1 collective-permute-start.10
  143.7 6.7 %collective-permute-done.10 = bf16[448,256]{1,0:T(8,128)(2,1)} collective-permute-done((bf16[448,256]{1,0:T(8,128)(2,1)S(1)}, bf16[448,256]{1,0:T(8,128)(2,1)}, u32[]{:S(2)}, u32[]{:S(2)}) %collective-permute-start.10) | collective-permute-done | bytes 229408 | tf_op jit(solution)/shard_map/ppermute | solution.py:208
  150.3 8.6 %all-to-all-done.3 = bf16[8,32,2048]{2,1,0:T(8,128)(2,1)S(1)} async-done(((bf16[8,32,2048]{2,1,0:T(8,128)(2,1)}), bf16[8,32,2048]{2,1,0:T(8,128)(2,1)S(1)}, u32[]{:S(2)}, u32[]{:S(2)}) %all-to-all-start.3) | async-done | bytes 1048608 | tf_op jit(solution)/shard_map/all_to_all | solution.py:197
  159.0 0.0 copy-start.1
  159.0 0.0 copy-start.3
  159.1 0.1 pad_maximum_fusion
  159.1 6.2 %collective-permute-start.11 = (bf16[256,1024]{1,0:T(8,128)(2,1)S(1)}, bf16[256,1024]{1,0:T(8,128)(2,1)S(1)}, u32[]{:S(2)}, u32[]{:S(2)}) collective-permute-start(bf16[256,1024]{1,0:T(8,128)(2,1)S(1)} %pad_maximum_fusion), channel_id=1, source_target_pairs={{0,1},{1,0},{2,3},{3,2},{4,5},{5,4},{6,7},{7,6},{8,9},{9,8},{10,11... | collective-permute-start | bytes 1572872 | tf_op jit(solution)/shard_map/ppermute | solution.py:208
  165.4 0.9 copy-done.15
  166.3 1.8 shard_map.118
  168.2 0.0 collective-permute-done.11.refs_3_
  168.2 22.9 %all-to-all-start.5 = ((bf16[16,16,896]{2,1,0:T(8,128)(2,1)}), bf16[16,16,896]{2,1,0:T(8,128)(2,1)S(1)}, u32[]{:S(2)}, u32[]{:S(2)}) async-start(bf16[16,16,896]{2,1,0:T(8,128)(2,1)} %bitcast.13), calls=%async_computation.5 | async-start | bytes 917504 | tf_op jit(solution)/shard_map/all_to_all | solution.py:197
  191.1 0.7 shard_map.121
  191.8 1.9 collective-permute-start.12
  193.7 0.0 copy-start.16
  193.8 0.0 copy-start.17
  193.8 1.8 multiply_bitcast_fusion
  195.5 0.2 shard_map.119
  195.7 16.4 %collective-permute-done.12.got_ref = bf16[448,512]{1,0:T(8,128)(2,1)S(1)} collective-permute-done((bf16[448,512]{1,0:T(8,128)(2,1)S(1)}, bf16[448,512]{1,0:T(8,128)(2,1)S(1)}, u32[]{:S(2)}, u32[]{:S(2)}) %collective-permute-start.12) | collective-permute-done | bytes 458784 | tf_op jit(solution)/shard_map/ppermute | solution.py:208
  212.1 1.0 shard_map.122
  213.1 2.7 %all-to-all-done.5 = bf16[16,16,896]{2,1,0:T(8,128)(2,1)S(1)} async-done(((bf16[16,16,896]{2,1,0:T(8,128)(2,1)}), bf16[16,16,896]{2,1,0:T(8,128)(2,1)S(1)}, u32[]{:S(2)}, u32[]{:S(2)}) %all-to-all-start.5) | async-done | bytes 458784 | tf_op jit(solution)/shard_map/all_to_all | solution.py:197
  215.8 1.0 shard_map.120
  (37 shorter events, 0.2 us)
Async XLA Ops:
  2.9 17.2 %copy-start.20 = (bf16[1,448,256]{2,1,0:T(8,128)(2,1)S(1)}, bf16[1,448,256]{2,1,0:T(8,128)(2,1)}, u32[]{:S(2)}) copy-start(bf16[1,448,256]{2,1,0:T(8,128)(2,1)} %param.12) | copy-start | bytes 688132
  2.9 17.2 %copy-start.21 = (bf16[1,448,256]{2,1,0:T(8,128)(2,1)S(1)}, bf16[1,448,256]{2,1,0:T(8,128)(2,1)}, u32[]{:S(2)}) copy-start(bf16[1,448,256]{2,1,0:T(8,128)(2,1)} %param.11) | copy-start | bytes 688132
  2.9 40.6 %all-to-all-start = ((bf16[16,16,896]{2,1,0:T(8,128)(2,1)}), bf16[16,16,896]{2,1,0:T(8,128)(2,1)S(1)}, u32[]{:S(2)}, u32[]{:S(2)}) async-start(bf16[16,16,896]{2,1,0:T(8,128)(2,1)} %bitcast.41), calls=%async_computation | async-start | bytes 917504 | tf_op jit(solution)/shard_map/all_to_all | solution.py:197
  20.1 17.1 %collective-permute-start.1 = (bf16[448,512]{1,0:T(8,128)(2,1)S(1)}, bf16[448,512]{1,0:T(8,128)(2,1)S(1)}, u32[]{:S(2)}, u32[]{:S(2)}) collective-permute-start(bf16[448,512]{1,0:T(8,128)(2,1)S(1)} %pad_maximum_fusion.1.refs_0_), channel_id=1, source_target_pairs={{0,2},{2,0},{1,3},{3,1},{4,6},{6,4},{5,7},{7,5},{8,10},{10,8},{9,1... | collective-permute-start | bytes 1376264 | tf_op jit(solution)/shard_map/ppermute | solution.py:208
  24.1 16.4 %collective-permute-start = (bf16[448,512]{1,0:T(8,128)(2,1)S(1)}, bf16[448,512]{1,0:T(8,128)(2,1)S(1)}, u32[]{:S(2)}, u32[]{:S(2)}) collective-permute-start(bf16[448,512]{1,0:T(8,128)(2,1)S(1)} %pad_maximum_fusion.1.refs_0_), channel_id=1, source_target_pairs={{0,1},{1,0},{2,3},{3,2},{4,5},{5,4},{6,7},{7,6},{8,9},{9,8},{10,11... | collective-permute-start | bytes 1376264 | tf_op jit(solution)/shard_map/ppermute | solution.py:208
  37.3 8.0 %copy-start = (bf16[448,512]{1,0:T(8,128)(2,1)}, bf16[448,512]{1,0:T(8,128)(2,1)S(1)}, u32[]{:S(2)}) copy-start(bf16[448,512]{1,0:T(8,128)(2,1)S(1)} %collective-permute-done.1.refs_2_) | copy-start | bytes 1376260
  37.3 4.7 %collective-permute-start.2 = (bf16[448,512]{1,0:T(8,128)(2,1)S(1)}, bf16[448,512]{1,0:T(8,128)(2,1)S(1)}, u32[]{:S(2)}, u32[]{:S(2)}) collective-permute-start(bf16[448,512]{1,0:T(8,128)(2,1)S(1)} %collective-permute-done.1.refs_2_), channel_id=1, source_target_pairs={{0,1},{1,0},{2,3},{3,2},{4,5},{5,4},{6,7},{7,6},{8,9},{9,8},{10,11... | collective-permute-start | bytes 1376264 | tf_op jit(solution)/shard_map/ppermute | solution.py:208
  40.5 4.7 %copy-start.2 = (bf16[448,512]{1,0:T(8,128)(2,1)}, bf16[448,512]{1,0:T(8,128)(2,1)S(1)}, u32[]{:S(2)}) copy-start(bf16[448,512]{1,0:T(8,128)(2,1)S(1)} %collective-permute-done.refs_1_) | copy-start | bytes 1376260
  41.9 3.3 %copy-start.4 = (bf16[448,512]{1,0:T(8,128)(2,1)}, bf16[448,512]{1,0:T(8,128)(2,1)S(1)}, u32[]{:S(2)}) copy-start(bf16[448,512]{1,0:T(8,128)(2,1)S(1)} %collective-permute-done.2.refs_3_) | copy-start | bytes 1376260
  45.2 7.0 %copy-start.8 = (bf16[1,256,448]{1,2,0:T(8,128)(2,1)S(1)}, bf16[1,256,448]{1,2,0:T(8,128)(2,1)}, u32[]{:S(2)}) copy-start(bf16[1,256,448]{1,2,0:T(8,128)(2,1)} %param.13) | copy-start | bytes 688132
  45.2 32.1 %all-to-all-start.1 = ((bf16[8,32,2048]{2,1,0:T(8,128)(2,1)}), bf16[8,32,2048]{2,1,0:T(8,128)(2,1)S(1)}, u32[]{:S(2)}, u32[]{:S(2)}) async-start(bf16[8,32,2048]{2,1,0:T(8,128)(2,1)} %bitcast.6), calls=%async_computation.1 | async-start | bytes 2097152 | tf_op jit(solution)/shard_map/all_to_all | solution.py:197
  52.2 11.6 %collective-permute-start.5 = (bf16[448,256]{1,0:T(8,128)(2,1)S(1)}, bf16[448,256]{1,0:T(8,128)(2,1)S(1)}, u32[]{:S(2)}, u32[]{:S(2)}) collective-permute-start(bf16[448,256]{1,0:T(8,128)(2,1)S(1)} %bitcast.33), channel_id=1, source_target_pairs={{0,2},{2,0},{1,3},{3,1},{4,6},{6,4},{5,7},{7,5},{8,10},{10,8},{9,1... | collective-permute-start | bytes 688136 | tf_op jit(solution)/shard_map/ppermute | solution.py:208
  58.8 11.5 %collective-permute-start.7 = (bf16[256,896]{1,0:T(8,128)(2,1)S(1)}, bf16[256,896]{1,0:T(8,128)(2,1)S(1)}, u32[]{:S(2)}, u32[]{:S(2)}) collective-permute-start(bf16[256,896]{1,0:T(8,128)(2,1)S(1)} %bitcast.28), channel_id=1, source_target_pairs={{0,1},{1,0},{2,3},{3,2},{4,5},{5,4},{6,7},{7,6},{8,9},{9,8},{10,11... | collective-permute-start | bytes 1376264 | tf_op jit(solution)/shard_map/ppermute | solution.py:208
  61.9 6.0 %collective-permute-start.4 = (bf16[448,256]{1,0:T(8,128)(2,1)S(1)}, bf16[448,256]{1,0:T(8,128)(2,1)S(1)}, u32[]{:S(2)}, u32[]{:S(2)}) collective-permute-start(bf16[448,256]{1,0:T(8,128)(2,1)S(1)} %bitcast.34), channel_id=1, source_target_pairs={{0,1},{1,0},{2,3},{3,2},{4,5},{5,4},{6,7},{7,6},{8,9},{9,8},{10,11... | collective-permute-start | bytes 688136 | tf_op jit(solution)/shard_map/ppermute | solution.py:208
  63.9 6.4 %copy-start.10 = (bf16[448,256]{1,0:T(8,128)(2,1)}, bf16[448,256]{1,0:T(8,128)(2,1)S(1)}, u32[]{:S(2)}) copy-start(bf16[448,256]{1,0:T(8,128)(2,1)S(1)} %collective-permute-done.5.refs_2_.refs_6_) | copy-start | bytes 688132
  63.9 5.1 %collective-permute-start.6 = (bf16[448,256]{1,0:T(8,128)(2,1)S(1)}, bf16[448,256]{1,0:T(8,128)(2,1)S(1)}, u32[]{:S(2)}, u32[]{:S(2)}) collective-permute-start(bf16[448,256]{1,0:T(8,128)(2,1)S(1)} %collective-permute-done.5.refs_2_.refs_6_), channel_id=1, source_target_pairs={{0,1},{1,0},{2,3},{3,2},{4,5},{5,4},{6,7},{7,6},{8,9},{9,8},{10,11... | collective-permute-start | bytes 688136 | tf_op jit(solution)/shard_map/ppermute | solution.py:208
  67.9 2.4 %copy-start.12 = (bf16[448,256]{1,0:T(8,128)(2,1)}, bf16[448,256]{1,0:T(8,128)(2,1)S(1)}, u32[]{:S(2)}) copy-start(bf16[448,256]{1,0:T(8,128)(2,1)S(1)} %collective-permute-done.4.refs_1_.refs_5_) | copy-start | bytes 688132
  69.0 1.3 copy-start.14
  70.3 70.5 %copy-start.6 = (bf16[256,896]{1,0:T(8,128)(2,1)}, bf16[256,896]{1,0:T(8,128)(2,1)S(1)}, u32[]{:S(2)}) copy-start(bf16[256,896]{1,0:T(8,128)(2,1)S(1)} %collective-permute-done.7.next_ref.refs_1_) | copy-start | bytes 1376260
  77.3 22.1 %all-to-all-start.2 = ((bf16[8,32,1024]{2,1,0:T(8,128)(2,1)}), bf16[8,32,1024]{2,1,0:T(8,128)(2,1)S(1)}, u32[]{:S(2)}, u32[]{:S(2)}) async-start(bf16[8,32,1024]{2,1,0:T(8,128)(2,1)} %bitcast.10), calls=%async_computation.2 | async-start | bytes 1048576 | tf_op jit(solution)/shard_map/all_to_all | solution.py:197
  81.0 0.7 copy-start.18
  81.7 20.2 %copy-start.19 = (f32[32,2048]{1,0:T(8,128)S(1)}, f32[32,2048]{1,0:T(8,128)}, u32[]{:S(2)}) copy-start(f32[32,2048]{1,0:T(8,128)} %copy-done.18) | copy-start | bytes 786436
  81.7 20.2 %collective-permute-start.3 = (bf16[32,2048]{1,0:T(8,128)(2,1)S(1)}, bf16[32,2048]{1,0:T(8,128)(2,1)S(1)}, u32[]{:S(2)}, u32[]{:S(2)}) collective-permute-start(bf16[32,2048]{1,0:T(8,128)(2,1)S(1)} %get-tuple-element.41), channel_id=1, source_target_pairs={{0,64},{64,0},{1,65},{65,1},{2,66},{66,2},{3,67},{67,3},{4,68},{68... | collective-permute-start | bytes 393224 | tf_op jit(solution)/shard_map/ppermute | solution.py:208
  102.7 24.1 %all-to-all-start.4 = ((bf16[8,32,1024]{2,1,0:T(8,128)(2,1)}), bf16[8,32,1024]{2,1,0:T(8,128)(2,1)S(1)}, u32[]{:S(2)}, u32[]{:S(2)}) async-start(bf16[8,32,1024]{2,1,0:T(8,128)(2,1)} %shard_map.115), calls=%async_computation.4 | async-start | bytes 1048576 | tf_op jit(solution)/shard_map/all_to_all | solution.py:197
  109.3 16.4 %collective-permute-start.8 = (bf16[32,1024]{1,0:T(8,128)(2,1)S(1)}, bf16[32,1024]{1,0:T(8,128)(2,1)S(1)}, u32[]{:S(2)}, u32[]{:S(2)}) collective-permute-start(bf16[32,1024]{1,0:T(8,128)(2,1)S(1)} %get-tuple-element.47), channel_id=1, source_target_pairs={{0,64},{64,0},{1,65},{65,1},{2,66},{66,2},{3,67},{67,3},{4,68},{68... | collective-permute-start | bytes 196616 | tf_op jit(solution)/shard_map/ppermute | solution.py:208
  126.8 32.1 %all-to-all-start.3 = ((bf16[8,32,2048]{2,1,0:T(8,128)(2,1)}), bf16[8,32,2048]{2,1,0:T(8,128)(2,1)S(1)}, u32[]{:S(2)}, u32[]{:S(2)}) async-start(bf16[8,32,2048]{2,1,0:T(8,128)(2,1)} %shard_map.116), calls=%async_computation.3 | async-start | bytes 2097152 | tf_op jit(solution)/shard_map/all_to_all | solution.py:197
  133.4 7.4 %collective-permute-start.9 = (bf16[256,512]{1,0:T(8,128)(2,1)S(1)}, bf16[256,512]{1,0:T(8,128)(2,1)S(1)}, u32[]{:S(2)}, u32[]{:S(2)}) collective-permute-start(bf16[256,512]{1,0:T(8,128)(2,1)S(1)} %pad_maximum_fusion.2), channel_id=1, source_target_pairs={{0,1},{1,0},{2,3},{3,2},{4,5},{5,4},{6,7},{7,6},{8,9},{9,8},{10,11... | collective-permute-start | bytes 786440 | tf_op jit(solution)/shard_map/ppermute | solution.py:208
  141.5 8.8 %collective-permute-start.10 = (bf16[448,256]{1,0:T(8,128)(2,1)S(1)}, bf16[448,256]{1,0:T(8,128)(2,1)}, u32[]{:S(2)}, u32[]{:S(2)}) collective-permute-start(bf16[448,256]{1,0:T(8,128)(2,1)S(1)} %get-tuple-element.50), channel_id=1, source_target_pairs={{0,2},{2,0},{1,3},{3,1},{4,6},{6,4},{5,7},{7,5},{8,10},{10,8},{9,1... | collective-permute-start | bytes 688136 | tf_op jit(solution)/shard_map/ppermute | solution.py:208
  159.0 6.3 %copy-start.5 = (bf16[448,512]{1,0:T(8,128)(2,1)S(1)}, bf16[448,512]{1,0:T(8,128)(2,1)}, u32[]{:S(2)}) copy-start(bf16[448,512]{1,0:T(8,128)(2,1)} %copy-done.4) | copy-start | bytes 1376260
  159.0 6.4 %copy-start.9 = (bf16[1,256,448]{1,2,0:T(8,128)(2,1)S(1)}, bf16[1,256,448]{1,2,0:T(8,128)(2,1)}, u32[]{:S(2)}) copy-start(bf16[1,256,448]{1,2,0:T(8,128)(2,1)} %param.13) | copy-start | bytes 688132
  159.0 6.4 %copy-start.11 = (bf16[448,256]{1,0:T(8,128)(2,1)S(1)}, bf16[448,256]{1,0:T(8,128)(2,1)}, u32[]{:S(2)}) copy-start(bf16[448,256]{1,0:T(8,128)(2,1)} %copy-done.10) | copy-start | bytes 688132
  159.0 6.4 %copy-start.13 = (bf16[448,256]{1,0:T(8,128)(2,1)S(1)}, bf16[448,256]{1,0:T(8,128)(2,1)}, u32[]{:S(2)}) copy-start(bf16[448,256]{1,0:T(8,128)(2,1)} %copy-done.12) | copy-start | bytes 688132
  159.0 6.3 %copy-start.1 = (bf16[448,512]{1,0:T(8,128)(2,1)S(1)}, bf16[448,512]{1,0:T(8,128)(2,1)}, u32[]{:S(2)}) copy-start(bf16[448,512]{1,0:T(8,128)(2,1)} %copy-done) | copy-start | bytes 1376260
  159.0 6.3 %copy-start.3 = (bf16[448,512]{1,0:T(8,128)(2,1)S(1)}, bf16[448,512]{1,0:T(8,128)(2,1)}, u32[]{:S(2)}) copy-start(bf16[448,512]{1,0:T(8,128)(2,1)} %copy-done.2) | copy-start | bytes 1376260
  159.1 9.0 %collective-permute-start.11 = (bf16[256,1024]{1,0:T(8,128)(2,1)S(1)}, bf16[256,1024]{1,0:T(8,128)(2,1)S(1)}, u32[]{:S(2)}, u32[]{:S(2)}) collective-permute-start(bf16[256,1024]{1,0:T(8,128)(2,1)S(1)} %pad_maximum_fusion), channel_id=1, source_target_pairs={{0,1},{1,0},{2,3},{3,2},{4,5},{5,4},{6,7},{7,6},{8,9},{9,8},{10,11... | collective-permute-start | bytes 1572872 | tf_op jit(solution)/shard_map/ppermute | solution.py:208
  165.4 0.9 copy-start.15
  168.2 23.0 %copy-start.7 = (bf16[256,896]{1,0:T(8,128)(2,1)S(1)}, bf16[256,896]{1,0:T(8,128)(2,1)}, u32[]{:S(2)}) copy-start(bf16[256,896]{1,0:T(8,128)(2,1)} %copy-done.6) | copy-start | bytes 1376260
  168.2 47.6 %all-to-all-start.5 = ((bf16[16,16,896]{2,1,0:T(8,128)(2,1)}), bf16[16,16,896]{2,1,0:T(8,128)(2,1)S(1)}, u32[]{:S(2)}, u32[]{:S(2)}) async-start(bf16[16,16,896]{2,1,0:T(8,128)(2,1)} %bitcast.13), calls=%async_computation.5 | async-start | bytes 917504 | tf_op jit(solution)/shard_map/all_to_all | solution.py:197
  191.8 20.3 %collective-permute-start.12 = (bf16[448,512]{1,0:T(8,128)(2,1)S(1)}, bf16[448,512]{1,0:T(8,128)(2,1)S(1)}, u32[]{:S(2)}, u32[]{:S(2)}) collective-permute-start(bf16[448,512]{1,0:T(8,128)(2,1)S(1)} %get-tuple-element.62), channel_id=1, source_target_pairs={{0,2},{2,0},{1,3},{3,1},{4,6},{6,4},{5,7},{7,5},{8,10},{10,8},{9,1... | collective-permute-start | bytes 1376264 | tf_op jit(solution)/shard_map/ppermute | solution.py:208
  193.7 1.8 copy-start.16
  193.8 1.8 copy-start.17

commit v8 on v7

--- a/solution.py
+++ b/solution.py
@@ -105,15 +105,13 @@
         out_ref[:, s * hs : (s + 1) * hs] = dot(rows, refs[s][...]).astype(BF)
 
 
-def sum_kernel(got_ref, sum_ref, round_ref):
-    total = jnp.sum(got_ref[...].astype(F32), axis=0)
-    sum_ref[...] = total
-    round_ref[...] = total.astype(BF)
+def sum_kernel(got_ref, sum_ref):
+    sum_ref[...] = jnp.sum(got_ref[...].astype(F32), axis=0).astype(BF)
 
 
 def hidden_kernel(part_ref, other_ref, hidden_ref):
     units = part_ref.shape[1] // 2
-    pre = part_ref[...] + other_ref[...].astype(F32)
+    pre = part_ref[...].astype(F32) + other_ref[...].astype(F32)
     gate_pre, up_pre = pre[:, :units], pre[:, units:]
     hidden = (gate_pre * jax.nn.sigmoid(gate_pre) * up_pre).astype(BF)
     hidden_ref[...] = jnp.broadcast_to(hidden[None], hidden_ref.shape)
@@ -121,8 +119,8 @@
 
 def delta_kernel(part_ref, other_ref, act_ref, act_other_ref, delta_ref):
     units = act_ref.shape[1]
-    pre = part_ref[...] + other_ref[...].astype(F32)
-    act_grad = act_ref[...] + act_other_ref[...].astype(F32)
+    pre = part_ref[...].astype(F32) + other_ref[...].astype(F32)
+    act_grad = act_ref[...].astype(F32) + act_other_ref[...].astype(F32)
     gate_pre, up_pre = pre[:, :units], pre[:, units:]
     sig = jax.nn.sigmoid(gate_pre)
     gate_delta = act_grad * up_pre * sig * (1.0 + gate_pre * (1.0 - sig))
@@ -200,8 +198,8 @@
 def sum_y(part):
     rows, cols = part.shape
     got = swap(part.reshape(8, rows // 8, cols), "y")
-    shape = (rows // 8, cols)
-    return local(sum_kernel, [(shape, F32), (shape, BF)], got)
+    (total,) = local(sum_kernel, [((rows // 8, cols), BF)], got)
+    return total
 
 
 def swap_pair(value, axis):
@@ -232,19 +230,19 @@
     w_in = share(jnp.concatenate([w_gate[0], w_up[0]], axis=1))
     (pre_local,) = local(pre_kernel, [((slots, 2 * units), BF)], rows, *w_in)
     pre_local, rows, w_down = lax.optimization_barrier((pre_local, rows, w_down))
-    pre_part, pre_round = sum_y(pre_local)
+    pre_part = sum_y(pre_local)
     w_out = share(w_down[0].T)
     rows_next = swap_pair(rows, "c")
     (act_local,) = local(act_kernel, [((slots, units), BF)], rows, *w_out)
     act_local, rows_next = lax.optimization_barrier((act_local, rows_next))
-    act_part, act_round = sum_y(act_local)
-
-    pre_other = swap_pair(pre_round, "zh")
+    act_part = sum_y(act_local)
+
+    pre_other = swap_pair(pre_part, "zh")
     copies = (8, slots // 8)
     (hidden,) = local(hidden_kernel, [(copies + (units,), BF)], pre_part, pre_other)
-    hidden, act_round = lax.optimization_barrier((hidden, act_round))
+    hidden, act_part = lax.optimization_barrier((hidden, act_part))
     hidden = gather_y(hidden)
-    act_other = swap_pair(act_round, "zh")
+    act_other = swap_pair(act_part, "zh")
     (deltas,) = local(
         delta_kernel, [(copies + (2 * units,), BF)], pre_part, pre_other, act_part, act_other
     )

time: 219 us -> 219 us (level)
  no operation moved by 1% of the time
where the time goes in v8:
time: 219 us; the launch traced here: 216 us
  starting transfers between devices  138 us (63%)
  waiting for transfers between devices  61.5 us (28%)
  Pallas kernels  12.9 us (6%)
    ppermute x13, starting transfers between devices, swap_pair(): return lax.ppermute(value, axis, [(0, 1), (1, 0)])  73.9 us
    all_to_all x6, starting transfers between devices, swap(): return lax.all_to_all(value, axis, split_axis=0, concat_axis=0, tiled=True)  63.7 us
    ppermute x13, waiting for transfers between devices, swap_pair(): return lax.ppermute(value, axis, [(0, 1), (1, 0)])  41.7 us
    all_to_all x6, waiting for transfers between devices, swap(): return lax.all_to_all(value, axis, split_axis=0, concat_axis=0, tiled=True)  19.8 us
    pallas_call x13, Pallas kernels, local(): pl.pallas_call(fetching if fetch else kernel, out_shape=[jax.ShapeDtypeSt...  12.9 us
  transfers between devices with their start and end apart: 19, of which 12 were waited for; matrix products, arithmetic and copies ran while one was open for 1% of the time, Pallas kernels for 3%

profile of v8, /device:TPU:1, one launch (start us, length us, event | category | flops | bytes accessed | tf_op | source)
XLA Modules:
  0.0 216.0 jit_solution(3307496589305582538)
XLA Ops:
  0.6 2.2 %shard_map.110 = bf16[256,896]{1,0:T(8,128)(2,1)} custom-call(s32[2,64]{1,0:T(2,128)} %bitcast.37, f32[2,64]{1,0:T(2,128)} %bitcast.39, bf16[64,448]{1,0:T(8,128)(2,1)} %refs_2_.1, bf16[64,448]{1,0:T(8,128)(2,1)} %refs_3_.1), custom_call_target="tpu_custom_call" | custom-call | flops 2000000000 | bytes 1148928 | tf_op jit(solution)/shard_map/pallas_call | solution.py:48
  2.9 0.0 copy-start.18
  2.9 0.0 copy-start.19
  2.9 17.2 %all-to-all-start = ((bf16[16,16,896]{2,1,0:T(8,128)(2,1)}), bf16[16,16,896]{2,1,0:T(8,128)(2,1)S(1)}, u32[]{:S(2)}, u32[]{:S(2)}) async-start(bf16[16,16,896]{2,1,0:T(8,128)(2,1)} %bitcast.41), calls=%async_computation | async-start | bytes 917504 | tf_op jit(solution)/shard_map/all_to_all | solution.py:195
  20.1 4.0 %collective-permute-start.1 = (bf16[448,512]{1,0:T(8,128)(2,1)S(1)}, bf16[448,512]{1,0:T(8,128)(2,1)S(1)}, u32[]{:S(2)}, u32[]{:S(2)}) collective-permute-start(bf16[448,512]{1,0:T(8,128)(2,1)S(1)} %pad_maximum_fusion.1.refs_0_), channel_id=1, source_target_pairs={{0,2},{2,0},{1,3},{3,1},{4,6},{6,4},{5,7},{7,5},{8,10},{10,8},{9,1... | collective-permute-start | bytes 1376264 | tf_op jit(solution)/shard_map/ppermute | solution.py:206
  24.1 3.1 %collective-permute-start = (bf16[448,512]{1,0:T(8,128)(2,1)S(1)}, bf16[448,512]{1,0:T(8,128)(2,1)S(1)}, u32[]{:S(2)}, u32[]{:S(2)}) collective-permute-start(bf16[448,512]{1,0:T(8,128)(2,1)S(1)} %pad_maximum_fusion.1.refs_0_), channel_id=1, source_target_pairs={{0,1},{1,0},{2,3},{3,2},{4,5},{5,4},{6,7},{7,6},{8,9},{9,8},{10,11... | collective-permute-start | bytes 1376264 | tf_op jit(solution)/shard_map/ppermute | solution.py:206
  27.3 10.0 %collective-permute-done.1.refs_2_ = bf16[448,512]{1,0:T(8,128)(2,1)S(1)} collective-permute-done((bf16[448,512]{1,0:T(8,128)(2,1)S(1)}, bf16[448,512]{1,0:T(8,128)(2,1)S(1)}, u32[]{:S(2)}, u32[]{:S(2)}) %collective-permute-start.1) | collective-permute-done | bytes 458784 | tf_op jit(solution)/shard_map/ppermute | solution.py:206
  37.3 3.3 %collective-permute-start.2 = (bf16[448,512]{1,0:T(8,128)(2,1)S(1)}, bf16[448,512]{1,0:T(8,128)(2,1)S(1)}, u32[]{:S(2)}, u32[]{:S(2)}) collective-permute-start(bf16[448,512]{1,0:T(8,128)(2,1)S(1)} %collective-permute-done.1.refs_2_), channel_id=1, source_target_pairs={{0,1},{1,0},{2,3},{3,2},{4,5},{5,4},{6,7},{7,6},{8,9},{9,8},{10,11... | collective-permute-start | bytes 1376264 | tf_op jit(solution)/shard_map/ppermute | solution.py:206
  40.5 0.0 collective-permute-done.refs_1_
  40.5 0.0 copy-start.2
  40.5 1.4 collective-permute-done.2.refs_3_
  42.0 1.6 all-to-all-done
  43.5 1.7 shard_map.111
  45.2 0.0 copy-done
  45.2 7.0 %all-to-all-start.1 = ((bf16[8,32,2048]{2,1,0:T(8,128)(2,1)}), bf16[8,32,2048]{2,1,0:T(8,128)(2,1)S(1)}, u32[]{:S(2)}, u32[]{:S(2)}) async-start(bf16[8,32,2048]{2,1,0:T(8,128)(2,1)} %bitcast.6), calls=%async_computation.1 | async-start | bytes 2097152 | tf_op jit(solution)/shard_map/all_to_all | solution.py:195
  52.2 6.5 %collective-permute-start.5 = (bf16[448,256]{1,0:T(8,128)(2,1)S(1)}, bf16[448,256]{1,0:T(8,128)(2,1)S(1)}, u32[]{:S(2)}, u32[]{:S(2)}) collective-permute-start(bf16[448,256]{1,0:T(8,128)(2,1)S(1)} %bitcast.33), channel_id=1, source_target_pairs={{0,2},{2,0},{1,3},{3,1},{4,6},{6,4},{5,7},{7,5},{8,10},{10,8},{9,1... | collective-permute-start | bytes 688136 | tf_op jit(solution)/shard_map/ppermute | solution.py:206
  58.7 3.2 %collective-permute-start.7 = (bf16[256,896]{1,0:T(8,128)(2,1)S(1)}, bf16[256,896]{1,0:T(8,128)(2,1)S(1)}, u32[]{:S(2)}, u32[]{:S(2)}) collective-permute-start(bf16[256,896]{1,0:T(8,128)(2,1)S(1)} %bitcast.28), channel_id=1, source_target_pairs={{0,1},{1,0},{2,3},{3,2},{4,5},{5,4},{6,7},{7,6},{8,9},{9,8},{10,11... | collective-permute-start | bytes 1376264 | tf_op jit(solution)/shard_map/ppermute | solution.py:206
  61.9 1.9 collective-permute-start.4
  63.8 0.0 collective-permute-done.5.refs_2_.refs_6_
  63.8 0.0 copy-start.10
  63.9 4.0 %collective-permute-start.6 = (bf16[448,256]{1,0:T(8,128)(2,1)S(1)}, bf16[448,256]{1,0:T(8,128)(2,1)S(1)}, u32[]{:S(2)}, u32[]{:S(2)}) collective-permute-start(bf16[448,256]{1,0:T(8,128)(2,1)S(1)} %collective-permute-done.5.refs_2_.refs_6_), channel_id=1, source_target_pairs={{0,1},{1,0},{2,3},{3,2},{4,5},{5,4},{6,7},{7,6},{8,9},{9,8},{10,11... | collective-permute-start | bytes 688136 | tf_op jit(solution)/shard_map/ppermute | solution.py:206
  67.9 0.0 collective-permute-done.4.refs_1_.refs_5_
  67.9 1.1 collective-permute-done.6.refs_3_.refs_7_
  69.0 1.3 shard_map.114
  70.3 0.0 collective-permute-done.7.next_ref.refs_1_
  70.3 0.0 copy-start.6
  70.3 7.0 %all-to-all-done.1.got_ref = bf16[8,32,2048]{2,1,0:T(8,128)(2,1)S(1)} async-done(((bf16[8,32,2048]{2,1,0:T(8,128)(2,1)}), bf16[8,32,2048]{2,1,0:T(8,128)(2,1)S(1)}, u32[]{:S(2)}, u32[]{:S(2)}) %all-to-all-start.1) | async-done | bytes 1048608 | tf_op jit(solution)/shard_map/all_to_all | solution.py:195
  77.3 3.5 %all-to-all-start.2 = ((bf16[8,32,1024]{2,1,0:T(8,128)(2,1)}), bf16[8,32,1024]{2,1,0:T(8,128)(2,1)S(1)}, u32[]{:S(2)}, u32[]{:S(2)}) async-start(bf16[8,32,1024]{2,1,0:T(8,128)(2,1)} %bitcast.10), calls=%async_computation.2 | async-start | bytes 1048576 | tf_op jit(solution)/shard_map/all_to_all | solution.py:195
  80.8 0.1 shard_map.112.part_ref
  80.9 17.6 %collective-permute-start.3 = (bf16[32,2048]{1,0:T(8,128)(2,1)S(1)}, bf16[32,2048]{1,0:T(8,128)(2,1)S(1)}, u32[]{:S(2)}, u32[]{:S(2)}) collective-permute-start(bf16[32,2048]{1,0:T(8,128)(2,1)S(1)} %shard_map.112.part_ref), channel_id=1, source_target_pairs={{0,64},{64,0},{1,65},{65,1},{2,66},{66,2},{3,67},{67,3},{4,68},{68... | collective-permute-start | bytes 393224 | tf_op jit(solution)/shard_map/ppermute | solution.py:206
  98.6 0.0 all-to-all-done.2.got_ref
  98.6 0.1 shard_map.115.act_ref
  98.7 2.3 %collective-permute-done.3.other_ref = bf16[32,2048]{1,0:T(8,128)(2,1)S(1)} collective-permute-done((bf16[32,2048]{1,0:T(8,128)(2,1)S(1)}, bf16[32,2048]{1,0:T(8,128)(2,1)S(1)}, u32[]{:S(2)}, u32[]{:S(2)}) %collective-permute-start.3) | collective-permute-done | bytes 131104 | tf_op jit(solution)/shard_map/ppermute | solution.py:206
  101.0 0.9 shard_map.113
  101.9 6.6 %all-to-all-start.4 = ((bf16[8,32,1024]{2,1,0:T(8,128)(2,1)}), bf16[8,32,1024]{2,1,0:T(8,128)(2,1)S(1)}, u32[]{:S(2)}, u32[]{:S(2)}) async-start(bf16[8,32,1024]{2,1,0:T(8,128)(2,1)} %shard_map.113), calls=%async_computation.4 | async-start | bytes 1048576 | tf_op jit(solution)/shard_map/all_to_all | solution.py:195
  108.5 13.7 %collective-permute-start.8 = (bf16[32,1024]{1,0:T(8,128)(2,1)S(1)}, bf16[32,1024]{1,0:T(8,128)(2,1)S(1)}, u32[]{:S(2)}, u32[]{:S(2)}) collective-permute-start(bf16[32,1024]{1,0:T(8,128)(2,1)S(1)} %shard_map.115.act_ref), channel_id=1, source_target_pairs={{0,64},{64,0},{1,65},{65,1},{2,66},{66,2},{3,67},{67,3},{4,68},{68... | collective-permute-start | bytes 196616 | tf_op jit(solution)/shard_map/ppermute | solution.py:206
  122.2 2.7 %collective-permute-done.8.act_other_ref = bf16[32,1024]{1,0:T(8,128)(2,1)S(1)} collective-permute-done((bf16[32,1024]{1,0:T(8,128)(2,1)S(1)}, bf16[32,1024]{1,0:T(8,128)(2,1)S(1)}, u32[]{:S(2)}, u32[]{:S(2)}) %collective-permute-start.8) | collective-permute-done | bytes 65568 | tf_op jit(solution)/shard_map/ppermute | solution.py:206
  124.9 1.1 shard_map.116
  126.0 0.0 all-to-all-done.4
  126.0 6.6 %all-to-all-start.3 = ((bf16[8,32,2048]{2,1,0:T(8,128)(2,1)}), bf16[8,32,2048]{2,1,0:T(8,128)(2,1)S(1)}, u32[]{:S(2)}, u32[]{:S(2)}) async-start(bf16[8,32,2048]{2,1,0:T(8,128)(2,1)} %shard_map.116), calls=%async_computation.3 | async-start | bytes 2097152 | tf_op jit(solution)/shard_map/all_to_all | solution.py:195
  132.6 6.2 %collective-permute-start.9 = (bf16[256,512]{1,0:T(8,128)(2,1)S(1)}, bf16[256,512]{1,0:T(8,128)(2,1)S(1)}, u32[]{:S(2)}, u32[]{:S(2)}) collective-permute-start(bf16[256,512]{1,0:T(8,128)(2,1)S(1)} %pad_maximum_fusion.2), channel_id=1, source_target_pairs={{0,1},{1,0},{2,3},{3,2},{4,5},{5,4},{6,7},{7,6},{8,9},{9,8},{10,11... | collective-permute-start | bytes 786440 | tf_op jit(solution)/shard_map/ppermute | solution.py:206
  138.9 1.1 collective-permute-done.9.got_ref
  140.0 0.7 shard_map.117
  140.7 2.1 collective-permute-start.10
  142.8 6.7 %collective-permute-done.10 = bf16[448,256]{1,0:T(8,128)(2,1)} collective-permute-done((bf16[448,256]{1,0:T(8,128)(2,1)S(1)}, bf16[448,256]{1,0:T(8,128)(2,1)}, u32[]{:S(2)}, u32[]{:S(2)}) %collective-permute-start.10) | collective-permute-done | bytes 229408 | tf_op jit(solution)/shard_map/ppermute | solution.py:206
  149.5 8.6 %all-to-all-done.3 = bf16[8,32,2048]{2,1,0:T(8,128)(2,1)S(1)} async-done(((bf16[8,32,2048]{2,1,0:T(8,128)(2,1)}), bf16[8,32,2048]{2,1,0:T(8,128)(2,1)S(1)}, u32[]{:S(2)}, u32[]{:S(2)}) %all-to-all-start.3) | async-done | bytes 1048608 | tf_op jit(solution)/shard_map/all_to_all | solution.py:195
  158.2 0.0 copy-start.1
  158.2 0.0 copy-start.3
  158.2 0.1 pad_maximum_fusion
  158.3 6.2 %collective-permute-start.11 = (bf16[256,1024]{1,0:T(8,128)(2,1)S(1)}, bf16[256,1024]{1,0:T(8,128)(2,1)S(1)}, u32[]{:S(2)}, u32[]{:S(2)}) collective-permute-start(bf16[256,1024]{1,0:T(8,128)(2,1)S(1)} %pad_maximum_fusion), channel_id=1, source_target_pairs={{0,1},{1,0},{2,3},{3,2},{4,5},{5,4},{6,7},{7,6},{8,9},{9,8},{10,11... | collective-permute-start | bytes 1572872 | tf_op jit(solution)/shard_map/ppermute | solution.py:206
  164.5 0.9 copy-done.15
  165.5 1.8 shard_map.118
  167.3 0.0 collective-permute-done.11.refs_3_
  167.3 23.0 %all-to-all-start.5 = ((bf16[16,16,896]{2,1,0:T(8,128)(2,1)}), bf16[16,16,896]{2,1,0:T(8,128)(2,1)S(1)}, u32[]{:S(2)}, u32[]{:S(2)}) async-start(bf16[16,16,896]{2,1,0:T(8,128)(2,1)} %bitcast.13), calls=%async_computation.5 | async-start | bytes 917504 | tf_op jit(solution)/shard_map/all_to_all | solution.py:195
  190.3 0.7 shard_map.121
  191.0 1.9 collective-permute-start.12
  192.9 0.0 copy-start.16
  192.9 0.0 copy-start.17
  192.9 1.8 multiply_bitcast_fusion
  194.7 0.2 shard_map.119
  194.9 16.4 %collective-permute-done.12.got_ref = bf16[448,512]{1,0:T(8,128)(2,1)S(1)} collective-permute-done((bf16[448,512]{1,0:T(8,128)(2,1)S(1)}, bf16[448,512]{1,0:T(8,128)(2,1)S(1)}, u32[]{:S(2)}, u32[]{:S(2)}) %collective-permute-start.12) | collective-permute-done | bytes 458784 | tf_op jit(solution)/shard_map/ppermute | solution.py:206
  211.3 1.0 shard_map.122
  212.3 2.7 %all-to-all-done.5 = bf16[16,16,896]{2,1,0:T(8,128)(2,1)S(1)} async-done(((bf16[16,16,896]{2,1,0:T(8,128)(2,1)}), bf16[16,16,896]{2,1,0:T(8,128)(2,1)S(1)}, u32[]{:S(2)}, u32[]{:S(2)}) %all-to-all-start.5) | async-done | bytes 458784 | tf_op jit(solution)/shard_map/all_to_all | solution.py:195
  215.0 1.0 shard_map.120
  (33 shorter events, 0.2 us)
Async XLA Ops:
  2.9 17.2 %copy-start.18 = (bf16[1,448,256]{2,1,0:T(8,128)(2,1)S(1)}, bf16[1,448,256]{2,1,0:T(8,128)(2,1)}, u32[]{:S(2)}) copy-start(bf16[1,448,256]{2,1,0:T(8,128)(2,1)} %param.12) | copy-start | bytes 688132
  2.9 17.2 %copy-start.19 = (bf16[1,448,256]{2,1,0:T(8,128)(2,1)S(1)}, bf16[1,448,256]{2,1,0:T(8,128)(2,1)}, u32[]{:S(2)}) copy-start(bf16[1,448,256]{2,1,0:T(8,128)(2,1)} %param.11) | copy-start | bytes 688132
  2.9 40.6 %all-to-all-start = ((bf16[16,16,896]{2,1,0:T(8,128)(2,1)}), bf16[16,16,896]{2,1,0:T(8,128)(2,1)S(1)}, u32[]{:S(2)}, u32[]{:S(2)}) async-start(bf16[16,16,896]{2,1,0:T(8,128)(2,1)} %bitcast.41), calls=%async_computation | async-start | bytes 917504 | tf_op jit(solution)/shard_map/all_to_all | solution.py:195
  20.1 17.1 %collective-permute-start.1 = (bf16[448,512]{1,0:T(8,128)(2,1)S(1)}, bf16[448,512]{1,0:T(8,128)(2,1)S(1)}, u32[]{:S(2)}, u32[]{:S(2)}) collective-permute-start(bf16[448,512]{1,0:T(8,128)(2,1)S(1)} %pad_maximum_fusion.1.refs_0_), channel_id=1, source_target_pairs={{0,2},{2,0},{1,3},{3,1},{4,6},{6,4},{5,7},{7,5},{8,10},{10,8},{9,1... | collective-permute-start | bytes 1376264 | tf_op jit(solution)/shard_map/ppermute | solution.py:206
  24.1 16.4 %collective-permute-start = (bf16[448,512]{1,0:T(8,128)(2,1)S(1)}, bf16[448,512]{1,0:T(8,128)(2,1)S(1)}, u32[]{:S(2)}, u32[]{:S(2)}) collective-permute-start(bf16[448,512]{1,0:T(8,128)(2,1)S(1)} %pad_maximum_fusion.1.refs_0_), channel_id=1, source_target_pairs={{0,1},{1,0},{2,3},{3,2},{4,5},{5,4},{6,7},{7,6},{8,9},{9,8},{10,11... | collective-permute-start | bytes 1376264 | tf_op jit(solution)/shard_map/ppermute | solution.py:206
  37.3 7.9 %copy-start = (bf16[448,512]{1,0:T(8,128)(2,1)}, bf16[448,512]{1,0:T(8,128)(2,1)S(1)}, u32[]{:S(2)}) copy-start(bf16[448,512]{1,0:T(8,128)(2,1)S(1)} %collective-permute-done.1.refs_2_) | copy-start | bytes 1376260
  37.3 4.7 %collective-permute-start.2 = (bf16[448,512]{1,0:T(8,128)(2,1)S(1)}, bf16[448,512]{1,0:T(8,128)(2,1)S(1)}, u32[]{:S(2)}, u32[]{:S(2)}) collective-permute-start(bf16[448,512]{1,0:T(8,128)(2,1)S(1)} %collective-permute-done.1.refs_2_), channel_id=1, source_target_pairs={{0,1},{1,0},{2,3},{3,2},{4,5},{5,4},{6,7},{7,6},{8,9},{9,8},{10,11... | collective-permute-start | bytes 1376264 | tf_op jit(solution)/shard_map/ppermute | solution.py:206
  40.5 4.7 %copy-start.2 = (bf16[448,512]{1,0:T(8,128)(2,1)}, bf16[448,512]{1,0:T(8,128)(2,1)S(1)}, u32[]{:S(2)}) copy-start(bf16[448,512]{1,0:T(8,128)(2,1)S(1)} %collective-permute-done.refs_1_) | copy-start | bytes 1376260
  41.9 3.3 %copy-start.4 = (bf16[448,512]{1,0:T(8,128)(2,1)}, bf16[448,512]{1,0:T(8,128)(2,1)S(1)}, u32[]{:S(2)}) copy-start(bf16[448,512]{1,0:T(8,128)(2,1)S(1)} %collective-permute-done.2.refs_3_) | copy-start | bytes 1376260
  45.2 7.0 %copy-start.8 = (bf16[1,256,448]{1,2,0:T(8,128)(2,1)S(1)}, bf16[1,256,448]{1,2,0:T(8,128)(2,1)}, u32[]{:S(2)}) copy-start(bf16[1,256,448]{1,2,0:T(8,128)(2,1)} %param.13) | copy-start | bytes 688132
  45.2 32.1 %all-to-all-start.1 = ((bf16[8,32,2048]{2,1,0:T(8,128)(2,1)}), bf16[8,32,2048]{2,1,0:T(8,128)(2,1)S(1)}, u32[]{:S(2)}, u32[]{:S(2)}) async-start(bf16[8,32,2048]{2,1,0:T(8,128)(2,1)} %bitcast.6), calls=%async_computation.1 | async-start | bytes 2097152 | tf_op jit(solution)/shard_map/all_to_all | solution.py:195
  52.2 11.6 %collective-permute-start.5 = (bf16[448,256]{1,0:T(8,128)(2,1)S(1)}, bf16[448,256]{1,0:T(8,128)(2,1)S(1)}, u32[]{:S(2)}, u32[]{:S(2)}) collective-permute-start(bf16[448,256]{1,0:T(8,128)(2,1)S(1)} %bitcast.33), channel_id=1, source_target_pairs={{0,2},{2,0},{1,3},{3,1},{4,6},{6,4},{5,7},{7,5},{8,10},{10,8},{9,1... | collective-permute-start | bytes 688136 | tf_op jit(solution)/shard_map/ppermute | solution.py:206
  58.7 11.6 %collective-permute-start.7 = (bf16[256,896]{1,0:T(8,128)(2,1)S(1)}, bf16[256,896]{1,0:T(8,128)(2,1)S(1)}, u32[]{:S(2)}, u32[]{:S(2)}) collective-permute-start(bf16[256,896]{1,0:T(8,128)(2,1)S(1)} %bitcast.28), channel_id=1, source_target_pairs={{0,1},{1,0},{2,3},{3,2},{4,5},{5,4},{6,7},{7,6},{8,9},{9,8},{10,11... | collective-permute-start | bytes 1376264 | tf_op jit(solution)/shard_map/ppermute | solution.py:206
  61.9 6.0 %collective-permute-start.4 = (bf16[448,256]{1,0:T(8,128)(2,1)S(1)}, bf16[448,256]{1,0:T(8,128)(2,1)S(1)}, u32[]{:S(2)}, u32[]{:S(2)}) collective-permute-start(bf16[448,256]{1,0:T(8,128)(2,1)S(1)} %bitcast.34), channel_id=1, source_target_pairs={{0,1},{1,0},{2,3},{3,2},{4,5},{5,4},{6,7},{7,6},{8,9},{9,8},{10,11... | collective-permute-start | bytes 688136 | tf_op jit(solution)/shard_map/ppermute | solution.py:206
  63.8 6.4 %copy-start.10 = (bf16[448,256]{1,0:T(8,128)(2,1)}, bf16[448,256]{1,0:T(8,128)(2,1)S(1)}, u32[]{:S(2)}) copy-start(bf16[448,256]{1,0:T(8,128)(2,1)S(1)} %collective-permute-done.5.refs_2_.refs_6_) | copy-start | bytes 688132
  63.9 5.1 %collective-permute-start.6 = (bf16[448,256]{1,0:T(8,128)(2,1)S(1)}, bf16[448,256]{1,0:T(8,128)(2,1)S(1)}, u32[]{:S(2)}, u32[]{:S(2)}) collective-permute-start(bf16[448,256]{1,0:T(8,128)(2,1)S(1)} %collective-permute-done.5.refs_2_.refs_6_), channel_id=1, source_target_pairs={{0,1},{1,0},{2,3},{3,2},{4,5},{5,4},{6,7},{7,6},{8,9},{9,8},{10,11... | collective-permute-start | bytes 688136 | tf_op jit(solution)/shard_map/ppermute | solution.py:206
  67.9 2.4 %copy-start.12 = (bf16[448,256]{1,0:T(8,128)(2,1)}, bf16[448,256]{1,0:T(8,128)(2,1)S(1)}, u32[]{:S(2)}) copy-start(bf16[448,256]{1,0:T(8,128)(2,1)S(1)} %collective-permute-done.4.refs_1_.refs_5_) | copy-start | bytes 688132
  69.0 1.3 copy-start.14
  70.3 69.7 %copy-start.6 = (bf16[256,896]{1,0:T(8,128)(2,1)}, bf16[256,896]{1,0:T(8,128)(2,1)S(1)}, u32[]{:S(2)}) copy-start(bf16[256,896]{1,0:T(8,128)(2,1)S(1)} %collective-permute-done.7.next_ref.refs_1_) | copy-start | bytes 1376260
  77.3 21.3 %all-to-all-start.2 = ((bf16[8,32,1024]{2,1,0:T(8,128)(2,1)}), bf16[8,32,1024]{2,1,0:T(8,128)(2,1)S(1)}, u32[]{:S(2)}, u32[]{:S(2)}) async-start(bf16[8,32,1024]{2,1,0:T(8,128)(2,1)} %bitcast.10), calls=%async_computation.2 | async-start | bytes 1048576 | tf_op jit(solution)/shard_map/all_to_all | solution.py:195
  80.9 20.1 %collective-permute-start.3 = (bf16[32,2048]{1,0:T(8,128)(2,1)S(1)}, bf16[32,2048]{1,0:T(8,128)(2,1)S(1)}, u32[]{:S(2)}, u32[]{:S(2)}) collective-permute-start(bf16[32,2048]{1,0:T(8,128)(2,1)S(1)} %shard_map.112.part_ref), channel_id=1, source_target_pairs={{0,64},{64,0},{1,65},{65,1},{2,66},{66,2},{3,67},{67,3},{4,68},{68... | collective-permute-start | bytes 393224 | tf_op jit(solution)/shard_map/ppermute | solution.py:206
  101.9 24.1 %all-to-all-start.4 = ((bf16[8,32,1024]{2,1,0:T(8,128)(2,1)}), bf16[8,32,1024]{2,1,0:T(8,128)(2,1)S(1)}, u32[]{:S(2)}, u32[]{:S(2)}) async-start(bf16[8,32,1024]{2,1,0:T(8,128)(2,1)} %shard_map.113), calls=%async_computation.4 | async-start | bytes 1048576 | tf_op jit(solution)/shard_map/all_to_all | solution.py:195
  108.5 16.4 %collective-permute-start.8 = (bf16[32,1024]{1,0:T(8,128)(2,1)S(1)}, bf16[32,1024]{1,0:T(8,128)(2,1)S(1)}, u32[]{:S(2)}, u32[]{:S(2)}) collective-permute-start(bf16[32,1024]{1,0:T(8,128)(2,1)S(1)} %shard_map.115.act_ref), channel_id=1, source_target_pairs={{0,64},{64,0},{1,65},{65,1},{2,66},{66,2},{3,67},{67,3},{4,68},{68... | collective-permute-start | bytes 196616 | tf_op jit(solution)/shard_map/ppermute | solution.py:206
  126.0 32.1 %all-to-all-start.3 = ((bf16[8,32,2048]{2,1,0:T(8,128)(2,1)}), bf16[8,32,2048]{2,1,0:T(8,128)(2,1)S(1)}, u32[]{:S(2)}, u32[]{:S(2)}) async-start(bf16[8,32,2048]{2,1,0:T(8,128)(2,1)} %shard_map.116), calls=%async_computation.3 | async-start | bytes 2097152 | tf_op jit(solution)/shard_map/all_to_all | solution.py:195
  132.6 7.4 %collective-permute-start.9 = (bf16[256,512]{1,0:T(8,128)(2,1)S(1)}, bf16[256,512]{1,0:T(8,128)(2,1)S(1)}, u32[]{:S(2)}, u32[]{:S(2)}) collective-permute-start(bf16[256,512]{1,0:T(8,128)(2,1)S(1)} %pad_maximum_fusion.2), channel_id=1, source_target_pairs={{0,1},{1,0},{2,3},{3,2},{4,5},{5,4},{6,7},{7,6},{8,9},{9,8},{10,11... | collective-permute-start | bytes 786440 | tf_op jit(solution)/shard_map/ppermute | solution.py:206
  140.7 8.8 %collective-permute-start.10 = (bf16[448,256]{1,0:T(8,128)(2,1)S(1)}, bf16[448,256]{1,0:T(8,128)(2,1)}, u32[]{:S(2)}, u32[]{:S(2)}) collective-permute-start(bf16[448,256]{1,0:T(8,128)(2,1)S(1)} %get-tuple-element.42), channel_id=1, source_target_pairs={{0,2},{2,0},{1,3},{3,1},{4,6},{6,4},{5,7},{7,5},{8,10},{10,8},{9,1... | collective-permute-start | bytes 688136 | tf_op jit(solution)/shard_map/ppermute | solution.py:206
  158.1 6.4 %copy-start.5 = (bf16[448,512]{1,0:T(8,128)(2,1)S(1)}, bf16[448,512]{1,0:T(8,128)(2,1)}, u32[]{:S(2)}) copy-start(bf16[448,512]{1,0:T(8,128)(2,1)} %copy-done.4) | copy-start | bytes 1376260
  158.1 6.4 %copy-start.9 = (bf16[1,256,448]{1,2,0:T(8,128)(2,1)S(1)}, bf16[1,256,448]{1,2,0:T(8,128)(2,1)}, u32[]{:S(2)}) copy-start(bf16[1,256,448]{1,2,0:T(8,128)(2,1)} %param.13) | copy-start | bytes 688132
  158.1 6.4 %copy-start.11 = (bf16[448,256]{1,0:T(8,128)(2,1)S(1)}, bf16[448,256]{1,0:T(8,128)(2,1)}, u32[]{:S(2)}) copy-start(bf16[448,256]{1,0:T(8,128)(2,1)} %copy-done.10) | copy-start | bytes 688132
  158.1 6.4 %copy-start.13 = (bf16[448,256]{1,0:T(8,128)(2,1)S(1)}, bf16[448,256]{1,0:T(8,128)(2,1)}, u32[]{:S(2)}) copy-start(bf16[448,256]{1,0:T(8,128)(2,1)} %copy-done.12) | copy-start | bytes 688132
  158.2 6.4 %copy-start.1 = (bf16[448,512]{1,0:T(8,128)(2,1)S(1)}, bf16[448,512]{1,0:T(8,128)(2,1)}, u32[]{:S(2)}) copy-start(bf16[448,512]{1,0:T(8,128)(2,1)} %copy-done) | copy-start | bytes 1376260
  158.2 6.4 %copy-start.3 = (bf16[448,512]{1,0:T(8,128)(2,1)S(1)}, bf16[448,512]{1,0:T(8,128)(2,1)}, u32[]{:S(2)}) copy-start(bf16[448,512]{1,0:T(8,128)(2,1)} %copy-done.2) | copy-start | bytes 1376260
  158.3 9.1 %collective-permute-start.11 = (bf16[256,1024]{1,0:T(8,128)(2,1)S(1)}, bf16[256,1024]{1,0:T(8,128)(2,1)S(1)}, u32[]{:S(2)}, u32[]{:S(2)}) collective-permute-start(bf16[256,1024]{1,0:T(8,128)(2,1)S(1)} %pad_maximum_fusion), channel_id=1, source_target_pairs={{0,1},{1,0},{2,3},{3,2},{4,5},{5,4},{6,7},{7,6},{8,9},{9,8},{10,11... | collective-permute-start | bytes 1572872 | tf_op jit(solution)/shard_map/ppermute | solution.py:206
  164.5 0.9 copy-start.15
  167.3 23.0 %copy-start.7 = (bf16[256,896]{1,0:T(8,128)(2,1)S(1)}, bf16[256,896]{1,0:T(8,128)(2,1)}, u32[]{:S(2)}) copy-start(bf16[256,896]{1,0:T(8,128)(2,1)} %copy-done.6) | copy-start | bytes 1376260
  167.3 47.7 %all-to-all-start.5 = ((bf16[16,16,896]{2,1,0:T(8,128)(2,1)}), bf16[16,16,896]{2,1,0:T(8,128)(2,1)S(1)}, u32[]{:S(2)}, u32[]{:S(2)}) async-start(bf16[16,16,896]{2,1,0:T(8,128)(2,1)} %bitcast.13), calls=%async_computation.5 | async-start | bytes 917504 | tf_op jit(solution)/shard_map/all_to_all | solution.py:195
  191.0 20.3 %collective-permute-start.12 = (bf16[448,512]{1,0:T(8,128)(2,1)S(1)}, bf16[448,512]{1,0:T(8,128)(2,1)S(1)}, u32[]{:S(2)}, u32[]{:S(2)}) collective-permute-start(bf16[448,512]{1,0:T(8,128)(2,1)S(1)} %get-tuple-element.54), channel_id=1, source_target_pairs={{0,2},{2,0},{1,3},{3,1},{4,6},{6,4},{5,7},{7,5},{8,10},{10,8},{9,1... | collective-permute-start | bytes 1376264 | tf_op jit(solution)/shard_map/ppermute | solution.py:206
  192.9 1.8 copy-start.16
  192.9 1.8 copy-start.17

commit v9 on v8

--- a/solution.py
+++ b/solution.py
@@ -261,11 +261,11 @@
     )
     down_got = swap_pair(down_away, "zb")
     deltas, hidden, down_got = lax.optimization_barrier((deltas, hidden, down_got))
-    deltas_got = to_next(deltas)
     (back,) = local(
         back_kernel, [((slots, 2 * width), BF)], hidden, deltas, *w_in, *w_out
     )
-    back, deltas_got, ids, weight = lax.optimization_barrier((back, deltas_got, ids, weight))
+    back, ids, weight, deltas = lax.optimization_barrier((back, ids, weight, deltas))
+    deltas_got = to_next(deltas)
     count = TOP * tok_rows
     place, column = local(
         place_kernel, [((slots, count), BF), ((count, count), F32)], ids, weight

time: 219 us -> 221 us (level)
  local copies, waits for them, and re-layouts: 1.08 us -> 6.66 us
  waiting for transfers between devices: 61.5 us -> 57.7 us
    unnamed x40 -> x38, local copies, waits for them, and re-layouts: 1.02 us -> 6.61 us
    all_to_all x6, waiting for transfers between devices: 19.8 us -> 16.3 us  [swap(): return lax.all_to_all(value, axis, split_axis=0, concat_axis=0, tiled=True)]
  transfers between devices with their start and end apart: 19 -> 19, of which waited for: 12 -> 12; matrix products, arithmetic and copies ran while one was open for 1% -> 1% of each run, Pallas kernels for 3% -> 2%
where the time goes in v9:
time: 221 us; the launch traced here: 218 us
  starting transfers between devices  138 us (62%)
  waiting for transfers between devices  57.7 us (26%)
  Pallas kernels  12.9 us (6%)
  local copies, waits for them, and re-layouts  6.66 us (3%)
    ppermute x13, starting transfers between devices, swap_pair(): return lax.ppermute(value, axis, [(0, 1), (1, 0)])  72.4 us
    all_to_all x6, starting transfers between devices, swap(): return lax.all_to_all(value, axis, split_axis=0, concat_axis=0, tiled=True)  65.4 us
    ppermute x13, waiting for transfers between devices, swap_pair(): return lax.ppermute(value, axis, [(0, 1), (1, 0)])  41.4 us
    all_to_all x6, waiting for transfers between devices, swap(): return lax.all_to_all(value, axis, split_axis=0, concat_axis=0, tiled=True)  16.3 us
    pallas_call x13, Pallas kernels, local(): pl.pallas_call(fetching if fetch else kernel, out_shape=[jax.ShapeDtypeSt...  12.9 us
    unnamed x38, local copies, waits for them, and re-layouts  6.61 us
  transfers between devices with their start and end apart: 19, of which 12 were waited for; matrix products, arithmetic and copies ran while one was open for 1% of the time, Pallas kernels for 2%

profile of v9, /device:TPU:1, one launch (start us, length us, event | category | flops | bytes accessed | tf_op | source)
XLA Modules:
  0.0 217.9 jit_solution(6478719526287396466)
XLA Ops:
  0.6 2.2 %shard_map.110 = bf16[256,896]{1,0:T(8,128)(2,1)} custom-call(s32[2,64]{1,0:T(2,128)} %bitcast.37, f32[2,64]{1,0:T(2,128)} %bitcast.39, bf16[64,448]{1,0:T(8,128)(2,1)} %refs_2_.1, bf16[64,448]{1,0:T(8,128)(2,1)} %refs_3_.1), custom_call_target="tpu_custom_call" | custom-call | flops 2000000000 | bytes 1148928 | tf_op jit(solution)/shard_map/pallas_call | solution.py:48
  2.9 0.0 copy-start.17
  2.9 0.0 copy-start.18
  2.9 17.2 %all-to-all-start = ((bf16[16,16,896]{2,1,0:T(8,128)(2,1)}), bf16[16,16,896]{2,1,0:T(8,128)(2,1)S(1)}, u32[]{:S(2)}, u32[]{:S(2)}) async-start(bf16[16,16,896]{2,1,0:T(8,128)(2,1)} %bitcast.41), calls=%async_computation | async-start | bytes 917504 | tf_op jit(solution)/shard_map/all_to_all | solution.py:195
  20.1 4.0 %collective-permute-start.1 = (bf16[448,512]{1,0:T(8,128)(2,1)S(1)}, bf16[448,512]{1,0:T(8,128)(2,1)S(1)}, u32[]{:S(2)}, u32[]{:S(2)}) collective-permute-start(bf16[448,512]{1,0:T(8,128)(2,1)S(1)} %pad_maximum_fusion.1.refs_0_), channel_id=1, source_target_pairs={{0,2},{2,0},{1,3},{3,1},{4,6},{6,4},{5,7},{7,5},{8,10},{10,8},{9,1... | collective-permute-start | bytes 1376264 | tf_op jit(solution)/shard_map/ppermute | solution.py:206
  24.1 3.1 %collective-permute-start = (bf16[448,512]{1,0:T(8,128)(2,1)S(1)}, bf16[448,512]{1,0:T(8,128)(2,1)S(1)}, u32[]{:S(2)}, u32[]{:S(2)}) collective-permute-start(bf16[448,512]{1,0:T(8,128)(2,1)S(1)} %pad_maximum_fusion.1.refs_0_), channel_id=1, source_target_pairs={{0,1},{1,0},{2,3},{3,2},{4,5},{5,4},{6,7},{7,6},{8,9},{9,8},{10,11... | collective-permute-start | bytes 1376264 | tf_op jit(solution)/shard_map/ppermute | solution.py:206
  27.3 10.0 %collective-permute-done.1.refs_2_ = bf16[448,512]{1,0:T(8,128)(2,1)S(1)} collective-permute-done((bf16[448,512]{1,0:T(8,128)(2,1)S(1)}, bf16[448,512]{1,0:T(8,128)(2,1)S(1)}, u32[]{:S(2)}, u32[]{:S(2)}) %collective-permute-start.1) | collective-permute-done | bytes 458784 | tf_op jit(solution)/shard_map/ppermute | solution.py:206
  37.3 3.3 %collective-permute-start.2 = (bf16[448,512]{1,0:T(8,128)(2,1)S(1)}, bf16[448,512]{1,0:T(8,128)(2,1)S(1)}, u32[]{:S(2)}, u32[]{:S(2)}) collective-permute-start(bf16[448,512]{1,0:T(8,128)(2,1)S(1)} %collective-permute-done.1.refs_2_), channel_id=1, source_target_pairs={{0,1},{1,0},{2,3},{3,2},{4,5},{5,4},{6,7},{7,6},{8,9},{9,8},{10,11... | collective-permute-start | bytes 1376264 | tf_op jit(solution)/shard_map/ppermute | solution.py:206
  40.5 0.0 collective-permute-done.refs_1_
  40.5 0.0 copy-start.3
  40.5 1.4 collective-permute-done.2.refs_3_
  41.9 1.6 all-to-all-done
  43.5 1.7 shard_map.111
  45.2 7.0 %all-to-all-start.1 = ((bf16[8,32,2048]{2,1,0:T(8,128)(2,1)}), bf16[8,32,2048]{2,1,0:T(8,128)(2,1)S(1)}, u32[]{:S(2)}, u32[]{:S(2)}) async-start(bf16[8,32,2048]{2,1,0:T(8,128)(2,1)} %bitcast.6), calls=%async_computation.1 | async-start | bytes 2097152 | tf_op jit(solution)/shard_map/all_to_all | solution.py:195
  52.2 6.5 %collective-permute-start.5 = (bf16[448,256]{1,0:T(8,128)(2,1)S(1)}, bf16[448,256]{1,0:T(8,128)(2,1)S(1)}, u32[]{:S(2)}, u32[]{:S(2)}) collective-permute-start(bf16[448,256]{1,0:T(8,128)(2,1)S(1)} %bitcast.33), channel_id=1, source_target_pairs={{0,2},{2,0},{1,3},{3,1},{4,6},{6,4},{5,7},{7,5},{8,10},{10,8},{9,1... | collective-permute-start | bytes 688136 | tf_op jit(solution)/shard_map/ppermute | solution.py:206
  58.7 3.2 %collective-permute-start.7 = (bf16[256,896]{1,0:T(8,128)(2,1)S(1)}, bf16[256,896]{1,0:T(8,128)(2,1)S(1)}, u32[]{:S(2)}, u32[]{:S(2)}) collective-permute-start(bf16[256,896]{1,0:T(8,128)(2,1)S(1)} %bitcast.28), channel_id=1, source_target_pairs={{0,1},{1,0},{2,3},{3,2},{4,5},{5,4},{6,7},{7,6},{8,9},{9,8},{10,11... | collective-permute-start | bytes 1376264 | tf_op jit(solution)/shard_map/ppermute | solution.py:206
  61.9 1.9 collective-permute-start.4
  63.8 0.0 collective-permute-done.5.refs_2_.refs_6_
  63.8 4.0 %collective-permute-start.6 = (bf16[448,256]{1,0:T(8,128)(2,1)S(1)}, bf16[448,256]{1,0:T(8,128)(2,1)S(1)}, u32[]{:S(2)}, u32[]{:S(2)}) collective-permute-start(bf16[448,256]{1,0:T(8,128)(2,1)S(1)} %collective-permute-done.5.refs_2_.refs_6_), channel_id=1, source_target_pairs={{0,1},{1,0},{2,3},{3,2},{4,5},{5,4},{6,7},{7,6},{8,9},{9,8},{10,11... | collective-permute-start | bytes 688136 | tf_op jit(solution)/shard_map/ppermute | solution.py:206
  67.9 1.1 collective-permute-done.6.refs_3_.refs_7_
  69.0 1.3 shard_map.114
  70.3 0.0 collective-permute-done.7.next_ref.refs_1_
  70.3 0.0 copy-start
  70.3 0.8 copy-done
  71.0 6.2 %all-to-all-done.1.got_ref = bf16[8,32,2048]{2,1,0:T(8,128)(2,1)S(1)} async-done(((bf16[8,32,2048]{2,1,0:T(8,128)(2,1)}), bf16[8,32,2048]{2,1,0:T(8,128)(2,1)S(1)}, u32[]{:S(2)}, u32[]{:S(2)}) %all-to-all-start.1) | async-done | bytes 1048608 | tf_op jit(solution)/shard_map/all_to_all | solution.py:195
  77.3 3.5 %all-to-all-start.2 = ((bf16[8,32,1024]{2,1,0:T(8,128)(2,1)}), bf16[8,32,1024]{2,1,0:T(8,128)(2,1)S(1)}, u32[]{:S(2)}, u32[]{:S(2)}) async-start(bf16[8,32,1024]{2,1,0:T(8,128)(2,1)} %bitcast.10), calls=%async_computation.2 | async-start | bytes 1048576 | tf_op jit(solution)/shard_map/all_to_all | solution.py:195
  80.8 0.1 shard_map.112.part_ref
  80.9 17.6 %collective-permute-start.3 = (bf16[32,2048]{1,0:T(8,128)(2,1)S(1)}, bf16[32,2048]{1,0:T(8,128)(2,1)S(1)}, u32[]{:S(2)}, u32[]{:S(2)}) collective-permute-start(bf16[32,2048]{1,0:T(8,128)(2,1)S(1)} %shard_map.112.part_ref), channel_id=1, source_target_pairs={{0,64},{64,0},{1,65},{65,1},{2,66},{66,2},{3,67},{67,3},{4,68},{68... | collective-permute-start | bytes 393224 | tf_op jit(solution)/shard_map/ppermute | solution.py:206
  98.6 0.0 all-to-all-done.2.got_ref
  98.6 0.1 shard_map.115.act_ref
  98.7 2.3 %collective-permute-done.3.other_ref = bf16[32,2048]{1,0:T(8,128)(2,1)S(1)} collective-permute-done((bf16[32,2048]{1,0:T(8,128)(2,1)S(1)}, bf16[32,2048]{1,0:T(8,128)(2,1)S(1)}, u32[]{:S(2)}, u32[]{:S(2)}) %collective-permute-start.3) | collective-permute-done | bytes 131104 | tf_op jit(solution)/shard_map/ppermute | solution.py:206
  101.0 0.9 shard_map.113
  101.9 6.6 %all-to-all-start.4 = ((bf16[8,32,1024]{2,1,0:T(8,128)(2,1)}), bf16[8,32,1024]{2,1,0:T(8,128)(2,1)S(1)}, u32[]{:S(2)}, u32[]{:S(2)}) async-start(bf16[8,32,1024]{2,1,0:T(8,128)(2,1)} %shard_map.113), calls=%async_computation.4 | async-start | bytes 1048576 | tf_op jit(solution)/shard_map/all_to_all | solution.py:195
  108.4 13.7 %collective-permute-start.8 = (bf16[32,1024]{1,0:T(8,128)(2,1)S(1)}, bf16[32,1024]{1,0:T(8,128)(2,1)S(1)}, u32[]{:S(2)}, u32[]{:S(2)}) collective-permute-start(bf16[32,1024]{1,0:T(8,128)(2,1)S(1)} %shard_map.115.act_ref), channel_id=1, source_target_pairs={{0,64},{64,0},{1,65},{65,1},{2,66},{66,2},{3,67},{67,3},{4,68},{68... | collective-permute-start | bytes 196616 | tf_op jit(solution)/shard_map/ppermute | solution.py:206
  122.2 2.7 %collective-permute-done.8.act_other_ref = bf16[32,1024]{1,0:T(8,128)(2,1)S(1)} collective-permute-done((bf16[32,1024]{1,0:T(8,128)(2,1)S(1)}, bf16[32,1024]{1,0:T(8,128)(2,1)S(1)}, u32[]{:S(2)}, u32[]{:S(2)}) %collective-permute-start.8) | collective-permute-done | bytes 65568 | tf_op jit(solution)/shard_map/ppermute | solution.py:206
  124.9 1.1 shard_map.116
  126.0 0.0 all-to-all-done.4
  126.0 6.6 %all-to-all-start.3 = ((bf16[8,32,2048]{2,1,0:T(8,128)(2,1)}), bf16[8,32,2048]{2,1,0:T(8,128)(2,1)S(1)}, u32[]{:S(2)}, u32[]{:S(2)}) async-start(bf16[8,32,2048]{2,1,0:T(8,128)(2,1)} %shard_map.116), calls=%async_computation.3 | async-start | bytes 2097152 | tf_op jit(solution)/shard_map/all_to_all | solution.py:195
  132.6 6.4 %collective-permute-start.9 = (bf16[256,512]{1,0:T(8,128)(2,1)S(1)}, bf16[256,512]{1,0:T(8,128)(2,1)S(1)}, u32[]{:S(2)}, u32[]{:S(2)}) collective-permute-start(bf16[256,512]{1,0:T(8,128)(2,1)S(1)} %pad_maximum_fusion.2), channel_id=1, source_target_pairs={{0,1},{1,0},{2,3},{3,2},{4,5},{5,4},{6,7},{7,6},{8,9},{9,8},{10,11... | collective-permute-start | bytes 786440 | tf_op jit(solution)/shard_map/ppermute | solution.py:206
  139.0 1.1 collective-permute-done.9.got_ref
  140.1 0.7 shard_map.117
  140.8 2.1 collective-permute-start.10
  142.9 6.7 %collective-permute-done.10 = bf16[448,256]{1,0:T(8,128)(2,1)} collective-permute-done((bf16[448,256]{1,0:T(8,128)(2,1)S(1)}, bf16[448,256]{1,0:T(8,128)(2,1)}, u32[]{:S(2)}, u32[]{:S(2)}) %collective-permute-start.10) | collective-permute-done | bytes 229408 | tf_op jit(solution)/shard_map/ppermute | solution.py:206
  149.6 8.5 %all-to-all-done.3 = bf16[8,32,2048]{2,1,0:T(8,128)(2,1)S(1)} async-done(((bf16[8,32,2048]{2,1,0:T(8,128)(2,1)}), bf16[8,32,2048]{2,1,0:T(8,128)(2,1)S(1)}, u32[]{:S(2)}, u32[]{:S(2)}) %all-to-all-start.3) | async-done | bytes 1048608 | tf_op jit(solution)/shard_map/all_to_all | solution.py:195
  158.1 1.0 copy-done.4
  159.1 1.0 copy-done.6
  160.1 0.9 copy-done.8
  161.1 0.9 copy-done.10
  162.0 0.9 copy-done.12
  163.0 0.9 copy-done.14
  163.9 1.8 shard_map.118
  165.7 24.7 %all-to-all-start.5 = ((bf16[16,16,896]{2,1,0:T(8,128)(2,1)}), bf16[16,16,896]{2,1,0:T(8,128)(2,1)S(1)}, u32[]{:S(2)}, u32[]{:S(2)}) async-start(bf16[16,16,896]{2,1,0:T(8,128)(2,1)} %bitcast.13), calls=%async_computation.5 | async-start | bytes 917504 | tf_op jit(solution)/shard_map/all_to_all | solution.py:195
  190.5 0.0 copy-start.2
  190.5 0.1 pad_maximum_fusion
  190.6 4.6 %collective-permute-start.11 = (bf16[256,1024]{1,0:T(8,128)(2,1)S(1)}, bf16[256,1024]{1,0:T(8,128)(2,1)S(1)}, u32[]{:S(2)}, u32[]{:S(2)}) collective-permute-start(bf16[256,1024]{1,0:T(8,128)(2,1)S(1)} %pad_maximum_fusion), channel_id=1, source_target_pairs={{0,1},{1,0},{2,3},{3,2},{4,5},{5,4},{6,7},{7,6},{8,9},{9,8},{10,11... | collective-permute-start | bytes 1572872 | tf_op jit(solution)/shard_map/ppermute | solution.py:206
  195.2 1.5 collective-permute-done.11.refs_3_
  196.7 0.7 shard_map.121
  197.4 0.0 copy-start.15
  197.4 1.9 collective-permute-start.12
  199.4 0.2 shard_map.119
  199.6 1.8 multiply_bitcast_fusion
  201.3 14.5 %collective-permute-done.12.got_ref = bf16[448,512]{1,0:T(8,128)(2,1)S(1)} collective-permute-done((bf16[448,512]{1,0:T(8,128)(2,1)S(1)}, bf16[448,512]{1,0:T(8,128)(2,1)S(1)}, u32[]{:S(2)}, u32[]{:S(2)}) %collective-permute-start.12) | collective-permute-done | bytes 458784 | tf_op jit(solution)/shard_map/ppermute | solution.py:206
  215.9 1.0 shard_map.122
  216.9 1.0 shard_map.120
  (31 shorter events, 0.2 us)
Async XLA Ops:
  2.9 17.2 %copy-start.17 = (bf16[1,448,256]{2,1,0:T(8,128)(2,1)S(1)}, bf16[1,448,256]{2,1,0:T(8,128)(2,1)}, u32[]{:S(2)}) copy-start(bf16[1,448,256]{2,1,0:T(8,128)(2,1)} %param.12) | copy-start | bytes 688132
  2.9 17.2 %copy-start.18 = (bf16[1,448,256]{2,1,0:T(8,128)(2,1)S(1)}, bf16[1,448,256]{2,1,0:T(8,128)(2,1)}, u32[]{:S(2)}) copy-start(bf16[1,448,256]{2,1,0:T(8,128)(2,1)} %param.11) | copy-start | bytes 688132
  2.9 40.6 %all-to-all-start = ((bf16[16,16,896]{2,1,0:T(8,128)(2,1)}), bf16[16,16,896]{2,1,0:T(8,128)(2,1)S(1)}, u32[]{:S(2)}, u32[]{:S(2)}) async-start(bf16[16,16,896]{2,1,0:T(8,128)(2,1)} %bitcast.41), calls=%async_computation | async-start | bytes 917504 | tf_op jit(solution)/shard_map/all_to_all | solution.py:195
  20.1 17.1 %collective-permute-start.1 = (bf16[448,512]{1,0:T(8,128)(2,1)S(1)}, bf16[448,512]{1,0:T(8,128)(2,1)S(1)}, u32[]{:S(2)}, u32[]{:S(2)}) collective-permute-start(bf16[448,512]{1,0:T(8,128)(2,1)S(1)} %pad_maximum_fusion.1.refs_0_), channel_id=1, source_target_pairs={{0,2},{2,0},{1,3},{3,1},{4,6},{6,4},{5,7},{7,5},{8,10},{10,8},{9,1... | collective-permute-start | bytes 1376264 | tf_op jit(solution)/shard_map/ppermute | solution.py:206
  24.1 16.4 %collective-permute-start = (bf16[448,512]{1,0:T(8,128)(2,1)S(1)}, bf16[448,512]{1,0:T(8,128)(2,1)S(1)}, u32[]{:S(2)}, u32[]{:S(2)}) collective-permute-start(bf16[448,512]{1,0:T(8,128)(2,1)S(1)} %pad_maximum_fusion.1.refs_0_), channel_id=1, source_target_pairs={{0,1},{1,0},{2,3},{3,2},{4,5},{5,4},{6,7},{7,6},{8,9},{9,8},{10,11... | collective-permute-start | bytes 1376264 | tf_op jit(solution)/shard_map/ppermute | solution.py:206
  37.3 4.7 %collective-permute-start.2 = (bf16[448,512]{1,0:T(8,128)(2,1)S(1)}, bf16[448,512]{1,0:T(8,128)(2,1)S(1)}, u32[]{:S(2)}, u32[]{:S(2)}) collective-permute-start(bf16[448,512]{1,0:T(8,128)(2,1)S(1)} %collective-permute-done.1.refs_2_), channel_id=1, source_target_pairs={{0,1},{1,0},{2,3},{3,2},{4,5},{5,4},{6,7},{7,6},{8,9},{9,8},{10,11... | collective-permute-start | bytes 1376264 | tf_op jit(solution)/shard_map/ppermute | solution.py:206
  40.5 4.7 %copy-start.3 = (bf16[448,512]{1,0:T(8,128)(2,1)}, bf16[448,512]{1,0:T(8,128)(2,1)S(1)}, u32[]{:S(2)}) copy-start(bf16[448,512]{1,0:T(8,128)(2,1)S(1)} %collective-permute-done.refs_1_) | copy-start | bytes 1376260
  41.9 3.3 %copy-start.5 = (bf16[448,512]{1,0:T(8,128)(2,1)}, bf16[448,512]{1,0:T(8,128)(2,1)S(1)}, u32[]{:S(2)}) copy-start(bf16[448,512]{1,0:T(8,128)(2,1)S(1)} %collective-permute-done.2.refs_3_) | copy-start | bytes 1376260
  45.2 7.0 %copy-start.7 = (bf16[1,256,448]{1,2,0:T(8,128)(2,1)S(1)}, bf16[1,256,448]{1,2,0:T(8,128)(2,1)}, u32[]{:S(2)}) copy-start(bf16[1,256,448]{1,2,0:T(8,128)(2,1)} %param.13) | copy-start | bytes 688132
  45.2 32.1 %all-to-all-start.1 = ((bf16[8,32,2048]{2,1,0:T(8,128)(2,1)}), bf16[8,32,2048]{2,1,0:T(8,128)(2,1)S(1)}, u32[]{:S(2)}, u32[]{:S(2)}) async-start(bf16[8,32,2048]{2,1,0:T(8,128)(2,1)} %bitcast.6), calls=%async_computation.1 | async-start | bytes 2097152 | tf_op jit(solution)/shard_map/all_to_all | solution.py:195
  52.2 11.6 %collective-permute-start.5 = (bf16[448,256]{1,0:T(8,128)(2,1)S(1)}, bf16[448,256]{1,0:T(8,128)(2,1)S(1)}, u32[]{:S(2)}, u32[]{:S(2)}) collective-permute-start(bf16[448,256]{1,0:T(8,128)(2,1)S(1)} %bitcast.33), channel_id=1, source_target_pairs={{0,2},{2,0},{1,3},{3,1},{4,6},{6,4},{5,7},{7,5},{8,10},{10,8},{9,1... | collective-permute-start | bytes 688136 | tf_op jit(solution)/shard_map/ppermute | solution.py:206
  58.7 11.5 %collective-permute-start.7 = (bf16[256,896]{1,0:T(8,128)(2,1)S(1)}, bf16[256,896]{1,0:T(8,128)(2,1)S(1)}, u32[]{:S(2)}, u32[]{:S(2)}) collective-permute-start(bf16[256,896]{1,0:T(8,128)(2,1)S(1)} %bitcast.28), channel_id=1, source_target_pairs={{0,1},{1,0},{2,3},{3,2},{4,5},{5,4},{6,7},{7,6},{8,9},{9,8},{10,11... | collective-permute-start | bytes 1376264 | tf_op jit(solution)/shard_map/ppermute | solution.py:206
  61.9 6.0 %collective-permute-start.4 = (bf16[448,256]{1,0:T(8,128)(2,1)S(1)}, bf16[448,256]{1,0:T(8,128)(2,1)S(1)}, u32[]{:S(2)}, u32[]{:S(2)}) collective-permute-start(bf16[448,256]{1,0:T(8,128)(2,1)S(1)} %bitcast.34), channel_id=1, source_target_pairs={{0,1},{1,0},{2,3},{3,2},{4,5},{5,4},{6,7},{7,6},{8,9},{9,8},{10,11... | collective-permute-start | bytes 688136 | tf_op jit(solution)/shard_map/ppermute | solution.py:206
  63.8 6.4 %copy-start.9 = (bf16[448,256]{1,0:T(8,128)(2,1)}, bf16[448,256]{1,0:T(8,128)(2,1)S(1)}, u32[]{:S(2)}) copy-start(bf16[448,256]{1,0:T(8,128)(2,1)S(1)} %collective-permute-done.5.refs_2_.refs_6_) | copy-start | bytes 688132
  63.8 5.1 %collective-permute-start.6 = (bf16[448,256]{1,0:T(8,128)(2,1)S(1)}, bf16[448,256]{1,0:T(8,128)(2,1)S(1)}, u32[]{:S(2)}, u32[]{:S(2)}) collective-permute-start(bf16[448,256]{1,0:T(8,128)(2,1)S(1)} %collective-permute-done.5.refs_2_.refs_6_), channel_id=1, source_target_pairs={{0,1},{1,0},{2,3},{3,2},{4,5},{5,4},{6,7},{7,6},{8,9},{9,8},{10,11... | collective-permute-start | bytes 688136 | tf_op jit(solution)/shard_map/ppermute | solution.py:206
  67.9 2.4 %copy-start.11 = (bf16[448,256]{1,0:T(8,128)(2,1)}, bf16[448,256]{1,0:T(8,128)(2,1)S(1)}, u32[]{:S(2)}) copy-start(bf16[448,256]{1,0:T(8,128)(2,1)S(1)} %collective-permute-done.4.refs_1_.refs_5_) | copy-start | bytes 688132
  69.0 1.3 copy-start.13
  70.3 0.8 copy-start
  77.3 21.3 %all-to-all-start.2 = ((bf16[8,32,1024]{2,1,0:T(8,128)(2,1)}), bf16[8,32,1024]{2,1,0:T(8,128)(2,1)S(1)}, u32[]{:S(2)}, u32[]{:S(2)}) async-start(bf16[8,32,1024]{2,1,0:T(8,128)(2,1)} %bitcast.10), calls=%async_computation.2 | async-start | bytes 1048576 | tf_op jit(solution)/shard_map/all_to_all | solution.py:195
  80.9 20.1 %collective-permute-start.3 = (bf16[32,2048]{1,0:T(8,128)(2,1)S(1)}, bf16[32,2048]{1,0:T(8,128)(2,1)S(1)}, u32[]{:S(2)}, u32[]{:S(2)}) collective-permute-start(bf16[32,2048]{1,0:T(8,128)(2,1)S(1)} %shard_map.112.part_ref), channel_id=1, source_target_pairs={{0,64},{64,0},{1,65},{65,1},{2,66},{66,2},{3,67},{67,3},{4,68},{68... | collective-permute-start | bytes 393224 | tf_op jit(solution)/shard_map/ppermute | solution.py:206
  101.9 24.1 %all-to-all-start.4 = ((bf16[8,32,1024]{2,1,0:T(8,128)(2,1)}), bf16[8,32,1024]{2,1,0:T(8,128)(2,1)S(1)}, u32[]{:S(2)}, u32[]{:S(2)}) async-start(bf16[8,32,1024]{2,1,0:T(8,128)(2,1)} %shard_map.113), calls=%async_computation.4 | async-start | bytes 1048576 | tf_op jit(solution)/shard_map/all_to_all | solution.py:195
  108.4 16.4 %collective-permute-start.8 = (bf16[32,1024]{1,0:T(8,128)(2,1)S(1)}, bf16[32,1024]{1,0:T(8,128)(2,1)S(1)}, u32[]{:S(2)}, u32[]{:S(2)}) collective-permute-start(bf16[32,1024]{1,0:T(8,128)(2,1)S(1)} %shard_map.115.act_ref), channel_id=1, source_target_pairs={{0,64},{64,0},{1,65},{65,1},{2,66},{66,2},{3,67},{67,3},{4,68},{68... | collective-permute-start | bytes 196616 | tf_op jit(solution)/shard_map/ppermute | solution.py:206
  126.0 32.1 %all-to-all-start.3 = ((bf16[8,32,2048]{2,1,0:T(8,128)(2,1)}), bf16[8,32,2048]{2,1,0:T(8,128)(2,1)S(1)}, u32[]{:S(2)}, u32[]{:S(2)}) async-start(bf16[8,32,2048]{2,1,0:T(8,128)(2,1)} %shard_map.116), calls=%async_computation.3 | async-start | bytes 2097152 | tf_op jit(solution)/shard_map/all_to_all | solution.py:195
  132.5 7.6 %copy-start.1 = (bf16[256,896]{1,0:T(8,128)(2,1)S(1)}, bf16[256,896]{1,0:T(8,128)(2,1)}, u32[]{:S(2)}) copy-start(bf16[256,896]{1,0:T(8,128)(2,1)} %copy-done) | copy-start | bytes 1376260
  132.6 7.5 %collective-permute-start.9 = (bf16[256,512]{1,0:T(8,128)(2,1)S(1)}, bf16[256,512]{1,0:T(8,128)(2,1)S(1)}, u32[]{:S(2)}, u32[]{:S(2)}) collective-permute-start(bf16[256,512]{1,0:T(8,128)(2,1)S(1)} %pad_maximum_fusion.2), channel_id=1, source_target_pairs={{0,1},{1,0},{2,3},{3,2},{4,5},{5,4},{6,7},{7,6},{8,9},{9,8},{10,11... | collective-permute-start | bytes 786440 | tf_op jit(solution)/shard_map/ppermute | solution.py:206
  140.8 8.8 %collective-permute-start.10 = (bf16[448,256]{1,0:T(8,128)(2,1)S(1)}, bf16[448,256]{1,0:T(8,128)(2,1)}, u32[]{:S(2)}, u32[]{:S(2)}) collective-permute-start(bf16[448,256]{1,0:T(8,128)(2,1)S(1)} %get-tuple-element.42), channel_id=1, source_target_pairs={{0,2},{2,0},{1,3},{3,1},{4,6},{6,4},{5,7},{7,5},{8,10},{10,8},{9,1... | collective-permute-start | bytes 688136 | tf_op jit(solution)/shard_map/ppermute | solution.py:206
  158.1 1.0 copy-start.4
  159.1 1.0 copy-start.6
  160.1 0.9 copy-start.8
  161.1 0.9 copy-start.10
  162.0 0.9 copy-start.12
  163.0 0.9 copy-start.14
  165.7 51.1 %all-to-all-start.5 = ((bf16[16,16,896]{2,1,0:T(8,128)(2,1)}), bf16[16,16,896]{2,1,0:T(8,128)(2,1)S(1)}, u32[]{:S(2)}, u32[]{:S(2)}) async-start(bf16[16,16,896]{2,1,0:T(8,128)(2,1)} %bitcast.13), calls=%async_computation.5 | async-start | bytes 917504 | tf_op jit(solution)/shard_map/all_to_all | solution.py:195
  190.5 6.2 %copy-start.2 = (bf16[256,896]{1,0:T(8,128)(2,1)S(1)}, bf16[256,896]{1,0:T(8,128)(2,1)}, u32[]{:S(2)}) copy-start(bf16[256,896]{1,0:T(8,128)(2,1)} %copy-done) | copy-start | bytes 1376260
  190.6 6.1 %collective-permute-start.11 = (bf16[256,1024]{1,0:T(8,128)(2,1)S(1)}, bf16[256,1024]{1,0:T(8,128)(2,1)S(1)}, u32[]{:S(2)}, u32[]{:S(2)}) collective-permute-start(bf16[256,1024]{1,0:T(8,128)(2,1)S(1)} %pad_maximum_fusion), channel_id=1, source_target_pairs={{0,1},{1,0},{2,3},{3,2},{4,5},{5,4},{6,7},{7,6},{8,9},{9,8},{10,11... | collective-permute-start | bytes 1572872 | tf_op jit(solution)/shard_map/ppermute | solution.py:206
  196.7 2.6 %copy-start.16 = (f32[64,2]{0,1:T(2,128)S(1)}, f32[64,2]{0,1:T(2,128)}, u32[]{:S(2)}) copy-start(f32[64,2]{0,1:T(2,128)} %param.9) | copy-start | bytes 1540
  197.4 2.0 copy-start.15
  197.4 18.4 %collective-permute-start.12 = (bf16[448,512]{1,0:T(8,128)(2,1)S(1)}, bf16[448,512]{1,0:T(8,128)(2,1)S(1)}, u32[]{:S(2)}, u32[]{:S(2)}) collective-permute-start(bf16[448,512]{1,0:T(8,128)(2,1)S(1)} %get-tuple-element.54), channel_id=1, source_target_pairs={{0,2},{2,0},{1,3},{3,1},{4,6},{6,4},{5,7},{7,5},{8,10},{10,8},{9,1... | collective-permute-start | bytes 1376264 | tf_op jit(solution)/shard_map/ppermute | solution.py:206
